TPU v7x, 32 devices: a whole 2x2x4 slice. The times are simulated.
32 devices in a mesh: fsdp: 8 (over y, x, core), seq: 4 (over z).
Axes of the slice: x: 2, y: 2, z: 4, core: 2. Of those that a mesh axis runs over, the one named last changes fastest.
Arguments:
- pixels: bfloat16 [24, 1024, 768], P('fsdp', 'seq'), may hold values from -6 to 6
- restore: int32 [24, 1024], P('fsdp'), may hold values from 0 to 1023, each once within a row
- enc_w: float32 [768, 10496], P('fsdp'), may hold values from -0.21875 to 0.21875
- enc_m: float32 [768, 10496], P('fsdp'), may hold values from -0.00318944 to 0.00318944
- enc_v: float32 [768, 10496], P('fsdp'), may hold values from 2.1192763e-07 to 8.477105e-07
- dec_w: float32 [512, 6144], P('fsdp'), may hold values from -0.25 to 0.25
- dec_m: float32 [512, 6144], P('fsdp'), may hold values from -0.00318944 to 0.00318944
- dec_v: float32 [512, 6144], P('fsdp'), may hold values from 2.1192763e-07 to 8.477105e-07
- head_w: float32 [512, 768], replicated, may hold values from -0.25 to 0.25
- head_m: float32 [512, 768], replicated, may hold values from -0.000115088995 to 0.000115088995
- head_v: float32 [512, 768], replicated, may hold values from 2.7594743e-10 to 1.1037897e-09
- gain_w: float32 [3840], replicated, may hold values from 0.5 to 1.5
- gain_m: float32 [3840], replicated, may hold values from -0.00318944 to 0.00318944
- gain_v: float32 [3840], replicated, may hold values from 2.1192763e-07 to 8.477105e-07
- bias_w: float32 [17408], replicated, may hold values from -1.5 to 1.5
- bias_m: float32 [17408], replicated, may hold values from -0.00318944 to 0.00318944
- bias_v: float32 [17408], replicated, may hold values from 2.1192763e-07 to 8.477105e-07
Outputs:
- loss: float32 [], replicated
- enc_m_new: float32 [768, 10496], P('fsdp')
- enc_v_new: float32 [768, 10496], P('fsdp')
- enc_w_new: float32 [768, 10496], P('fsdp')
- dec_m_new: float32 [512, 6144], P('fsdp')
- dec_v_new: float32 [512, 6144], P('fsdp')
- dec_w_new: float32 [512, 6144], P('fsdp')
- head_m_new: float32 [512, 768], replicated
- head_v_new: float32 [512, 768], replicated
- head_w_new: float32 [512, 768], replicated
- gain_m_new: float32 [3840], replicated
- gain_v_new: float32 [3840], replicated
- gain_w_new: float32 [3840], replicated
- bias_m_new: float32 [17408], replicated
- bias_v_new: float32 [17408], replicated
- bias_w_new: float32 [17408], replicated
Inputs may be any that keep to these rules, and one draw needn't show every extreme that they name: `restore`: each image's row is a permutation of 0 to 1023; a patch is visible when its entry is under 256.
All inputs are finite; a program needn't handle non-finite values.
Results may differ from a plain program's by a relative error of at most 0.00075.
The roundings to bfloat16 on the way count: a program that leaves them out, or rounds other values in their place, can miss the bound.
Values may be sent and summed in bfloat16 or wider, within the bound.
A program may use at most 256 MiB of HBM per device.

v0:
```python
from functools import partial

import jax
import jax.numpy as jnp
from jax import lax
from jax.sharding import PartitionSpec as P

D_E = 768
H_E = 12
FF_E = 3072
D_D = 512
H_D = 16
FF_D = 2048
PIX = 768
PATCHES = 1024
KEEP = 256
STEP = 5


NORM_EPS = 1e-06
PIXEL_EPS = 1e-06
BETA_ONE = 0.5
BETA_TWO = 0.75
MATRIX_RATE = 0.03
SMALL_RATE = 0.1
MATRIX_DECAY = 0.05
ADAM_EPS = 1e-08


def bias_widths():
    return [
        D_E,
        D_E,
        D_E,
        D_E,
        D_E,
        D_E,
        D_E,
        FF_E,
        D_E,
        D_E,
        D_D,
        D_D,
        D_D,
        D_D,
        D_D,
        D_D,
        D_D,
        FF_D,
        D_D,
        D_D,
        PIX,
    ]


def split_vector(vector, widths):
    pieces = []
    offset = 0
    for span_width in widths:
        pieces.append(vector[offset : offset + span_width])
        offset += span_width
    return pieces


def positions(index_arr, width_dim):
    halves = width_dim // 2
    frequency = 10000.0 ** (-jnp.arange(halves, dtype=jnp.float32) / halves)
    angles = (index_arr.astype(jnp.float32) + 1.0)[..., None] * frequency
    return jnp.concatenate([jnp.sin(angles), jnp.cos(angles)], axis=-1)


def norm_forward(inputs, gain_vec, shift_vec):
    centre = inputs - jnp.mean(inputs, axis=-1, keepdims=True)
    inverse = lax.rsqrt(jnp.mean(centre * centre, axis=-1, keepdims=True) + NORM_EPS)
    scaled = centre * inverse
    return (scaled * gain_vec + shift_vec, scaled, inverse)


def norm_backward(upstream, scaled, inverse, gain_vec):
    weighted = upstream * gain_vec
    inner_part = (
        weighted
        - jnp.mean(weighted, axis=-1, keepdims=True)
        - scaled * jnp.mean(weighted * scaled, axis=-1, keepdims=True)
    )
    return (
        inverse * inner_part,
        jnp.sum(upstream * scaled, axis=(0, 1)),
        jnp.sum(upstream, axis=(0, 1)),
    )


def project(row_block, weight):
    return jnp.einsum("isd,de->ise", row_block, weight, preferred_element_type=jnp.float32)


def project_back(row_block, weight):
    return jnp.einsum("ise,de->isd", row_block, weight, preferred_element_type=jnp.float32)


def weight_grad(row_block, upstream):
    return jnp.einsum("isd,ise->de", row_block, upstream, preferred_element_type=jnp.float32)


def row_sum(tensor):
    return jnp.sum(tensor.astype(jnp.float32), axis=(0, 1))


def enc_mats_of(full_rows):
    return (
        full_rows[:, D_E : 4 * D_E],
        full_rows[:, 4 * D_E : 5 * D_E],
        full_rows[:, 5 * D_E : 5 * D_E + FF_E],
        full_rows[:, 5 * D_E + FF_E : 5 * D_E + 2 * FF_E],
    )


def dec_mats_of(full_rows):
    return (
        full_rows[:, : 3 * D_D],
        full_rows[:, 3 * D_D : 4 * D_D],
        full_rows[:, 4 * D_D : 4 * D_D + FF_D],
        full_rows[:, 4 * D_D + FF_D :],
    )


def head_scores(query_h, key_h, live_count):
    scale_val = query_h.shape[1] ** (-0.5)
    scores = jnp.dot(query_h, key_h.T, preferred_element_type=jnp.float32) * scale_val
    valid_keys = lax.broadcasted_iota(jnp.int32, scores.shape, 1) < live_count
    return (jnp.where(valid_keys, scores, -1e30), scale_val)


def attend_forward(stacked, live_count):

    def one_head(parts):
        query_h, key_h, value_h = parts
        scores, _ = head_scores(query_h, key_h, live_count)
        row_max = jnp.max(scores, axis=-1, keepdims=True)
        expo_rows = jnp.exp(scores - row_max)
        row_total = jnp.sum(expo_rows, axis=-1, keepdims=True)
        prob_rows = (expo_rows / row_total).astype(jnp.bfloat16)
        head_out = jnp.dot(prob_rows, value_h, preferred_element_type=jnp.float32).astype(
            jnp.bfloat16
        )
        return (head_out, (row_max + jnp.log(row_total))[:, 0])

    def one_image(image_rows):
        by_head = jnp.moveaxis(image_rows, 2, 0)
        out_heads, logsum = lax.map(
            one_head, (by_head[:, :, 0], by_head[:, :, 1], by_head[:, :, 2])
        )
        return (jnp.moveaxis(out_heads, 0, 1), logsum)

    return lax.map(one_image, stacked)


def attend_backward(stacked, logsum, upstream, live_count):

    def one_head(parts):
        query_h, key_h, value_h, lse_h, grad_h = parts
        scores, scale_val = head_scores(query_h, key_h, live_count)
        prob_rows = jnp.exp(scores - lse_h[:, None])
        grad_v = jnp.dot(
            prob_rows.astype(jnp.bfloat16).T, grad_h, preferred_element_type=jnp.float32
        )
        grad_p = jnp.dot(grad_h, value_h.T, preferred_element_type=jnp.float32)
        grad_s = (
            prob_rows * (grad_p - jnp.sum(prob_rows * grad_p, axis=-1, keepdims=True))
        ).astype(jnp.bfloat16)
        grad_q = jnp.dot(grad_s, key_h, preferred_element_type=jnp.float32) * scale_val
        grad_k = jnp.dot(grad_s.T, query_h, preferred_element_type=jnp.float32) * scale_val
        return jnp.stack([grad_q, grad_k, grad_v], axis=1).astype(jnp.bfloat16)

    def one_image(parts):
        image_rows, lse_rows, grad_rows = parts
        by_head = jnp.moveaxis(image_rows, 2, 0)
        out_heads = lax.map(
            one_head,
            (
                by_head[:, :, 0],
                by_head[:, :, 1],
                by_head[:, :, 2],
                lse_rows,
                jnp.moveaxis(grad_rows, 1, 0),
            ),
        )
        return jnp.moveaxis(out_heads, 0, 2)

    return lax.map(one_image, (stacked, logsum, upstream))


def layer_forward(inputs, mats, gain_one, gain_two, vecs, head_count, live_count):
    w_qkv, w_out, w_up, w_down = mats
    shift_one, bias_q, bias_v, bias_out, shift_two, bias_up, bias_down = vecs
    image_count, row_count, width_dim = inputs.shape
    normed, scaled_one, inverse_one = norm_forward(inputs, gain_one, shift_one)
    normed_low = normed.astype(jnp.bfloat16)
    qkv_bias = jnp.concatenate([bias_q, jnp.zeros_like(bias_q), bias_v])
    mixed_qkv = (project(normed_low, w_qkv) + qkv_bias).astype(jnp.bfloat16)
    mixed_qkv = mixed_qkv.reshape(image_count, row_count, 3, head_count, width_dim // head_count)
    stacked = lax.all_to_all(mixed_qkv, "seq", split_axis=3, concat_axis=1, tiled=True)
    attended, logsum = attend_forward(stacked, live_count)
    merged = lax.all_to_all(attended, "seq", split_axis=1, concat_axis=2, tiled=True).reshape(
        image_count, row_count, width_dim
    )
    middle = inputs + project(merged, w_out) + bias_out
    second, scaled_two, inverse_two = norm_forward(middle, gain_two, shift_two)
    second_low = second.astype(jnp.bfloat16)
    hidden = project(second_low, w_up) + bias_up
    active = jax.nn.gelu(hidden, approximate=False).astype(jnp.bfloat16)
    output = middle + project_back(active, w_down) + bias_down
    saved = (
        scaled_one,
        inverse_one,
        normed_low,
        stacked,
        logsum,
        merged,
        scaled_two,
        inverse_two,
        second_low,
        hidden,
        active,
    )
    return (output, saved)


def layer_backward(upstream, saved, mats, gain_one, gain_two, head_count, live_count):
    w_qkv, w_out, w_up, w_down = mats
    (
        scaled_one,
        inverse_one,
        normed_low,
        stacked,
        logsum,
        merged,
        scaled_two,
        inverse_two,
        second_low,
        hidden,
        active,
    ) = saved
    image_count, row_count, width_dim = upstream.shape
    down_low = upstream.astype(jnp.bfloat16)
    grad_down = weight_grad(down_low, active)
    grad_bias_down = row_sum(upstream)
    _, gelu_pull = jax.vjp(partial(jax.nn.gelu, approximate=False), hidden)
    hidden_grad = gelu_pull(project(down_low, w_down))[0].astype(jnp.bfloat16)
    grad_up = weight_grad(second_low, hidden_grad)
    grad_bias_up = row_sum(hidden_grad)
    through, grad_gain_two, grad_shift_two = norm_backward(
        project_back(hidden_grad, w_up), scaled_two, inverse_two, gain_two
    )
    middle_grad = upstream + through
    middle_low = middle_grad.astype(jnp.bfloat16)
    grad_out = weight_grad(merged, middle_low)
    grad_bias_out = row_sum(middle_grad)
    attn_grad = project_back(middle_low, w_out).astype(jnp.bfloat16)
    attn_grad = attn_grad.reshape(image_count, row_count, head_count, width_dim // head_count)
    back_heads = lax.all_to_all(attn_grad, "seq", split_axis=2, concat_axis=1, tiled=True)
    grad_stacked = attend_backward(stacked, logsum, back_heads, live_count)
    grad_mixed = lax.all_to_all(
        grad_stacked, "seq", split_axis=1, concat_axis=3, tiled=True
    ).reshape(image_count, row_count, 3 * width_dim)
    grad_qkv = weight_grad(normed_low, grad_mixed)
    grad_bias_q = row_sum(grad_mixed[:, :, :width_dim])
    grad_bias_v = row_sum(grad_mixed[:, :, 2 * width_dim :])
    through_one, grad_gain_one, grad_shift_one = norm_backward(
        project_back(grad_mixed, w_qkv), scaled_one, inverse_one, gain_one
    )
    mats_grad = (grad_qkv, grad_out, grad_up, grad_down)
    gains_grad = (grad_gain_one, grad_gain_two)
    vecs_grad = (
        grad_shift_one,
        grad_bias_q,
        grad_bias_v,
        grad_bias_out,
        grad_shift_two,
        grad_bias_up,
        grad_bias_down,
    )
    return (middle_grad + through_one, mats_grad, gains_grad, vecs_grad)


def adamw(weight, moment_one, moment_two, gradient, step_rate, decay_rate):
    moment_one = BETA_ONE * moment_one + (1 - BETA_ONE) * gradient
    moment_two = BETA_TWO * moment_two + (1 - BETA_TWO) * gradient * gradient
    fixed_one = moment_one / (1 - BETA_ONE**STEP)
    fixed_two = moment_two / (1 - BETA_TWO**STEP)
    weight = weight - step_rate * (
        fixed_one / (jnp.sqrt(fixed_two) + ADAM_EPS) + decay_rate * weight
    )
    return (moment_one, moment_two, weight)


def shards(
    pixels,
    restore,
    enc_w,
    enc_m,
    enc_v,
    dec_w,
    dec_m,
    dec_v,
    head_w,
    head_m,
    head_v,
    gain_w,
    gain_m,
    gain_v,
    bias_w,
    bias_m,
    bias_v,
):
    seq_count = lax.axis_size("seq")
    seq_place = lax.axis_index("seq")
    image_count = pixels.shape[0]
    masked_total = image_count * lax.axis_size("fsdp") * (PATCHES - KEEP)
    enc_rows = (KEEP + seq_count) // seq_count
    dec_rows = (PATCHES + seq_count) // seq_count
    enc_full, dec_full = (
        lax.all_gather(enc_w.astype(jnp.bfloat16), "fsdp", axis=0, tiled=True),
        lax.all_gather(dec_w.astype(jnp.bfloat16), "fsdp", axis=0, tiled=True),
    )
    all_pixels = lax.all_gather(pixels, "seq", axis=1, tiled=True)
    pieces = split_vector(bias_w, bias_widths())
    gain_parts = split_vector(gain_w, [D_E, D_E, D_E, D_D, D_D, D_D])
    token_ids = seq_place * enc_rows + jnp.arange(enc_rows, dtype=jnp.int32)
    patch_ids = jnp.arange(PATCHES, dtype=jnp.int32)
    keep_ids = jnp.sum(
        jnp.where(restore[:, None, :] == (token_ids - 1)[None, :, None], patch_ids, 0), axis=2
    )
    is_patch = (token_ids >= 1) & (token_ids <= KEEP)
    is_class = token_ids == 0
    kept_pixels = jnp.take_along_axis(all_pixels, keep_ids[:, :, None], axis=1)
    w_patch = enc_full[:, :D_E]
    w_embed = enc_full[:, 5 * D_E + 2 * FF_E :]
    embedded = project(kept_pixels, w_patch) + pieces[0] + positions(keep_ids, D_E)
    first_rows = jnp.where(
        is_patch[None, :, None], embedded, jnp.where(is_class[None, :, None], pieces[1], 0.0)
    )
    encoded, enc_saved = layer_forward(
        first_rows, enc_mats_of(enc_full), gain_parts[0], gain_parts[1], pieces[2:9], H_E, KEEP + 1
    )
    final_rows, final_scaled, final_inverse = norm_forward(encoded, gain_parts[2], pieces[9])
    final_low = final_rows.astype(jnp.bfloat16)
    shrunk = (project(final_low, w_embed) + pieces[10]).astype(jnp.bfloat16)
    all_shrunk = lax.all_gather(shrunk, "seq", axis=1, tiled=True)
    row_ids = seq_place * dec_rows + jnp.arange(dec_rows, dtype=jnp.int32)
    patch_of = jnp.clip(row_ids - 1, 0, PATCHES - 1)
    rank_of = jnp.take(restore, patch_of, axis=1)
    in_range = (row_ids >= 1) & (row_ids <= PATCHES)
    is_kept = in_range[None, :] & (rank_of < KEEP)
    is_masked = in_range[None, :] & (rank_of >= KEEP)
    take_rows = is_kept | (row_ids == 0)[None, :]
    source = jnp.where(is_kept, rank_of + 1, 0)
    picked = jnp.take_along_axis(all_shrunk, source[:, :, None], axis=1).astype(jnp.float32)
    dec_input = (
        jnp.where(take_rows[..., None], picked, 0.0)
        + jnp.where(is_masked[..., None], pieces[11], 0.0)
        + jnp.where(in_range[:, None], positions(patch_of, D_D), 0.0)[None]
    )
    decoded, dec_saved = layer_forward(
        dec_input,
        dec_mats_of(dec_full),
        gain_parts[3],
        gain_parts[4],
        pieces[12:19],
        H_D,
        PATCHES + 1,
    )
    out_norm, out_scaled, out_inverse = norm_forward(decoded, gain_parts[5], pieces[19])
    out_low = out_norm.astype(jnp.bfloat16)
    head_low = head_w.astype(jnp.bfloat16)
    predicted = project(out_low, head_low) + pieces[20]
    targets = jnp.take(all_pixels, patch_of, axis=1).astype(jnp.float32)
    centre = targets - jnp.mean(targets, axis=-1, keepdims=True)
    targets = centre * lax.rsqrt(
        jnp.sum(centre * centre, axis=-1, keepdims=True) / (PIX - 1) + PIXEL_EPS
    )
    errors = predicted - targets
    loss_part = (
        jnp.sum(jnp.where(is_masked, jnp.mean(errors * errors, axis=-1), 0.0)) / masked_total
    )
    pred_grad = jnp.where(is_masked[..., None], errors * (2.0 / (PIX * masked_total)), 0.0)
    pred_low = pred_grad.astype(jnp.bfloat16)
    grad_head = weight_grad(out_low, pred_low)
    grad_bias_head = row_sum(pred_grad)
    back_grad, grad_gain_out, grad_shift_out = norm_backward(
        project_back(pred_low, head_low), out_scaled, out_inverse, gain_parts[5]
    )
    dec_back, dec_grads, dec_gains, dec_vecs = layer_backward(
        back_grad, dec_saved, dec_mats_of(dec_full), gain_parts[3], gain_parts[4], H_D, PATCHES + 1
    )
    grad_mask = jnp.sum(jnp.where(is_masked[..., None], dec_back, 0.0), axis=(0, 1))
    image_ids = jnp.arange(image_count, dtype=jnp.int32)[:, None]
    spread = (
        jnp.zeros(all_shrunk.shape, jnp.float32)
        .at[image_ids, source]
        .add(jnp.where(take_rows[..., None], dec_back, 0.0))
    )
    shrunk_grad = lax.psum_scatter(
        spread.astype(jnp.bfloat16), "seq", scatter_dimension=1, tiled=True
    )
    grad_embed = weight_grad(final_low, shrunk_grad)
    grad_bias_embed = row_sum(shrunk_grad)
    through, grad_gain_final, grad_shift_final = norm_backward(
        project_back(shrunk_grad, w_embed), final_scaled, final_inverse, gain_parts[2]
    )
    enc_back, enc_grads, enc_gains, enc_vecs = layer_backward(
        through, enc_saved, enc_mats_of(enc_full), gain_parts[0], gain_parts[1], H_E, KEEP + 1
    )
    embed_grad = jnp.where(is_patch[None, :, None], enc_back, 0.0)
    grad_patch = weight_grad(kept_pixels, embed_grad.astype(jnp.bfloat16))
    grad_bias_patch = row_sum(embed_grad)
    grad_class = jnp.sum(jnp.where(is_class[None, :, None], enc_back, 0.0), axis=(0, 1))
    enc_qkv, enc_out, enc_up, enc_down = enc_grads
    dec_qkv, dec_out, dec_up, dec_down = dec_grads
    shard_parts = (
        lax.psum_scatter(grad_patch, "fsdp", scatter_dimension=0, tiled=True),
        lax.psum_scatter(enc_qkv, "fsdp", scatter_dimension=0, tiled=True),
        lax.psum_scatter(enc_out, "fsdp", scatter_dimension=0, tiled=True),
        lax.psum_scatter(enc_up, "fsdp", scatter_dimension=0, tiled=True),
        lax.psum_scatter(enc_down, "fsdp", scatter_dimension=0, tiled=True),
        lax.psum_scatter(grad_embed, "fsdp", scatter_dimension=0, tiled=True),
        lax.psum_scatter(dec_qkv, "fsdp", scatter_dimension=0, tiled=True),
        lax.psum_scatter(dec_out, "fsdp", scatter_dimension=0, tiled=True),
        lax.psum_scatter(dec_up, "fsdp", scatter_dimension=0, tiled=True),
        lax.psum_scatter(dec_down, "fsdp", scatter_dimension=0, tiled=True),
    )
    seq_parts = lax.psum(
        (
            shard_parts[0],
            shard_parts[1],
            shard_parts[2],
            shard_parts[3],
            shard_parts[4],
            shard_parts[5],
            shard_parts[6],
            shard_parts[7],
            shard_parts[8],
            shard_parts[9],
        ),
        "seq",
    )
    enc_grad = jnp.concatenate(seq_parts[:6], axis=1)
    dec_grad = jnp.concatenate(seq_parts[6:], axis=1)
    bias_grad = jnp.concatenate(
        [grad_bias_patch, grad_class]
        + list(enc_vecs)
        + [grad_shift_final, grad_bias_embed, grad_mask]
        + list(dec_vecs)
        + [grad_shift_out, grad_bias_head]
    )
    gain_grad = jnp.concatenate(
        [enc_gains[0], enc_gains[1], grad_gain_final, dec_gains[0], dec_gains[1], grad_gain_out]
    )
    head_sum, gain_sum, bias_sum, loss_total = lax.psum(
        (grad_head, gain_grad, bias_grad, loss_part), ("fsdp", "seq")
    )
    enc_new = adamw(enc_w, enc_m, enc_v, enc_grad, MATRIX_RATE, MATRIX_DECAY)
    dec_new = adamw(dec_w, dec_m, dec_v, dec_grad, MATRIX_RATE, MATRIX_DECAY)
    head_new = adamw(head_w, head_m, head_v, head_sum, MATRIX_RATE, MATRIX_DECAY)
    gain_new = adamw(gain_w, gain_m, gain_v, gain_sum, SMALL_RATE, 0.0)
    bias_new = adamw(bias_w, bias_m, bias_v, bias_sum, SMALL_RATE, 0.0)
    return (
        loss_total,
        enc_new[0],
        enc_new[1],
        enc_new[2],
        dec_new[0],
        dec_new[1],
        dec_new[2],
        head_new[0],
        head_new[1],
        head_new[2],
        gain_new[0],
        gain_new[1],
        gain_new[2],
        bias_new[0],
        bias_new[1],
        bias_new[2],
    )


def solution(mesh):
    in_specs = (
        P("fsdp", "seq", None),
        P("fsdp", None),
        P("fsdp", None),
        P("fsdp", None),
        P("fsdp", None),
        P("fsdp", None),
        P("fsdp", None),
        P("fsdp", None),
        P(),
        P(),
        P(),
        P(),
        P(),
        P(),
        P(),
        P(),
        P(),
    )
    out_specs = (
        P(),
        P("fsdp", None),
        P("fsdp", None),
        P("fsdp", None),
        P("fsdp", None),
        P("fsdp", None),
        P("fsdp", None),
        P(),
        P(),
        P(),
        P(),
        P(),
        P(),
        P(),
        P(),
        P(),
    )
    return jax.shard_map(shards, mesh=mesh, in_specs=in_specs, out_specs=out_specs, check_vma=False)
```

profile of v0, /device:TPU:9, one launch (start us, length us, event | category | flops | bytes accessed | tf_op | source)
XLA Modules:
  0.0 1895.3 jit_solution(14066609127515304357)
XLA Ops:
  18.5 79.1 %all-gather.4.cloned.1.call-done = bf16[3,1024,768]{2,1,0:T(8,128)(2,1)} async-done(((bf16[3,256,768]{2,1,0:T(8,128)(2,1)}), bf16[3,1024,768]{2,1,0:T(8,128)(2,1)}) %all-gather.4.cloned.1.call-update) | async-done | bytes 4718608 | tf_op jit(solution)/shard_map/all_gather | solution.py:326
  101.3 87.4 %all-gather.6.cloned.1.call-done = bf16[768,10496]{1,0:T(8,128)(2,1)} async-done(((bf16[96,10496]{1,0:T(8,128)(2,1)}), bf16[768,10496]{1,0:T(8,128)(2,1)}) %all-gather.6.cloned.1.call-update) | async-done | bytes 16121872 | tf_op jit(solution)/shard_map/all_gather | solution.py:323
  208.6 34.5 %all-to-all-done = bf16[3,65,3,12,64]{1,4,2,0,3:T(8,128)(2,1)S(1)} async-done(((bf16[3,65,3,12,64]{1,4,2,0,3:T(8,128)(2,1)}), bf16[3,65,3,12,64]{1,4,2,0,3:T(8,128)(2,1)S(1)}, u32[]{:S(2)}, u32[]{:S(2)}) %all-to-all-start) | async-done | bytes 898592 | tf_op jit(solution)/shard_map/all_to_all | solution.py:202
  356.7 72.3 %all-to-all-done.2 = bf16[3,257,3,16,32]{1,4,2,0,3:T(8,128)(2,1)S(1)} async-done(((bf16[3,257,3,16,32]{1,4,2,0,3:T(8,128)(2,1)}), bf16[3,257,3,16,32]{1,4,2,0,3:T(8,128)(2,1)S(1)}, u32[]{:S(2)}, u32[]{:S(2)}) %all-to-all-start.2) | async-done | bytes 2368544 | tf_op jit(solution)/shard_map/all_to_all | solution.py:202
  445.8 42.3 %while.91 = (s32[]{:T(128)}, bf16[3,1028,4,32]{1,3,2,0:T(8,128)(2,1)}, f32[3,4,1028]{2,1,0:T(4,128)S(1)}, bf16[3,1028,3,4,32]{4,1,3,2,0:T(8,128)(2,1)}, s32[]{:T(128)}, /*index=5*/s32[]{:T(128)}, s32[]{:T(128)}, s32[]{:T(128)}) while((s32[]{:T(128)}, bf16[3,1028,4,32]{1,3,2,0:T(8,128)(2,1)}, f32[3,4,1028]{2,1,0:T(4,128)S(1)}, ...), condition=%wide.region_20.21_spmd, body=%wide.region_15.20_spmd.sunk | while | flops 143755520 | bytes 17891892 | solution.py:155
  590.5 24.1 %all-to-all-done.4 = bf16[3,257,16,32]{1,3,0,2:T(8,128)(2,1)S(1)} async-done(((bf16[3,257,16,32]{1,3,0,2:T(8,128)(2,1)}), bf16[3,257,16,32]{1,3,0,2:T(8,128)(2,1)S(1)}, u32[]{:S(2)}, u32[]{:S(2)}) %all-to-all-start.4) | async-done | bytes 789536 | tf_op jit(solution)/shard_map/all_to_all | solution.py:261
  617.2 106.5 %while.93 = (s32[]{:T(128)}, bf16[3,1028,3,4,32]{1,4,2,3,0:T(8,128)(2,1)}, bf16[3,1028,3,4,32]{4,1,3,2,0:T(8,128)(2,1)}, f32[3,4,1028]{2,1,0:T(4,128)S(1)}, bf16...) while((s32[]{:T(128)}, bf16[3,1028,3,4,32]{1,4,2,3,0:T(8,128)(2,1)}, ...), condition=%wide.region_38.39_spmd, body=%wide.region_34.38_spmd.sunk | while | flops 348438528 | bytes 41796872 | solution.py:190
  622.0 28.6 %while.98 = (s32[]{:T(128)}, bf16[4,1028,3,32]{1,3,2,0:T(8,128)(2,1)}, bf16[4,1028,32]{2,1,0:T(8,128)(2,1)S(1)}, bf16[4,1028,32]{2,1,0:T(8,128)(2,1)S(1)}, f32[4...) while((s32[]{:T(128)}, ...), condition=%wide.region_37.37_spmd, body=%wide.region_35.36_spmd.sunk | while | flops 348438528 | bytes 35783636 | solution.py:178
  657.5 28.6 %while.98 = (s32[]{:T(128)}, bf16[4,1028,3,32]{1,3,2,0:T(8,128)(2,1)}, bf16[4,1028,32]{2,1,0:T(8,128)(2,1)S(1)}, bf16[4,1028,32]{2,1,0:T(8,128)(2,1)S(1)}, f32[4...) while((s32[]{:T(128)}, ...), condition=%wide.region_37.37_spmd, body=%wide.region_35.36_spmd.sunk | while | flops 348438528 | bytes 35783636 | solution.py:178
  693.0 28.6 %while.98 = (s32[]{:T(128)}, bf16[4,1028,3,32]{1,3,2,0:T(8,128)(2,1)}, bf16[4,1028,32]{2,1,0:T(8,128)(2,1)S(1)}, bf16[4,1028,32]{2,1,0:T(8,128)(2,1)S(1)}, f32[4...) while((s32[]{:T(128)}, ...), condition=%wide.region_37.37_spmd, body=%wide.region_35.36_spmd.sunk | while | flops 348438528 | bytes 35783636 | solution.py:178
  758.9 49.5 %all-to-all-done.5 = bf16[4,2,148032]{2,1,0:T(2,128)(2,1)S(1)} async-done(((bf16[4,2,148032]{2,1,0:T(2,128)(2,1)}), bf16[4,2,148032]{2,1,0:T(2,128)(2,1)S(1)}, u32[]{:S(2)}, u32[]{:S(2)}) %all-to-all-start.5) | async-done | bytes 2368544 | tf_op jit(solution)/shard_map/all_to_all | solution.py:263
  846.8 67.8 %scatter_fusion = f32[3,260,512]{2,1,0:T(8,128)S(1)} fusion(f32[3,260,512]{2,1,0:T(8,128)S(1)} %broadcast_in_dim.364, s32[771]{0:T(1024)S(1)} %reshape.727, f32[771,512]{1,0:T(8,128)} %reshape.729), kind=kCustom, calls=%fused_computation.4 | custom fusion | flops 394752 | bytes 4743192 | tf_op jit(solution)/shard_map/scatter-add | solution.py:401
  935.0 27.4 %all-reduce.8.cloned.1.call-done = bf16[3,260,512]{2,1,0:T(8,128)(2,1)} async-done(((bf16[3,260,512]{2,1,0:T(8,128)(2,1)}), bf16[3,260,512]{2,1,0:T(8,128)(2,1)}) %all-reduce.8.cloned.1.call-update) | async-done | bytes 798736
  1038.0 25.7 %all_to_all.132 = bf16[4,2,56160]{2,1,0:T(2,128)(2,1)S(1)} all-to-all(bf16[4,2,56160]{2,1,0:T(2,128)(2,1)S(1)} %reshape.769), channel_id=1, replica_groups=mesh['fsdp'=8,'seq'=4] {'seq'}, dimensions={0} | all-to-all | bytes 1797120 | tf_op jit(solution)/shard_map/all_to_all | solution.py:263
  1111.5 42.3 %reduce-scatter.22.cloned.1.call-done = f32[96,512]{1,0:T(8,128)} async-done(((f32[768,512]{1,0:T(8,128)}), f32[96,512]{1,0:T(8,128)}) %reduce-scatter.22.cloned.1.call-update) | async-done | bytes 196624 | tf_op jit(solution)/shard_map/reduce_scatter | solution.py:426
  1153.8 45.9 %reduce-scatter.16.cloned.1.call-done = f32[96,768]{1,0:T(8,128)} async-done(((f32[768,768]{1,0:T(8,128)}), f32[96,768]{1,0:T(8,128)}) %reduce-scatter.16.cloned.1.call-update) | async-done | bytes 294928 | tf_op jit(solution)/shard_map/reduce_scatter | solution.py:423
  1199.8 50.5 %reduce-scatter.24.cloned.1.call-done = f32[64,1536]{1,0:T(8,128)} async-done(((f32[512,1536]{1,0:T(8,128)}), f32[64,1536]{1,0:T(8,128)}) %reduce-scatter.24.cloned.1.call-update) | async-done | bytes 393232 | tf_op jit(solution)/shard_map/reduce_scatter | solution.py:427
  1250.2 46.5 %reduce-scatter.12.cloned.1.call-done = f32[96,768]{1,0:T(8,128)} async-done(((f32[768,768]{1,0:T(8,128)}), f32[96,768]{1,0:T(8,128)}) %reduce-scatter.12.cloned.1.call-update) | async-done | bytes 294928 | tf_op jit(solution)/shard_map/reduce_scatter | solution.py:421
  1296.7 69.3 %reduce-scatter.14.cloned.1.call-done = f32[96,2304]{1,0:T(8,128)} async-done(((f32[768,2304]{1,0:T(8,128)}), f32[96,2304]{1,0:T(8,128)}) %reduce-scatter.14.cloned.1.call-update) | async-done | bytes 884752 | tf_op jit(solution)/shard_map/reduce_scatter | solution.py:422
  1366.0 80.0 %reduce-scatter.18.cloned.1.call-done = f32[96,3072]{1,0:T(8,128)} async-done(((f32[768,3072]{1,0:T(8,128)}), f32[96,3072]{1,0:T(8,128)}) %reduce-scatter.18.cloned.1.call-update) | async-done | bytes 1179664 | tf_op jit(solution)/shard_map/reduce_scatter | solution.py:424
  1446.0 79.9 %reduce-scatter.20.cloned.1.call-done = f32[96,3072]{1,0:T(8,128)} async-done(((f32[768,3072]{1,0:T(8,128)}), f32[96,3072]{1,0:T(8,128)}) %reduce-scatter.20.cloned.1.call-update) | async-done | bytes 1179664 | tf_op jit(solution)/shard_map/reduce_scatter | solution.py:425
  1527.9 39.4 %all-reduce.1 = (f32[]{:T(128)}, f32[3840]{0:T(1024)S(1)}) all-reduce(f32[]{:T(128)S(6)} %div.215, f32[3840]{0:T(1024)S(1)} %constant_dynamic-update-slice_fusion.21), channel_id=1, replica_groups=mesh['fsdp'=8,'seq'=4] {'fsdp','seq'}, use_global_device_ids=true, to_apply=%region_29.30 | all-reduce | flops 3841 | bytes 30728 | tf_op jit(solution)/shard_map/psum | solution.py:459
  1568.0 95.1 %all-reduce.10.cloned.1.call-done = (f32[512,768]{1,0:T(8,128)}, f32[17408]{0:T(1024)}) async-done(((f32[512,768]{1,0:T(8,128)}, f32[17408]{0:T(1024)}), (f32[512,768]{1,0:T(8,128)}, f32[17408]{0:T(1024)})) %all-reduce.10.cloned.1.call-update) | async-done | bytes 1642512 | tf_op jit(solution)/shard_map/psum | solution.py:459
  1669.4 199.2 %all-reduce.12.cloned.1.call-done = (f32[96,768]{1,0:T(8,128)}, f32[96,2304]{1,0:T(8,128)}, f32[96,768]{1,0:T(8,128)}, f32[96,3072]{1,0:T(8,128)}, f32[96,3072]{...) async-done(((f32[96,768]{1,0:T(8,128)}, f32[96,2304]{1,0:T(8,128)}, ...) | async-done | bytes 5603344 | tf_op jit(solution)/shard_map/psum | solution.py:432
  (991 shorter events, 743.5 us)
Async XLA Ops:
  7.2 90.4 %all-gather.4.cloned.1.call-start = ((), (), s32[]{:S(2)}) async-start(), calls=%async_computation.18 | async-start | bytes 5898240 | tf_op jit(solution)/shard_map/all_gather | solution.py:326
  7.9 180.7 %all-gather.6.cloned.1.call-start = ((), (), s32[]{:S(2)}) async-start(), calls=%async_computation.19 | async-start | bytes 18137088 | tf_op jit(solution)/shard_map/all_gather | solution.py:323
  11.6 328.6 %all-gather.8.cloned.1.call-start = ((), (), s32[]{:S(2)}) async-start(), calls=%async_computation.20 | async-start | bytes 7077888 | tf_op jit(solution)/shard_map/all_gather | solution.py:324
  15.1 291.3 %copy-start.110 = (f32[768]{0:T(1024)}, f32[768]{0:T(1024)S(1)}, u32[]{:S(2)}) copy-start(f32[768]{0:T(1024)S(1)} %get-tuple-element.548) | copy-start | bytes 9220
  200.8 42.3 %all-to-all-start = ((bf16[3,65,3,12,64]{1,4,2,0,3:T(8,128)(2,1)}), bf16[3,65,3,12,64]{1,4,2,0,3:T(8,128)(2,1)S(1)}, u32[]{:S(2)}, u32[]{:S(2)}) async-start(bf16[3,65,3,12,64]{1,4,2,0,3:T(8,128)(2,1)} %copy.229), calls=%async_computation | async-start | bytes 3538944 | tf_op jit(solution)/shard_map/all_to_all | solution.py:202
  262.5 21.8 %all-to-all-start.1 = ((bf16[4,2,18720]{2,1,0:T(2,128)(2,1)}), bf16[4,2,18720]{2,1,0:T(2,128)(2,1)S(1)}, u32[]{:S(2)}, u32[]{:S(2)}) async-start(bf16[4,2,18720]{2,1,0:T(2,128)(2,1)} %reshape.763), calls=%async_computation.1 | async-start | bytes 602112 | tf_op jit(solution)/shard_map/all_to_all | solution.py:204
  351.3 77.8 %all-to-all-start.2 = ((bf16[3,257,3,16,32]{1,4,2,0,3:T(8,128)(2,1)}), bf16[3,257,3,16,32]{1,4,2,0,3:T(8,128)(2,1)S(1)}, u32[]{:S(2)}, u32[]{:S(2)}) async-start(bf16[3,257,3,16,32]{1,4,2,0,3:T(8,128)(2,1)} %copy.239), calls=%async_computation.2 | async-start | bytes 7077888 | tf_op jit(solution)/shard_map/all_to_all | solution.py:202
  497.5 26.0 %all-to-all-start.3 = ((bf16[4,2,49344]{2,1,0:T(2,128)(2,1)}), bf16[4,2,49344]{2,1,0:T(2,128)(2,1)S(1)}, u32[]{:S(2)}, u32[]{:S(2)}) async-start(bf16[4,2,49344]{2,1,0:T(2,128)(2,1)} %reshape.765), calls=%async_computation.3 | async-start | bytes 1581056 | tf_op jit(solution)/shard_map/all_to_all | solution.py:204
  582.8 31.8 %all-to-all-start.4 = ((bf16[3,257,16,32]{1,3,0,2:T(8,128)(2,1)}), bf16[3,257,16,32]{1,3,0,2:T(8,128)(2,1)S(1)}, u32[]{:S(2)}, u32[]{:S(2)}) async-start(bf16[3,257,16,32]{1,3,0,2:T(8,128)(2,1)} %copy.248), calls=%async_computation.4 | async-start | bytes 2359296 | tf_op jit(solution)/shard_map/all_to_all | solution.py:261
  751.1 57.3 %all-to-all-start.5 = ((bf16[4,2,148032]{2,1,0:T(2,128)(2,1)}), bf16[4,2,148032]{2,1,0:T(2,128)(2,1)S(1)}, u32[]{:S(2)}, u32[]{:S(2)}) async-start(bf16[4,2,148032]{2,1,0:T(2,128)(2,1)} %reshape.767), calls=%async_computation.5 | async-start | bytes 4739072 | tf_op jit(solution)/shard_map/all_to_all | solution.py:263
  758.8 203.6 %all-reduce.8.cloned.1.call-start = ((), (), s32[]{:S(2)}) async-start(), calls=%async_computation.31 | async-start | bytes 1622016
  915.6 194.7 %reduce-scatter.26.cloned.1.call-start = ((), (), s32[]{:S(2)}) async-start(), calls=%async_computation.28 | async-start | bytes 1179648 | tf_op jit(solution)/shard_map/reduce_scatter | solution.py:428
  918.8 191.5 %reduce-scatter.30.cloned.1.call-start = ((), (), s32[]{:S(2)}) async-start(), calls=%async_computation.30 | async-start | bytes 4718592 | tf_op jit(solution)/shard_map/reduce_scatter | solution.py:430
  925.3 186.2 %reduce-scatter.28.cloned.1.call-start = ((), (), s32[]{:S(2)}) async-start(), calls=%async_computation.29 | async-start | bytes 4718592 | tf_op jit(solution)/shard_map/reduce_scatter | solution.py:429
  933.2 220.7 %reduce-scatter.22.cloned.1.call-start = ((), (), s32[]{:S(2)}) async-start(), calls=%async_computation.26 | async-start | bytes 1769472 | tf_op jit(solution)/shard_map/reduce_scatter | solution.py:426
  967.1 232.7 %reduce-scatter.16.cloned.1.call-start = ((), (), s32[]{:S(2)}) async-start(), calls=%async_computation.23 | async-start | bytes 2654208 | tf_op jit(solution)/shard_map/reduce_scatter | solution.py:423
  987.3 17.2 all-to-all-start.6
  992.3 257.9 %reduce-scatter.24.cloned.1.call-start = ((), (), s32[]{:S(2)}) async-start(), calls=%async_computation.27 | async-start | bytes 3538944 | tf_op jit(solution)/shard_map/reduce_scatter | solution.py:427
  999.6 297.1 %reduce-scatter.12.cloned.1.call-start = ((), (), s32[]{:S(2)}) async-start(), calls=%async_computation.21 | async-start | bytes 2654208 | tf_op jit(solution)/shard_map/reduce_scatter | solution.py:421
  1081.4 284.6 %reduce-scatter.14.cloned.1.call-start = ((), (), s32[]{:S(2)}) async-start(), calls=%async_computation.22 | async-start | bytes 7962624 | tf_op jit(solution)/shard_map/reduce_scatter | solution.py:422
  1088.1 357.9 %reduce-scatter.18.cloned.1.call-start = ((), (), s32[]{:S(2)}) async-start(), calls=%async_computation.24 | async-start | bytes 10616832 | tf_op jit(solution)/shard_map/reduce_scatter | solution.py:424
  1094.8 431.1 %reduce-scatter.20.cloned.1.call-start = ((), (), s32[]{:S(2)}) async-start(), calls=%async_computation.25 | async-start | bytes 10616832 | tf_op jit(solution)/shard_map/reduce_scatter | solution.py:425
  1101.4 561.7 %all-reduce.10.cloned.1.call-start = ((), (), s32[]{:S(2)}) async-start(), calls=%async_computation.32 | async-start | bytes 3284992 | tf_op jit(solution)/shard_map/psum | solution.py:459
  1110.2 758.4 %all-reduce.12.cloned.1.call-start = ((), (), s32[]{:S(2)}) async-start(), calls=%async_computation.33 | async-start | bytes 11206656 | tf_op jit(solution)/shard_map/psum | solution.py:432
  (153 other events, 4044.9 us)
Sparse Core Ops, SparseCore 0:
  9.6 87.9 all-gather.3
  100.1 88.5 all-gather.5
  191.1 45.5 all-gather.7
  915.7 46.6 all-reduce.7
  966.0 35.7 reduce-scatter.25
  1005.0 51.4 reduce-scatter.29
  1060.2 51.3 reduce-scatter.27
  1115.4 38.3 reduce-scatter.21
  1157.2 42.5 reduce-scatter.15
  1203.9 46.2 reduce-scatter.23
  1254.2 42.4 reduce-scatter.11
  1300.5 65.4 reduce-scatter.13
  1369.5 76.4 reduce-scatter.17
  1449.4 76.4 reduce-scatter.19
  1531.7 131.3 all-reduce.9
  1666.5 202.1 all-reduce.11
where the time goes:
time: 1910 us; the launch traced here: 1900 us
  waiting for transfers between devices  1090 us (57%)
  local copies, waits for them, and re-layouts  247 us (13%)
  matrix products  232 us (12%)
  other arithmetic  159 us (8%)
  blocking collectives  85 us (4%)
  starting transfers between devices  57.4 us (3%)
    psum x1, waiting for transfers between devices, shards(): lax.psum((shard_parts[0], shard_parts[1], shard_parts[2], shard_parts[3],...  199 us
    all_to_all x2, waiting for transfers between devices, layer_forward(): lax.all_to_all(mixed_qkv, 'seq', split_axis=3, concat_axis=1, tiled=True)  107 us
    psum x1, waiting for transfers between devices, shards(): lax.psum((grad_head, gain_grad, bias_grad, loss_part), ('fsdp', 'seq'))  95.1 us
    all_gather x1, waiting for transfers between devices, shards(): lax.all_gather(enc_w.astype(jnp.bfloat16), 'fsdp', axis=0, tiled=True)  87.4 us
    reduce_scatter x1, waiting for transfers between devices, shards(): lax.psum_scatter(enc_up, 'fsdp', scatter_dimension=0, tiled=True)  80 us
    reduce_scatter x1, waiting for transfers between devices, shards(): lax.psum_scatter(enc_down, 'fsdp', scatter_dimension=0, tiled=True)  79.9 us
    all_gather x1, waiting for transfers between devices, shards(): all_pixels = lax.all_gather(pixels, 'seq', axis=1, tiled=True)  79.1 us
    unnamed x351, local copies, waits for them, and re-layouts  73 us
  transfers between devices with their start and end apart: 23, of which 19 were waited for; matrix products, arithmetic and copies ran while one was open for 12% of the time, Pallas kernels for 0%

commit v1 on v0

v1 whole, which is shorter than its diff:
```python
from functools import partial

import jax
import jax.numpy as jnp
from jax import lax
from jax.experimental import pallas as pl
from jax.experimental.pallas import tpu as pltpu
from jax.sharding import PartitionSpec as P

D_E = 768
H_E = 12
FF_E = 3072
D_D = 512
H_D = 16
FF_D = 2048
PIX = 768
PATCHES = 1024
KEEP = 256
STEP = 5

NORM_EPS = 1e-06
PIXEL_EPS = 1e-06
BETA_ONE = 0.5
BETA_TWO = 0.75
MATRIX_RATE = 0.03
SMALL_RATE = 0.1
MATRIX_DECAY = 0.05
ADAM_EPS = 1e-08

TAIL = 16
E_ROWS = KEEP + TAIL
D_ROWS = PATCHES + TAIL
LOG2E = 1.4426950408889634
MASKED_SCORE = -1e30


def bias_widths():
    return [D_E] * 7 + [FF_E] + [D_E] * 2 + [D_D] * 7 + [FF_D] + [D_D] * 2 + [PIX]


def split_vector(vector, widths):
    pieces = []
    offset = 0
    for span_width in widths:
        pieces.append(vector[offset : offset + span_width])
        offset += span_width
    return pieces


def positions(index_arr, width_dim):
    halves = width_dim // 2
    frequency = 10000.0 ** (-jnp.arange(halves, dtype=jnp.float32) / halves)
    angles = (index_arr.astype(jnp.float32) + 1.0)[..., None] * frequency
    return jnp.concatenate([jnp.sin(angles), jnp.cos(angles)], axis=-1)


def norm_forward(inputs, gain_vec, shift_vec):
    centre = inputs - jnp.mean(inputs, axis=-1, keepdims=True)
    inverse = lax.rsqrt(jnp.mean(centre * centre, axis=-1, keepdims=True) + NORM_EPS)
    scaled = centre * inverse
    return (scaled * gain_vec + shift_vec, scaled, inverse)


def norm_backward(upstream, scaled, inverse, gain_vec):
    weighted = upstream * gain_vec
    inner_part = (
        weighted
        - jnp.mean(weighted, axis=-1, keepdims=True)
        - scaled * jnp.mean(weighted * scaled, axis=-1, keepdims=True)
    )
    return (
        inverse * inner_part,
        jnp.sum(upstream * scaled, axis=(0, 1)),
        jnp.sum(upstream, axis=(0, 1)),
    )


def low(tensor):
    return tensor.astype(jnp.bfloat16)


def project(row_block, weight):
    return jnp.einsum("isd,de->ise", row_block, weight, preferred_element_type=jnp.float32)


def project_back(row_block, weight):
    return jnp.einsum("ise,de->isd", row_block, weight, preferred_element_type=jnp.float32)


def weight_grad(row_block, upstream):
    return jnp.einsum("isd,ise->de", row_block, upstream, preferred_element_type=jnp.float32)


def row_sum(tensor):
    return jnp.sum(tensor.astype(jnp.float32), axis=(0, 1))


def enc_mats_of(full_rows):
    return (
        full_rows[:, D_E : 4 * D_E],
        full_rows[:, 4 * D_E : 5 * D_E],
        full_rows[:, 5 * D_E : 5 * D_E + FF_E],
        full_rows[:, 5 * D_E + FF_E : 5 * D_E + 2 * FF_E],
    )


def dot_f32(left, right, contract):
    return lax.dot_general(
        left, right, (contract, ((), ())), preferred_element_type=jnp.float32
    )


NN = ((1,), (0,))
TN = ((0,), (0,))


def pieces_of(value):
    first = low(value).astype(jnp.float32)
    rest = value - first
    second = low(rest).astype(jnp.float32)
    return first, second, rest - second


def own_span(shape, axis, head, head_dim):
    place = lax.broadcasted_iota(jnp.int32, shape, axis)
    return (place >= head * head_dim) & (place < (head + 1) * head_dim)


def live_tail(rows, scores, other):
    place = lax.broadcasted_iota(jnp.int32, (rows, scores.shape[1]), 0)
    return jnp.where(place < 1, scores, other)


def attend_forward_kernel(heads, head_dim, q_ref, k_ref, v_ref, o_ref, lse_ref):
    main = k_ref.shape[1] - TAIL
    scale = head_dim ** (-0.5) * LOG2E
    q_t = q_ref[0].astype(jnp.float32).T * scale
    q_high = low(q_t)
    q_rest = low(q_t - q_high.astype(jnp.float32))
    k_main = k_ref[0, :main]
    k_tail = k_ref[0, main:]
    k_main = jnp.concatenate([k_main, k_main], axis=1)
    k_tail = jnp.concatenate([k_tail, k_tail], axis=1)
    v_main = low(v_ref[0, :main].astype(jnp.float32).T)
    v_tail = v_ref[0, main:]
    ones = jnp.ones((TAIL, main), jnp.bfloat16)

    def scores_of(head):
        own = own_span(q_t.shape, 0, head, head_dim)
        none = jnp.zeros_like(q_high)
        q_h = jnp.concatenate([jnp.where(own, q_high, none), jnp.where(own, q_rest, none)], axis=0)
        return dot_f32(k_main, q_h, NN), live_tail(TAIL, dot_f32(k_tail, q_h, NN), MASKED_SCORE)

    outs = []
    following = scores_of(0)
    for head in range(heads):
        span = slice(head * head_dim, (head + 1) * head_dim)
        s_main, s_tail = following
        if head + 1 < heads:
            following = scores_of(head + 1)
        top = jnp.maximum(
            jnp.max(s_main, axis=0, keepdims=True), jnp.max(s_tail, axis=0, keepdims=True)
        )
        p_main = low(jnp.exp2(s_main - top))
        p_tail = low(jnp.exp2(s_tail - top))
        o_t = dot_f32(jnp.concatenate([v_main[span], ones], axis=0), p_main, NN)
        total = o_t[head_dim : head_dim + 1] + jnp.sum(
            p_tail.astype(jnp.float32), axis=0, keepdims=True
        )
        o_t = o_t[:head_dim] + dot_f32(v_tail, p_tail, TN)[span]
        outs.append(o_t * (1.0 / total))
        lse_ref[0, 0, head : head + 1, :] = top + jnp.log2(total)
    o_ref[0] = low(jnp.concatenate(outs, axis=0).T)


def attend_backward_kernel(
    heads, head_dim, q_ref, k_ref, v_ref, lse_ref, do_ref, o_ref, dq_ref, dk_ref, dv_ref
):
    main = k_ref.shape[1] - TAIL
    rows = q_ref.shape[1]
    unit = head_dim ** (-0.5)
    q = q_ref[0]
    do = do_ref[0]
    q_t = q.astype(jnp.float32).T * (unit * LOG2E)
    q_high = low(q_t).astype(jnp.float32)
    q_rest = q_t - q_high
    do_t = do.astype(jnp.float32).T
    inner_t = do_t * o_ref[0].astype(jnp.float32).T
    place = lax.broadcasted_iota(jnp.int32, q_t.shape, 0)

    def with_row(block, offset, value):
        for at, part in enumerate(pieces_of(value)):
            block = jnp.where(place == offset + at, part, block)
        return block

    score_sides, value_sides = [], []
    for head in range(heads):
        own = own_span(q_t.shape, 0, head, head_dim)
        span = slice(head * head_dim, (head + 1) * head_dim)
        other = ((head + 1) % heads) * head_dim
        lse = lse_ref[0, 0, head : head + 1, :]
        inner = jnp.sum(inner_t[span], axis=0, keepdims=True)
        rest = with_row(jnp.where(own, q_rest, 0.0), other, -lse)
        score_sides.append(low(jnp.concatenate([jnp.where(own, q_high, 0.0), rest], axis=0)))
        last = with_row(jnp.zeros_like(do_t), 0, -inner)
        value_sides.append(low(jnp.concatenate([jnp.where(own, do_t, 0.0), last], axis=0)))
    zero = jnp.zeros_like(q)
    q_sides = [jnp.where(own_span(q.shape, 1, h, head_dim), q, zero) for h in range(heads)]
    do_sides = [jnp.where(own_span(q.shape, 1, h, head_dim), do, zero) for h in range(heads)]
    stacked = rows % 128 == 0
    if stacked:
        q_sides = jnp.concatenate(q_sides, axis=0)
        do_sides = jnp.concatenate(do_sides, axis=0)

    def sum_heads(parts, sides):
        if stacked:
            return dot_f32(jnp.concatenate(parts, axis=1), sides, NN)
        terms = [dot_f32(part, side, NN) for part, side in zip(parts, sides)]
        return sum(terms[1:], terms[0])

    k_main = k_ref[0, :main]
    k_tail = k_ref[0, main:]
    k_main_t = low(k_main.astype(jnp.float32).T)

    def with_ones(block):
        return jnp.concatenate([block, jnp.ones_like(block)], axis=1)

    def beside_own(block, head):
        own = jnp.where(own_span(block.shape, 1, head, head_dim), block, jnp.ones_like(block))
        return jnp.concatenate([block, own], axis=1)

    v_main = with_ones(v_ref[0, :main])
    v_tail = with_ones(v_ref[0, main:])
    dq_parts, p_mains, s_mains, p_tails, s_tails = [], [], [], [], []
    for head in range(heads):
        span = slice(head * head_dim, (head + 1) * head_dim)
        p = jnp.exp2(dot_f32(beside_own(k_main, head), score_sides[head], NN))
        s = low(p * dot_f32(v_main, value_sides[head], NN))
        p_mains.append(low(p))
        s_mains.append(s)
        p = jnp.exp2(dot_f32(beside_own(k_tail, head), score_sides[head], NN))
        p = live_tail(TAIL, p, 0.0)
        s_tail = low(p * dot_f32(v_tail, value_sides[head], NN))
        p_tails.append(low(p))
        s_tails.append(s_tail)
        dq_parts.append(dot_f32(k_main_t[span], s, NN) + dot_f32(k_tail, s_tail, TN)[span])
    dk_ref[0, :main] = low(sum_heads(s_mains, q_sides) * unit)
    dk_ref[0, main:] = low(sum_heads(s_tails, q_sides) * unit)
    dv_ref[0, :main] = low(sum_heads(p_mains, do_sides))
    dv_ref[0, main:] = low(sum_heads(p_tails, do_sides))
    dq_ref[0] = low(jnp.concatenate(dq_parts, axis=0).T * unit)


VMEM_LIMIT = 32 * 1024 * 1024


def attend_specs(q_rows, k_rows, heads):
    return (
        pl.BlockSpec((1, q_rows, 128), lambda i, g: (i, 0, g)),
        pl.BlockSpec((1, k_rows, 128), lambda i, g: (i, 0, g)),
        pl.BlockSpec((1, 1, heads, q_rows), lambda i, g: (i, g, 0, 0)),
    )


def attend_forward(queries, key_rows, value_rows, head_count):
    images, q_rows, width = queries.shape
    k_rows = key_rows.shape[1]
    head_dim = width // head_count
    heads = 128 // head_dim
    groups = width // 128
    q_spec, k_spec, l_spec = attend_specs(q_rows, k_rows, heads)
    return pl.pallas_call(
        partial(attend_forward_kernel, heads, head_dim),
        grid=(images, groups),
        in_specs=[q_spec, k_spec, k_spec],
        out_specs=[q_spec, l_spec],
        out_shape=[
            jax.ShapeDtypeStruct((images, q_rows, width), jnp.bfloat16),
            jax.ShapeDtypeStruct((images, groups, heads, q_rows), jnp.float32),
        ],
        compiler_params=pltpu.CompilerParams(vmem_limit_bytes=VMEM_LIMIT),
        cost_estimate=pl.CostEstimate(
            flops=16 * images * q_rows * k_rows * width,
            bytes_accessed=4 * images * (q_rows + k_rows) * width,
            transcendentals=images * head_count * q_rows * k_rows,
        ),
    )(queries, key_rows, value_rows)


def attend_backward(queries, key_rows, value_rows, logsum, upstream, attended, head_count):
    images, q_rows, width = queries.shape
    k_rows = key_rows.shape[1]
    head_dim = width // head_count
    heads = 128 // head_dim
    groups = width // 128
    q_spec, k_spec, l_spec = attend_specs(q_rows, k_rows, heads)
    return pl.pallas_call(
        partial(attend_backward_kernel, heads, head_dim),
        grid=(images, groups),
        in_specs=[q_spec, k_spec, k_spec, l_spec, q_spec, q_spec],
        out_specs=[q_spec, k_spec, k_spec],
        out_shape=[
            jax.ShapeDtypeStruct((images, q_rows, width), jnp.bfloat16),
            jax.ShapeDtypeStruct((images, k_rows, width), jnp.bfloat16),
            jax.ShapeDtypeStruct((images, k_rows, width), jnp.bfloat16),
        ],
        compiler_params=pltpu.CompilerParams(vmem_limit_bytes=VMEM_LIMIT),
        cost_estimate=pl.CostEstimate(
            flops=40 * images * q_rows * k_rows * width,
            bytes_accessed=8 * images * (q_rows + k_rows) * width,
            transcendentals=images * head_count * q_rows * k_rows,
        ),
    )(queries, key_rows, value_rows, logsum, upstream, attended)


MESH = pl.DeviceIdType.MESH


def line_sum_kernel(
    chunks, x_ref, o_ref, from_left, from_right, to_left, to_right, send_sem, recv_sem
):
    count = lax.axis_size("seq")
    place = lax.axis_index("seq")
    has_left = place > 0
    has_right = place < count - 1
    rows = x_ref.shape[0] // chunks
    barrier = pltpu.get_barrier_semaphore()

    def greet(to):
        pl.semaphore_signal(barrier, inc=1, device_id={"seq": to}, device_id_type=MESH)

    pl.when(has_left)(lambda: greet(place - 1))
    pl.when(has_right)(lambda: greet(place + 1))
    peers = jnp.where(has_left, 1, 0) + jnp.where(has_right, 1, 0)
    pl.semaphore_wait(barrier, peers)

    def copy(way, at):
        span = pl.ds(at * rows, rows)
        source, target = ((to_right, from_left), (to_left, from_right))[way]
        return pltpu.make_async_remote_copy(
            src_ref=source.at[span],
            dst_ref=target.at[span],
            send_sem=send_sem.at[way, at],
            recv_sem=recv_sem.at[way, at],
            device_id={"seq": place + 1 if way == 0 else place - 1},
            device_id_type=MESH,
        )

    def end_copy(way, at):
        span = pl.ds(at * rows, rows)
        return pltpu.make_async_remote_copy(
            src_ref=x_ref.at[span],
            dst_ref=(from_left, from_right)[way].at[span],
            send_sem=send_sem.at[way, at],
            recv_sem=recv_sem.at[way, at],
            device_id={"seq": place + 1 if way == 0 else place - 1},
            device_id_type=MESH,
        )

    for way, is_end in ((0, jnp.logical_not(has_left)), (1, jnp.logical_not(has_right))):

        @pl.when(is_end)
        def _():
            for at in range(chunks):
                if at >= 2:
                    end_copy(way, at - 2).wait_send()
                end_copy(way, at).start()
            for at in range(chunks - 2, chunks):
                end_copy(way, at).wait_send()

    for at in range(chunks):
        span = pl.ds(at * rows, rows)

        @pl.when(has_left)
        def _():
            copy(0, at).wait_recv()

            @pl.when(has_right)
            def _():
                to_right[span] = x_ref[span] + from_left[span]
                copy(0, at).start()

        @pl.when(has_right)
        def _():
            copy(1, at).wait_recv()

            @pl.when(has_left)
            def _():
                to_left[span] = x_ref[span] + from_right[span]
                copy(1, at).start()

        @pl.when(has_left & has_right)
        def _():
            o_ref[span] = (x_ref[span] + from_left[span]) + from_right[span]

        @pl.when(jnp.logical_not(has_left))
        def _():
            o_ref[span] = x_ref[span] + from_right[span]

        @pl.when(jnp.logical_not(has_right))
        def _():
            o_ref[span] = x_ref[span] + from_left[span]

    @pl.when(has_left & has_right)
    def _():
        for at in range(chunks):
            copy(0, at).wait_send()
            copy(1, at).wait_send()


def line_sum(block, chunks, collective_id):
    shape = jax.ShapeDtypeStruct(block.shape, block.dtype)
    buffer = pltpu.VMEM(block.shape, block.dtype)
    return pl.pallas_call(
        partial(line_sum_kernel, chunks),
        out_shape=shape,
        in_specs=[pl.BlockSpec(memory_space=pltpu.VMEM)],
        out_specs=pl.BlockSpec(memory_space=pltpu.VMEM),
        scratch_shapes=[buffer] * 4
        + [pltpu.SemaphoreType.DMA((2, chunks)), pltpu.SemaphoreType.DMA((2, chunks))],
        compiler_params=pltpu.CompilerParams(
            collective_id=collective_id, has_side_effects=True, vmem_limit_bytes=VMEM_LIMIT
        ),
        cost_estimate=pl.CostEstimate(
            flops=0, bytes_accessed=100 * block.size, transcendentals=0
        ),
    )(block)


SMALL_BLOCK = (8, 384)
PLANE = 8


def exchange_kernel(
    chunks,
    g_ref,
    small_ref,
    out_ref,
    small_out,
    pair_in,
    plane_send,
    plane_recv,
    small_in,
    small_line,
    pair_sems,
    plane_sems,
    line_sems,
    small_plane_sems,
    small_line_sems,
    small_out_sems,
):
    own = lax.axis_index("fsdp")
    place = lax.axis_index("seq")
    line = lax.axis_size("seq")
    core = lax.rem(own, 2)
    chip = lax.div(own, 2)
    partner = own + 1 - 2 * core
    block = g_ref.shape[0] // PLANE
    rows = block // chunks

    def plane_peer(step):
        return lax.rem(own + step, PLANE)

    def line_peer(step):
        return lax.rem(place + step, line)

    barrier = pltpu.get_barrier_semaphore()
    for step in range(1, PLANE):
        pl.semaphore_signal(
            barrier, inc=1, device_id={"fsdp": plane_peer(step)}, device_id_type=MESH
        )
    for step in range(1, line):
        pl.semaphore_signal(
            barrier, inc=1, device_id={"seq": line_peer(step)}, device_id_type=MESH
        )
    pl.semaphore_wait(barrier, PLANE - 1 + line - 1)

    def send(source, target, sems, at, device):
        return pltpu.make_async_remote_copy(
            src_ref=source,
            dst_ref=target,
            send_sem=sems.at[(0,) + at],
            recv_sem=sems.at[(1,) + at],
            device_id=device,
            device_id_type=MESH,
        )

    def owned_rows(owner, at):
        return pl.ds(pl.multiple_of(owner * block + at * rows, 16), rows)

    def pair_copy(other, at):
        target = lax.rem(chip + other, 4)
        return send(
            g_ref.at[owned_rows(2 * target + 1 - core, at)],
            pair_in.at[other, pl.ds(at * rows, rows)],
            pair_sems,
            (other, at),
            {"fsdp": partner},
        )

    def plane_copy(other, at):
        target = lax.rem(chip + other, 4)
        span = pl.ds(at * rows, rows)
        return send(
            plane_send.at[other - 1, span],
            plane_recv.at[other - 1, span],
            plane_sems,
            (other - 1, at),
            {"fsdp": 2 * target + core},
        )

    def line_copy(step, at):
        span = pl.ds(at * rows, rows)
        return send(
            out_ref.at[place, span],
            out_ref.at[place, span],
            line_sems,
            (step - 1, at),
            {"seq": line_peer(step)},
        )

    def small_plane_copy(step):
        return send(
            small_ref.at[plane_peer(step)],
            small_in.at[step - 1],
            small_plane_sems,
            (step - 1,),
            {"fsdp": plane_peer(step)},
        )

    def small_line_copy(step):
        return send(
            small_line.at[place],
            small_line.at[place],
            small_line_sems,
            (step - 1,),
            {"seq": line_peer(step)},
        )

    def small_out_copy(step):
        return send(
            small_out.at[own],
            small_out.at[own],
            small_out_sems,
            (step - 1,),
            {"fsdp": plane_peer(step)},
        )

    for at in range(chunks):
        for other in (1, 2, 3, 0):
            pair_copy(other, at).start()
        if at == 0:
            for step in range(1, PLANE):
                small_plane_copy(step).start()
    for at in range(chunks):
        for other in (1, 2, 3, 0):
            pair_copy(other, at).wait_recv()
            if other:
                span = pl.ds(at * rows, rows)
                target = lax.rem(chip + other, 4)
                both = g_ref[owned_rows(2 * target + core, at)] + pair_in[other, span]
                plane_send[other - 1, span] = low(both)
                plane_copy(other, at).start()
    for step in range(1, PLANE):
        small_plane_copy(step).wait_recv()
    total = small_ref[own]
    for step in range(1, PLANE):
        total = total + small_in[step - 1]
    small_line[place] = total
    for step in range(1, line):
        small_line_copy(step).start()
    for at in range(chunks):
        span = pl.ds(at * rows, rows)
        total = g_ref[owned_rows(own, at)] + pair_in[0, span]
        for other in (1, 2, 3):
            plane_copy(other, at).wait_recv()
            total = total + plane_recv[other - 1, span].astype(jnp.float32)
        out_ref[place, span] = low(total)
        for step in range(1, line):
            line_copy(step, at).start()
    for step in range(1, line):
        small_line_copy(step).wait_recv()
    total = small_line[0]
    for at in range(1, small_line.shape[0]):
        total = total + small_line[at]
    small_out[own] = total
    for step in range(1, PLANE):
        small_out_copy(step).start()
    for step in range(1, PLANE):
        small_out_copy(step).wait()
        small_plane_copy(step).wait_send()
    for step in range(1, line):
        small_line_copy(step).wait_send()
        for at in range(chunks):
            line_copy(step, at).wait()
    for at in range(chunks):
        for other in range(4):
            pair_copy(other, at).wait_send()
            if other:
                plane_copy(other, at).wait_send()


def exchange(grads, small, line, collective_id, chunks=3):
    plane = lax.axis_size("fsdp")
    total, width = grads.shape
    if plane != PLANE or total % (PLANE * 16 * chunks):
        own = lax.psum_scatter(grads, "fsdp", scatter_dimension=0, tiled=True)
        return lax.all_gather(low(own), "seq", axis=0, tiled=False), lax.psum(
            small, ("fsdp", "seq")
        )
    block = total // PLANE
    padded = PLANE * SMALL_BLOCK[0] * SMALL_BLOCK[1]
    blocks = jnp.pad(small, (0, padded - small.shape[0])).reshape((PLANE,) + SMALL_BLOCK)
    dma = pltpu.SemaphoreType.DMA
    gathered, summed = pl.pallas_call(
        partial(exchange_kernel, chunks),
        out_shape=[
            jax.ShapeDtypeStruct((line, block, width), jnp.bfloat16),
            jax.ShapeDtypeStruct(blocks.shape, jnp.float32),
        ],
        in_specs=[pl.BlockSpec(memory_space=pltpu.VMEM)] * 2,
        out_specs=[pl.BlockSpec(memory_space=pltpu.VMEM)] * 2,
        scratch_shapes=[
            pltpu.VMEM((4, block, width), jnp.float32),
            pltpu.VMEM((3, block, width), jnp.bfloat16),
            pltpu.VMEM((3, block, width), jnp.bfloat16),
            pltpu.VMEM((PLANE - 1,) + SMALL_BLOCK, jnp.float32),
            pltpu.VMEM((line,) + SMALL_BLOCK, jnp.float32),
            dma((2, 4, chunks)),
            dma((2, 3, chunks)),
            dma((2, line - 1, chunks)),
            dma((2, PLANE - 1)),
            dma((2, line - 1)),
            dma((2, PLANE - 1)),
        ],
        compiler_params=pltpu.CompilerParams(
            collective_id=collective_id, has_side_effects=True, vmem_limit_bytes=VMEM_LIMIT
        ),
        cost_estimate=pl.CostEstimate(
            flops=0, bytes_accessed=200 * 1024 * 1024, transcendentals=0
        ),
    )(grads, blocks)
    return gathered, summed.reshape(-1)


def gelu_parts(hidden):
    cdf = 0.5 * (1.0 + lax.erf(hidden * (2.0**-0.5)))
    density = jnp.exp(-0.5 * hidden * hidden) * (0.3989422804014327)
    return hidden * cdf, cdf + hidden * density


def adamw(weight, moment_one, moment_two, gradient, step_rate, decay_rate):
    moment_one = BETA_ONE * moment_one + (1 - BETA_ONE) * gradient
    moment_two = BETA_TWO * moment_two + (1 - BETA_TWO) * gradient * gradient
    fixed_one = moment_one / (1 - BETA_ONE**STEP)
    fixed_two = moment_two / (1 - BETA_TWO**STEP)
    weight = weight - step_rate * (
        fixed_one / (jnp.sqrt(fixed_two) + ADAM_EPS) + decay_rate * weight
    )
    return (moment_one, moment_two, weight)


def shards(
    pixels,
    restore,
    enc_w,
    enc_m,
    enc_v,
    dec_w,
    dec_m,
    dec_v,
    head_w,
    head_m,
    head_v,
    gain_w,
    gain_m,
    gain_v,
    bias_w,
    bias_m,
    bias_v,
):
    seq_count = lax.axis_size("seq")
    place = lax.axis_index("seq")
    images, own_count, _ = pixels.shape
    masked_total = images * lax.axis_size("fsdp") * (PATCHES - KEEP)

    enc_low = low(enc_w)
    enc_first = lax.all_gather(enc_low[:, : 5 * D_E], "fsdp", axis=0, tiled=True)
    enc_second = lax.all_gather(enc_low[:, 5 * D_E :], "fsdp", axis=0, tiled=True)
    dec_full = lax.all_gather(low(dec_w), "fsdp", axis=0, tiled=True)
    head_low = low(head_w)
    w_patch = enc_first[:, :D_E]
    e_qkv = enc_first[:, D_E : 4 * D_E]
    e_out = enc_first[:, 4 * D_E :]
    e_up = enc_second[:, :FF_E]
    e_down = enc_second[:, FF_E : 2 * FF_E]
    w_embed = enc_second[:, 2 * FF_E :]
    d_query = dec_full[:, :D_D]
    d_key = dec_full[:, D_D : 2 * D_D]
    d_value = dec_full[:, 2 * D_D : 3 * D_D]
    d_out = dec_full[:, 3 * D_D : 4 * D_D]
    d_up = dec_full[:, 4 * D_D : 4 * D_D + FF_D]
    d_down = dec_full[:, 4 * D_D + FF_D :]

    pieces = split_vector(bias_w, bias_widths())
    gains = split_vector(gain_w, [D_E, D_E, D_E, D_D, D_D, D_D])
    (b_patch, cls_token, e_shift1, e_bq, e_bv, e_bo, e_shift2, e_bu, e_bd, e_shift3) = pieces[:10]
    (b_embed, mask_token, d_shift1, d_bq, d_bv, d_bo, d_shift2, d_bu, d_bd, d_shift3) = pieces[
        10:20
    ]
    b_head = pieces[20]

    ranks = jnp.arange(KEEP, dtype=jnp.int32)
    turned = lax.dynamic_slice_in_dim(
        jnp.concatenate([restore, restore], axis=1), place * own_count, PATCHES, axis=1
    )
    own_restore = turned[:, :own_count]
    own_pick = low(own_restore[:, None, :] == ranks[None, :, None])
    own_kept = jnp.einsum("irp,ipd->ird", own_pick, pixels, preferred_element_type=jnp.float32)
    kept = line_sum(low(own_kept).reshape(images * KEEP, PIX), 8, 0).reshape(images, KEEP, PIX)
    patch_ids = jnp.arange(PATCHES, dtype=jnp.int32)
    keep_ids = jnp.sum(
        jnp.where(restore[:, None, :] == ranks[None, :, None], patch_ids, 0), axis=2
    )

    embedded = project(kept, w_patch) + (b_patch + positions(keep_ids, D_E))
    e_tail = jnp.where(jnp.arange(TAIL)[:, None] == 0, cls_token[None, :], 0.0)
    x0 = jnp.concatenate(
        [embedded, jnp.broadcast_to(e_tail[None], (images, TAIL, D_E))], axis=1
    )
    e_n1, e_sc1, e_inv1 = norm_forward(x0, gains[0], e_shift1)
    e_n1 = low(e_n1)
    e_qkv_bias = jnp.concatenate([e_bq, jnp.zeros_like(e_bq), e_bv])
    e_mixed = low(project(e_n1, e_qkv) + e_qkv_bias)
    e_q = e_mixed[:, :, :D_E]
    e_k = e_mixed[:, :, D_E : 2 * D_E]
    e_v = e_mixed[:, :, 2 * D_E :]
    e_o, e_lse = attend_forward(e_q, e_k, e_v, H_E)
    e_mid = x0 + project(e_o, e_out) + e_bo
    e_n2, e_sc2, e_inv2 = norm_forward(e_mid, gains[1], e_shift2)
    e_n2 = low(e_n2)
    e_hidden = project(e_n2, e_up) + e_bu
    e_gelu, e_slope = gelu_parts(e_hidden)
    e_act = low(e_gelu)
    encoded = e_mid + project_back(e_act, e_down) + e_bd
    e_n3, e_sc3, e_inv3 = norm_forward(encoded, gains[2], e_shift3)
    e_n3 = low(e_n3)
    shrunk = low(project(e_n3, w_embed) + b_embed)

    pick = low(turned[:, :, None] == ranks[None, None, :])
    is_masked = turned >= KEEP
    turned_ids = lax.rem(patch_ids + place * own_count, PATCHES)
    spread = jnp.einsum(
        "ipr,ird->ipd", pick, shrunk[:, :KEEP], preferred_element_type=jnp.float32
    )
    patch_rows = (
        jnp.where(is_masked[..., None], mask_token, spread) + positions(turned_ids, D_D)[None]
    )
    d_tail = jnp.where(
        jnp.arange(TAIL)[None, :, None] == 0,
        shrunk[:, KEEP : KEEP + 1].astype(jnp.float32),
        0.0,
    )
    y0 = jnp.concatenate([patch_rows, d_tail], axis=1)
    d_n1, d_sc1, d_inv1 = norm_forward(y0, gains[3], d_shift1)
    d_n1 = low(d_n1)

    y0_own = y0[:, :own_count]
    n1_own = d_n1[:, :own_count]
    d_q = low(project(n1_own, d_query) + d_bq)
    d_k = low(project(d_n1, d_key))
    d_v = low(project(d_n1, d_value) + d_bv)
    d_o, d_lse = attend_forward(d_q, d_k, d_v, H_D)
    d_mid = y0_own + project(d_o, d_out) + d_bo
    d_n2, d_sc2, d_inv2 = norm_forward(d_mid, gains[4], d_shift2)
    d_n2 = low(d_n2)
    d_hidden = project(d_n2, d_up) + d_bu
    d_gelu, d_slope = gelu_parts(d_hidden)
    d_act = low(d_gelu)
    decoded = d_mid + project_back(d_act, d_down) + d_bd
    d_n3, d_sc3, d_inv3 = norm_forward(decoded, gains[5], d_shift3)
    d_n3 = low(d_n3)
    predicted = project(d_n3, head_low) + b_head
    targets = pixels.astype(jnp.float32)
    centre = targets - jnp.mean(targets, axis=-1, keepdims=True)
    targets = centre * lax.rsqrt(
        jnp.sum(centre * centre, axis=-1, keepdims=True) / (PIX - 1) + PIXEL_EPS
    )
    errors = predicted - targets
    own_masked = (own_restore >= KEEP)[..., None]
    loss_part = (
        jnp.sum(jnp.where(own_masked, jnp.mean(errors * errors, axis=-1, keepdims=True), 0.0))
        / masked_total
    )

    pred_grad = jnp.where(own_masked, errors * (2.0 / (PIX * masked_total)), 0.0)
    pred_low = low(pred_grad)
    g_head = weight_grad(d_n3, pred_low)
    g_b_head = row_sum(pred_grad)
    d_up3, g_d_gain3, g_d_shift3 = norm_backward(
        project_back(pred_low, head_low), d_sc3, d_inv3, gains[5]
    )
    d_up3_low = low(d_up3)
    g_d_down = weight_grad(d_up3_low, d_act)
    g_d_bd = row_sum(d_up3)
    d_dhidden = low(project(d_up3_low, d_down) * d_slope)
    g_d_up = weight_grad(d_n2, d_dhidden)
    g_d_bu = row_sum(d_dhidden)
    through, g_d_gain2, g_d_shift2 = norm_backward(
        project_back(d_dhidden, d_up), d_sc2, d_inv2, gains[4]
    )
    d_dmid = d_up3 + through
    d_dmid_low = low(d_dmid)
    g_d_out = weight_grad(d_o, d_dmid_low)
    g_d_bo = row_sum(d_dmid)
    d_do = low(project_back(d_dmid_low, d_out))
    late_grads, d_do = lax.optimization_barrier(
        (jnp.concatenate([g_d_out, g_d_up, g_d_down, g_head], axis=1), d_do)
    )
    dec_late = lax.psum_scatter(late_grads, "fsdp", scatter_dimension=0, tiled=True)
    d_dq, d_dk, d_dv = attend_backward(d_q, d_k, d_v, d_lse, d_do, d_o, H_D)
    g_d_qkv = jnp.concatenate(
        [weight_grad(n1_own, d_dq), weight_grad(d_n1, d_dk), weight_grad(d_n1, d_dv)], axis=1
    )
    g_d_bq = row_sum(d_dq)
    g_d_bv = row_sum(d_dv)
    dn1 = project_back(d_dk, d_key) + project_back(d_dv, d_value)
    others = ((0, 0), (0, D_ROWS - own_count), (0, 0))
    dn1 = dn1 + jnp.pad(project_back(d_dq, d_query), others)
    dy0, g_d_gain1, g_d_shift1 = norm_backward(dn1, d_sc1, d_inv1, gains[3])
    dy0 = dy0 + jnp.pad(d_dmid, others)
    dy0_patch = dy0[:, :PATCHES]
    g_mask = jnp.sum(jnp.where(is_masked[..., None], dy0_patch, 0.0), axis=(0, 1))
    dy0_high = low(dy0_patch)
    dy0_rest = low(dy0_patch - dy0_high.astype(jnp.float32))
    de_patch = jnp.einsum(
        "ipr,ipd->ird", pick, dy0_high, preferred_element_type=jnp.float32
    ) + jnp.einsum("ipr,ipd->ird", pick, dy0_rest, preferred_element_type=jnp.float32)
    de_part = jnp.concatenate(
        [de_patch.reshape(images * KEEP, D_D), dy0[:, PATCHES], jnp.zeros((TAIL - images, D_D))],
        axis=0,
    )
    g_d_qkv, de_part = lax.optimization_barrier((g_d_qkv, low(de_part)))
    dec_early = lax.psum_scatter(g_d_qkv, "fsdp", scatter_dimension=0, tiled=True)
    de_sum = line_sum(de_part, 7, 1)
    dec_late, de_sum = lax.optimization_barrier((dec_late, de_sum))
    de = jnp.concatenate(
        [
            de_sum[: images * KEEP].reshape(images, KEEP, D_D),
            jnp.pad(de_sum[images * KEEP :][:images, None], ((0, 0), (0, TAIL - 1), (0, 0))),
        ],
        axis=1,
    )

    def own_columns(tensor):
        size = tensor.shape[2] // seq_count
        return lax.dynamic_slice_in_dim(tensor, place * size, size, axis=2)

    g_embed = weight_grad(e_n3, own_columns(de))
    g_b_embed = row_sum(de)
    e_up3, g_e_gain3, g_e_shift3 = norm_backward(
        project_back(de, w_embed), e_sc3, e_inv3, gains[2]
    )
    e_up3_low = low(e_up3)
    g_e_down = weight_grad(e_up3_low, own_columns(e_act))
    g_e_bd = row_sum(e_up3)
    e_dhidden = low(project(e_up3_low, e_down) * e_slope)
    g_e_up = weight_grad(e_n2, own_columns(e_dhidden))
    g_e_bu = row_sum(e_dhidden)
    through, g_e_gain2, g_e_shift2 = norm_backward(
        project_back(e_dhidden, e_up), e_sc2, e_inv2, gains[1]
    )
    e_dmid = e_up3 + through
    e_dmid_low = low(e_dmid)
    g_e_out = weight_grad(e_o, own_columns(e_dmid_low))
    g_e_bo = row_sum(e_dmid)
    e_do = low(project_back(e_dmid_low, e_out))
    dec_early, e_do = lax.optimization_barrier((dec_early, e_do))
    dec_grad_all = lax.psum(jnp.concatenate([dec_early, dec_late], axis=1), "seq")
    e_dq, e_dk, e_dv = attend_backward(e_q, e_k, e_v, e_lse, e_do, e_o, H_E)
    g_e_qkv = [weight_grad(e_n1, own_columns(part)) for part in (e_dq, e_dk, e_dv)]
    g_e_bq = row_sum(e_dq)
    g_e_bv = row_sum(e_dv)
    e_dmixed = jnp.concatenate([e_dq, e_dk, e_dv], axis=2)
    through, g_e_gain1, g_e_shift1 = norm_backward(
        project_back(e_dmixed, e_qkv), e_sc1, e_inv1, gains[0]
    )
    dx0 = e_dmid + through
    dx0_patch = dx0[:, :KEEP]
    g_patch = weight_grad(kept, own_columns(low(dx0_patch)))
    g_b_patch = row_sum(dx0_patch)
    g_cls = jnp.sum(dx0[:, KEEP], axis=0)
    enc_grads = jnp.concatenate([g_patch] + g_e_qkv + [g_e_out, g_e_up, g_e_down], axis=1)
    embed_own = lax.psum_scatter(g_embed, "fsdp", scatter_dimension=0, tiled=True)
    embed_all = lax.all_gather(embed_own, "seq", axis=0, tiled=False)

    once = jnp.where(place == 0, 1.0, 0.0)
    enc_bias = [g_b_patch, g_cls, g_e_shift1, g_e_bq, g_e_bv, g_e_bo, g_e_shift2, g_e_bu]
    enc_bias = jnp.concatenate(enc_bias + [g_e_bd, g_e_shift3, g_b_embed]) * once
    dec_bias = [g_mask, g_d_shift1, g_d_bq, g_d_bv, g_d_bo, g_d_shift2, g_d_bu, g_d_bd]
    dec_bias = jnp.concatenate(dec_bias + [g_d_shift3, g_b_head])
    enc_gain = jnp.concatenate([g_e_gain1, g_e_gain2, g_e_gain3]) * once
    dec_gain = jnp.concatenate([g_d_gain1, g_d_gain2, g_d_gain3])
    small = jnp.concatenate([enc_gain, dec_gain, enc_bias, dec_bias, loss_part[None]])
    dec_grad_all, enc_grads = lax.optimization_barrier((dec_grad_all, enc_grads))
    enc_all, small = exchange(enc_grads, small, seq_count, 2)
    dec_grad = dec_grad_all[:, : 4 * D_D + 2 * FF_D]
    head_grad = lax.all_gather(
        dec_grad_all[:, 4 * D_D + 2 * FF_D :], "fsdp", axis=0, tiled=True
    )

    def by_column(gathered, offset, size):
        return [gathered[at, :, offset : offset + size] for at in range(seq_count)]

    quarter_e = D_E // seq_count
    quarter_f = FF_E // seq_count
    spans = []
    for at in range(5):
        spans += by_column(enc_all, at * quarter_e, quarter_e)
    spans += by_column(enc_all, 5 * quarter_e, quarter_f)
    spans += by_column(enc_all, 5 * quarter_e + quarter_f, quarter_f)
    spans = [part.astype(jnp.float32) for part in spans]
    enc_grad = jnp.concatenate(spans + [embed_all[at] for at in range(seq_count)], axis=1)
    n_gain = gain_w.shape[0]
    n_bias = bias_w.shape[0]
    gain_grad = small[:n_gain]
    bias_grad = small[n_gain : n_gain + n_bias]
    loss_total = small[n_gain + n_bias]

    enc_new = adamw(enc_w, enc_m, enc_v, enc_grad, MATRIX_RATE, MATRIX_DECAY)
    dec_new = adamw(dec_w, dec_m, dec_v, dec_grad, MATRIX_RATE, MATRIX_DECAY)
    head_new = adamw(head_w, head_m, head_v, head_grad, MATRIX_RATE, MATRIX_DECAY)
    gain_new = adamw(gain_w, gain_m, gain_v, gain_grad, SMALL_RATE, 0.0)
    bias_new = adamw(bias_w, bias_m, bias_v, bias_grad, SMALL_RATE, 0.0)
    return (loss_total,) + enc_new + dec_new + head_new + gain_new + bias_new


def solution(mesh):
    rows = P("fsdp", None)
    in_specs = (P("fsdp", "seq", None), rows) + (rows,) * 6 + (P(),) * 9
    out_specs = (P(),) + (rows,) * 6 + (P(),) * 9
    return jax.shard_map(shards, mesh=mesh, in_specs=in_specs, out_specs=out_specs, check_vma=False)
```

time: 1910 us -> 802 us (0.42)
  waiting for transfers between devices: 1090 us -> 102 us
  Pallas kernels: 0 us -> 283 us
  local copies, waits for them, and re-layouts: 247 us -> 63.6 us
  matrix products: 232 us -> 148 us
  blocking collectives: 85 us -> 12.6 us
  starting transfers between devices: 57.4 us -> 0.33 us
    reduce_scatter x10 -> x3, waiting for transfers between devices: 416 us -> 37.1 us  [the longest x1 33.3 us: shards(): lax.psum_scatter(g_d_qkv, 'fsdp', scatter_dimension=0, tiled=True)]
    pallas_call x0 -> x7, Pallas kernels: none -> 283 us  [the longest x2 120 us: line_sum(): pl.pallas_call(partial(line_sum_kernel, chunks), out_shape=shape, in_spec...]
    psum x2 -> x1, waiting for transfers between devices: 294 us -> 64.9 us  [shards(): lax.psum(jnp.concatenate([dec_early, dec_late], axis=1), 'seq')]
    all_to_all x7 -> x0, waiting for transfers between devices: 190 us -> none  [the longest x2 107 us: layer_forward(): lax.all_to_all(mixed_qkv, 'seq', split_axis=3, concat_axis=1, tiled=True)]
    all_gather x3 -> x4, waiting for transfers between devices: 166 us -> 0.06 us  [the longest x1 0.02 us: shards(): dec_full = lax.all_gather(low(dec_w), 'fsdp', axis=0, tiled=True)]
    dot_general x147 -> x4, matrix products: 106 us -> 4.01 us  [the longest x1 1.28 us: shards(): jnp.einsum('ipr,ipd->ird', pick, dy0_high, preferred_element_type=jnp.flo...]
    scatter-add x1 -> x0, other arithmetic: 67.8 us -> none  [shards(): spread = jnp.zeros(all_shrunk.shape, jnp.float32).at[image_ids, source].a...]
    all_to_all x7 -> x0, starting transfers between devices: 56 us -> none  [the longest x2 25.7 us: layer_forward(): lax.all_to_all(attended, 'seq', split_axis=1, concat_axis=2, tiled=True)]
  transfers between devices with their start and end apart: 23 -> 8, of which waited for: 19 -> 3; matrix products, arithmetic and copies ran while one was open for 12% -> 29% of each run, Pallas kernels for 0% -> 22%
where the time goes in v1:
time: 802 us; the launch traced here: 794 us
  Pallas kernels  283 us (35%)
  other arithmetic  166 us (21%)
  matrix products  148 us (18%)
  waiting for transfers between devices  102 us (13%)
  local copies, waits for them, and re-layouts  63.6 us (8%)
  between operations  17.6 us (2%)
  blocking collectives  12.6 us (2%)
    pallas_call x2, Pallas kernels, line_sum(): pl.pallas_call(partial(line_sum_kernel, chunks), out_shape=shape, in_spec...  120 us
    pallas_call x2, Pallas kernels, attend_backward(): pl.pallas_call(partial(attend_backward_kernel, heads, head_dim), grid=(im...  66.2 us
    psum x1, waiting for transfers between devices, shards(): lax.psum(jnp.concatenate([dec_early, dec_late], axis=1), 'seq')  64.9 us
    pallas_call x1, Pallas kernels, exchange(): pl.pallas_call(partial(exchange_kernel, chunks), out_shape=[jax.ShapeDtyp...  58.9 us
    dot_general x13, matrix products, project(): jnp.einsum('isd,de->ise', row_block, weight, preferred_element_type=jnp.f...  58.4 us
    dot_general x12, matrix products, project_back(): jnp.einsum('ise,de->isd', row_block, weight, preferred_element_type=jnp.f...  50.4 us
    pallas_call x2, Pallas kernels, attend_forward(): pl.pallas_call(partial(attend_forward_kernel, heads, head_dim), grid=(ima...  37.7 us
    dot_general x15, matrix products, weight_grad(): jnp.einsum('isd,ise->de', row_block, upstream, preferred_element_type=jnp...  35.6 us
  transfers between devices with their start and end apart: 8, of which 3 were waited for; matrix products, arithmetic and copies ran while one was open for 29% of the time, Pallas kernels for 22%

profile of v1, /device:TPU:9, one launch (start us, length us, event | category | flops | bytes accessed | tf_op | source)
XLA Modules:
  0.0 793.7 jit_solution(3471094758534812014)
XLA Ops:
  16.6 68.8 %shard_map.288 = bf16[768,768]{1,0:T(8,128)(2,1)S(1)} custom-call(bf16[768,768]{1,0:T(8,128)(2,1)S(1)} %bitcast.236), custom_call_target="tpu_custom_call" | custom-call | bytes 58982400 | tf_op jit(solution)/shard_map/pallas_call | solution.py:414
  105.7 15.2 %shard_map.289 = (bf16[3,272,768]{2,1,0:T(8,128)(2,1)S(1)}, f32[3,6,2,272]{3,2,1,0:T(2,128)S(1)}) custom-call(bf16[3,272,768]{2,1,0:T(8,128)(2,1)S(1)} %get-tuple-element.117.q_ref, bf16[3,272,768]{2,1,0:T(8,128)(2,1)S(1)} %get-tuple-element.116.k_ref, bf16[3,272,768]{2,1,0:T(8,128)(2,1)S(1)} %get-tuple-element.115.v_ref), custom_call_target="tpu_custom_call" | custom-call | flops 2727346176 | bytes 5013504 | tf_op jit(solution)/shard_map/pallas_call | solution.py:272
  122.9 9.3 %multiply_convert_fusion = (bf16[3,272,3072]{2,1,0:T(8,128)(2,1)S(1)}, f32[3,272,3072]{2,1,0:T(8,128)}) fusion(f32[3072]{0:T(1024)S(1)} %slice.299, bf16[768,6656]{1,0:T(8,128)(2,1)} %all-gather.8.cloned.1.call-done, f32[3,272,768]{2,1,0:T(8,128)S(1)} %get-tuple-element.183, f32[768]{0:T(1024)S(1)} %get-tuple-element.156, f32[768]{0:T(1024)S(1)} %get-tuple-element.203, ...), kind=kOutput, calls=%fused_computation.9 | convolution fusion | flops 3868545024 | bytes 22290816 | tf_op jit(solution)/shard_map/isd,de->ise/dot_general | solution.py:83
  139.8 6.6 fusion.7
  151.6 9.8 %multiply_reduce_fusion.2 = f32[3,1040]{0,1:T(8,128)S(1)} fusion(f32[3,1040]{0,1:T(8,128)S(1)} %broadcast_multiply_fusion.5, f32[3,16,512]{2,0,1:T(4,128)S(1)} %broadcast_select_fusion, f32[3,1024,512]{2,0,1:T(4,128)S(1)} %fusion.7), kind=kLoop, calls=%fused_computation.19 | loop fusion | flops 6386640 | bytes 6414720 | tf_op jit(solution)/shard_map/reduce_sum | solution.py:59
  161.6 7.4 add_convert_fusion
  181.4 22.5 %shard_map.290 = (bf16[3,256,512]{2,1,0:T(8,128)(2,1)S(1)}, f32[3,4,4,256]{3,2,1,0:T(4,128)S(1)}) custom-call(bf16[3,256,512]{2,1,0:T(8,128)(2,1)S(1)} %add_convert_fusion.10.q_ref, bf16[3,1040,512]{2,1,0:T(8,128)(2,1)S(1)} %convolution_convert_fusion.k_ref, bf16[3,1040,512]{2,1,0:T(8,128)(2,1)S(1)} %add_convert_fusion.2.v_ref), custom_call_target="tpu_custom_call" | custom-call | flops 6543114240 | bytes 7962624 | tf_op jit(solution)/shard_map/pallas_call | solution.py:272
  213.7 6.2 multiply_convert_fusion.1
  255.0 7.3 convert_reduce_fusion.2
  293.2 42.5 %shard_map.291 = (bf16[3,256,512]{2,1,0:T(8,128)(2,1)S(1)}, bf16[3,1040,512]{2,1,0:T(8,128)(2,1)S(1)}, bf16[3,1040,512]{2,1,0:T(8,128)(2,1)S(1)}) custom-call(bf16[3,256,512]{2,1,0:T(8,128)(2,1)S(1)} %copy-done.22, bf16[3,1040,512]{2,1,0:T(8,128)(2,1)S(1)} %copy-done.24, bf16[3,1040,512]{2,1,0:T(8,128)(2,1)S(1)} %copy-done.27, ...), custom_call_target="tpu_custom_call" | custom-call | flops 16357785600 | bytes 15925248 | tf_op jit(solution)/shard_map/pallas_call | solution.py:297
  347.6 27.7 %multiply_reduce_fusion = (f32[512]{0:T(512)}, f32[3,1040]{0,1:T(8,128)S(1)}, f32[3,1040]{0,1:T(8,128)S(1)}, f32[512]{0:T(512)}, f32[3,1040,512]{2,0,1:T(4,128)S(1)}) fusion(f32[3,1040]{0,1:T(8,128)S(1)} %copy-done.51, f32[3,1040]{0,1:T(8,128)S(1)} %copy-done.40, f32[3,16,512]{2,0,1:T(4,128)S(1)} %broadcast_select_fusion, f32[3,1024,512]{2,0,1:T(4,128)S(1)} %bitcast.241, ...), kind=kLoop, calls=%fused_computation.15 | loop fusion | flops 19162016 | bytes 27187968 | tf_op jit(solution)/shard_map/reduce_sum | solution.py:73
  376.9 11.7 %pad_add_fusion = f32[3,1040,512]{2,0,1:T(4,128)S(1)} fusion(f32[3,256,512]{2,0,1:T(4,128)S(1)} %copy-done.36, f32[3,1040,512]{2,0,1:T(4,128)S(1)} %get-tuple-element.106, f32[3,1040]{0,1:T(8,128)S(1)} %broadcast_multiply_fusion.3, f32[3,1040]{0,1:T(8,128)S(1)} %broadcast_multiply_fusion.4, f32[512]{0:T(512)S(1)} %get-tuple-element.173, ...), kind=kLoop, calls=%fused_computation.16 | loop fusion | flops 14376960 | bytes 20794112 | tf_op jit(solution)/shard_map/add | solution.py:831
  405.1 51.4 %shard_map.292 = bf16[784,512]{1,0:T(8,128)(2,1)S(1)} custom-call(bf16[784,512]{1,0:T(8,128)(2,1)S(1)} %copy-done.1), custom_call_target="tpu_custom_call" | custom-call | bytes 40140800 | tf_op jit(solution)/shard_map/pallas_call | solution.py:414
  469.0 11.4 %convert_reduce_fusion = (f32[3072]{0:T(1024)}, bf16[3,272,3072]{2,1,0:T(8,128)(2,1)S(1)}) fusion(f32[3,272,3072]{2,1,0:T(8,128)} %get-tuple-element.185, f32[3072]{0:T(1024)S(1)} %copy-done.111, bf16[768,6656]{1,0:T(8,128)(2,1)} %all-gather.8.cloned.1.call-done, f32[3,272,768]{2,1,0:T(8,128)S(1)} %get-tuple-element.101), kind=kOutput, calls=%fused_computation.8 | convolution fusion | flops 3883582464 | bytes 22290432 | tf_op jit(solution)/shard_map/isd,de->ise/dot_general | solution.py:83
  480.4 9.6 %multiply_reduce_fusion.5 = (f32[768]{0:T(1024)}, f32[3,272]{1,0:T(4,128)S(1)}, f32[3,272]{1,0:T(4,128)S(1)}, f32[768]{0:T(1024)}, f32[3,272,768]{2,1,0:T(8,128)S(1)}) fusion(f32[3,272,768]{2,1,0:T(8,128)S(1)} %copy-done.43, f32[3,272]{1,0:T(4,128)S(1)} %copy-done.99, f32[3,272]{1,0:T(4,128)S(1)} %copy-done.90, f32[768]{0:T(1024)S(1)} %copy-done.105, ...), kind=kOutput, calls=%fused_computation.74 | convolution fusion | flops 3856008192 | bytes 14767872 | tf_op jit(solution)/shard_map/ise,de->isd/dot_general | solution.py:87
  499.2 33.3 %reduce-scatter.4.cloned.1.call-done = f32[64,1536]{1,0:T(8,128)} async-done(((f32[512,1536]{1,0:T(8,128)}), f32[64,1536]{1,0:T(8,128)}) %reduce-scatter.4.cloned.1.call-update) | async-done | bytes 393232 | tf_op jit(solution)/shard_map/reduce_scatter | solution.py:844
  536.4 23.7 %shard_map.293 = (bf16[3,272,768]{2,1,0:T(8,128)(2,1)S(1)}, bf16[3,272,768]{2,1,0:T(8,128)(2,1)S(1)}, bf16[3,272,768]{2,1,0:T(8,128)(2,1)S(1)}) custom-call(bf16[3,272,768]{2,1,0:T(8,128)(2,1)S(1)} %copy-done.10, bf16[3,272,768]{2,1,0:T(8,128)(2,1)S(1)} %copy-done.8, bf16[3,272,768]{2,1,0:T(8,128)(2,1)S(1)} %copy-done.6, ...), custom_call_target="tpu_custom_call" | custom-call | flops 6818365440 | bytes 10027008 | tf_op jit(solution)/shard_map/pallas_call | solution.py:297
  562.8 5.9 multiply_reduce_fusion.6
  595.5 9.1 %concatenate.64.g_ref = f32[768,2496]{1,0:T(8,128)} concatenate(f32[768,192]{1,0:T(8,128)S(1)} %copy-done.79, f32[768,192]{1,0:T(8,128)} %convolution_bitcast_fusion.13, f32[768,192]{1,0:T(8,128)S(1)} %convolution_bitcast_fusion.12, f32[768,192]{1,0:T(8,128)} %convolution_bitcast_fusion.11, f32[768,192]{1,0:T(8,128)S(1)} %copy-done.78, f32[768,768]{1,0:T(8,128)} %convolution_bitcast_fusion.3, ...), dimensions={1} | concatenate | bytes 15335424 | tf_op jit(solution)/shard_map/concatenate | solution.py:893
  608.4 12.6 %all-gather = f32[384,128]{1,0:T(8,128)S(1)} all-gather(f32[96,128]{1,0:T(8,128)} %reduce-scatter.8.cloned.1.call-done), channel_id=2, replica_groups=mesh['fsdp'=8,'seq'=4] {'seq'}, dimensions={0}, use_global_device_ids=true | all-gather | bytes 245760 | tf_op jit(solution)/shard_map/all_gather | solution.py:895
  621.7 64.9 %all-reduce.6.cloned.1.call-done = f32[64,6912]{1,0:T(8,128)} async-done(((f32[64,6912]{1,0:T(8,128)}), f32[64,6912]{1,0:T(8,128)}) %all-reduce.6.cloned.1.call-update) | async-done | bytes 1769488 | tf_op jit(solution)/shard_map/psum | solution.py:879
  689.8 58.9 %shard_map.294 = (bf16[4,96,2496]{2,1,0:T(8,128)(2,1)S(1)}, f32[8,8,384]{2,1,0:T(8,128)S(1)}) custom-call(f32[768,2496]{1,0:T(8,128)S(1)} %copy-done, f32[8,8,384]{2,1,0:T(8,128)S(1)} %reshape.342.small_ref), custom_call_target="tpu_custom_call" | custom-call | bytes 209715200 | tf_op jit(solution)/shard_map/pallas_call | solution.py:615
  763.8 5.9 concatenate.68
  769.7 11.1 %multiply_subtract_fusion = (f32[96,10496]{1,0:T(8,128)}, f32[96,10496]{1,0:T(8,128)}, f32[96,10496]{1,0:T(8,128)}) fusion(f32[96,10496]{1,0:T(8,128)} %param.19, f32[96,10496]{1,0:T(8,128)} %param.20, f32[96,10496]{1,0:T(8,128)} %concatenate.68, f32[96,10496]{1,0:T(8,128)} %param.21), kind=kLoop, calls=%fused_computation.44 | loop fusion | flops 14106624 | bytes 28213248 | tf_op jit(solution)/shard_map/sub | solution.py:657
  (501 shorter events, 243.1 us)
Async XLA Ops:
  7.2 89.6 %all-gather.6.cloned.1.call-start = ((), (), s32[]{:S(2)}) async-start(), calls=%async_computation.3 | async-start | bytes 6635520 | tf_op jit(solution)/shard_map/all_gather | solution.py:688
  10.5 112.3 %all-gather.8.cloned.1.call-start = ((), (), s32[]{:S(2)}) async-start(), calls=%async_computation.4 | async-start | bytes 11501568 | tf_op jit(solution)/shard_map/all_gather | solution.py:689
  11.7 159.6 %all-gather.10.cloned.1.call-start = ((), (), s32[]{:S(2)}) async-start(), calls=%async_computation.5 | async-start | bytes 7077888 | tf_op jit(solution)/shard_map/all_gather | solution.py:690
  14.3 447.5 %reduce-scatter.6.cloned.1.call-start = ((), (), s32[]{:S(2)}) async-start(), calls=%async_computation.7 | async-start | bytes 12386304 | tf_op jit(solution)/shard_map/reduce_scatter | solution.py:820
  14.4 108.5 %copy-start.110 = (f32[3072]{0:T(1024)}, f32[3072]{0:T(1024)S(1)}, u32[]{:S(2)}) copy-start(f32[3072]{0:T(1024)S(1)} %slice.299) | copy-start | bytes 36868
  15.0 85.4 %copy-start.96 = (f32[768]{0:T(1024)}, f32[768]{0:T(1024)S(1)}, u32[]{:S(2)}) copy-start(f32[768]{0:T(1024)S(1)} %get-tuple-element.202) | copy-start | bytes 9220
  15.0 107.9 %copy-start.104 = (f32[768]{0:T(1024)}, f32[768]{0:T(1024)S(1)}, u32[]{:S(2)}) copy-start(f32[768]{0:T(1024)S(1)} %get-tuple-element.203) | copy-start | bytes 9220
  15.0 107.9 %copy-start.130 = (f32[768]{0:T(1024)}, f32[768]{0:T(1024)S(1)}, u32[]{:S(2)}) copy-start(f32[768]{0:T(1024)S(1)} %get-tuple-element.156) | copy-start | bytes 9220
  15.0 122.0 %copy-start.107 = (f32[768]{0:T(1024)}, f32[768]{0:T(1024)S(1)}, u32[]{:S(2)}) copy-start(f32[768]{0:T(1024)S(1)} %get-tuple-element.204) | copy-start | bytes 9220
  15.0 122.0 %copy-start.132 = (f32[768]{0:T(1024)}, f32[768]{0:T(1024)S(1)}, u32[]{:S(2)}) copy-start(f32[768]{0:T(1024)S(1)} %get-tuple-element.154) | copy-start | bytes 9220
  16.1 123.2 %copy-start.72 = (pred[3,1024]{0,1:T(8,128)(4,1)}, pred[3,1024]{0,1:T(8,128)(4,1)S(1)}, u32[]{:S(2)}) copy-start(pred[3,1024]{0,1:T(8,128)(4,1)S(1)} %copy.214) | copy-start | bytes 9220
  99.6 21.4 %copy-start.31 = (f32[3,256,768]{2,1,0:T(8,128)}, f32[3,256,768]{2,1,0:T(8,128)S(1)}, u32[]{:S(2)}) copy-start(f32[3,256,768]{2,1,0:T(8,128)S(1)} %fusion.34) | copy-start | bytes 7077892
  99.7 21.3 %copy-start.59 = (f32[3,16,768]{2,1,0:T(8,128)}, f32[3,16,768]{2,1,0:T(8,128)S(1)}, u32[]{:S(2)}) copy-start(f32[3,16,768]{2,1,0:T(8,128)S(1)} %broadcast_in_dim.99) | copy-start | bytes 442372
  179.3 24.6 %copy-start.26 = (bf16[3,1040,512]{2,1,0:T(8,128)(2,1)}, bf16[3,1040,512]{2,1,0:T(8,128)(2,1)S(1)}, u32[]{:S(2)}) copy-start(bf16[3,1040,512]{2,1,0:T(8,128)(2,1)S(1)} %add_convert_fusion.2.v_ref) | copy-start | bytes 9584644
  181.4 22.6 %copy-start.21 = (bf16[3,256,512]{2,1,0:T(8,128)(2,1)}, bf16[3,256,512]{2,1,0:T(8,128)(2,1)S(1)}, u32[]{:S(2)}) copy-start(bf16[3,256,512]{2,1,0:T(8,128)(2,1)S(1)} %add_convert_fusion.10.q_ref) | copy-start | bytes 2359300
  203.9 72.7 %copy-start.15 = (bf16[3,256,512]{2,1,0:T(8,128)(2,1)}, bf16[3,256,512]{2,1,0:T(8,128)(2,1)S(1)}, u32[]{:S(2)}) copy-start(bf16[3,256,512]{2,1,0:T(8,128)(2,1)S(1)} %get-tuple-element.40.o_ref) | copy-start | bytes 2359300
  285.8 246.7 %reduce-scatter.4.cloned.1.call-start = ((), (), s32[]{:S(2)}) async-start(), calls=%async_computation.6 | async-start | bytes 3538944 | tf_op jit(solution)/shard_map/reduce_scatter | solution.py:844
  335.7 53.0 %copy-start.4 = (bf16[3,256,512]{2,1,0:T(8,128)(2,1)}, bf16[3,256,512]{2,1,0:T(8,128)(2,1)S(1)}, u32[]{:S(2)}) copy-start(bf16[3,256,512]{2,1,0:T(8,128)(2,1)S(1)} %get-tuple-element.42) | copy-start | bytes 2359300
  461.7 146.7 %reduce-scatter.8.cloned.1.call-start = ((), (), s32[]{:S(2)}) async-start(), calls=%async_computation.9 | async-start | bytes 442368 | tf_op jit(solution)/shard_map/reduce_scatter | solution.py:894
  495.5 37.0 %copy-start.6 = (bf16[3,272,768]{2,1,0:T(8,128)(2,1)S(1)}, bf16[3,272,768]{2,1,0:T(8,128)(2,1)}, u32[]{:S(2)}) copy-start(bf16[3,272,768]{2,1,0:T(8,128)(2,1)} %copy-done.5) | copy-start | bytes 3760132
  495.5 37.0 %copy-start.8 = (bf16[3,272,768]{2,1,0:T(8,128)(2,1)S(1)}, bf16[3,272,768]{2,1,0:T(8,128)(2,1)}, u32[]{:S(2)}) copy-start(bf16[3,272,768]{2,1,0:T(8,128)(2,1)} %copy-done.7) | copy-start | bytes 3760132
  536.4 23.8 %copy-start.70 = (bf16[3,272,768]{2,1,0:T(8,128)(2,1)S(1)}, bf16[3,272,768]{2,1,0:T(8,128)(2,1)}, u32[]{:S(2)}) copy-start(bf16[3,272,768]{2,1,0:T(8,128)(2,1)} %copy-done.69) | copy-start | bytes 3760132
  575.0 111.6 %all-reduce.6.cloned.1.call-start = ((), (), s32[]{:S(2)}) async-start(), calls=%async_computation.8 | async-start | bytes 3538944 | tf_op jit(solution)/shard_map/psum | solution.py:879
  578.1 202.7 %all-gather.12.cloned.1.call-start = ((), (), s32[]{:S(2)}) async-start(), calls=%async_computation.10 | async-start | bytes 1769472 | tf_op jit(solution)/shard_map/all_gather | solution.py:908
  (130 other events, 572.7 us)
Sparse Core Ops, SparseCore 0:
  10.6 45.4 all-gather.5
  58.6 62.2 all-gather.7
  123.3 45.4 all-gather.9
  285.9 95.2 reduce-scatter.5
  461.8 70.6 reduce-scatter.3
  575.1 33.3 reduce-scatter.7
  611.0 75.5 all-reduce.5
  755.3 25.1 all-gather.11

commit v2 on v1

--- a/solution.py
+++ b/solution.py
@@ -317,7 +317,7 @@
 
 
 def line_sum_kernel(
-    chunks, x_ref, o_ref, from_left, from_right, to_left, to_right, send_sem, recv_sem
+    chunks, lines, x_ref, o_ref, from_left, from_right, to_left, to_right, send_sem, recv_sem
 ):
     count = lax.axis_size("seq")
     place = lax.axis_index("seq")
@@ -335,7 +335,7 @@
     pl.semaphore_wait(barrier, peers)
 
     def copy(way, at):
-        span = pl.ds(at * rows, rows)
+        span = pl.ds(pl.multiple_of(at * rows, 16), rows)
         source, target = ((to_right, from_left), (to_left, from_right))[way]
         return pltpu.make_async_remote_copy(
             src_ref=source.at[span],
@@ -368,41 +368,44 @@
             for at in range(chunks - 2, chunks):
                 end_copy(way, at).wait_send()
 
-    for at in range(chunks):
-        span = pl.ds(at * rows, rows)
-
-        @pl.when(has_left)
+    def span_of(at):
+        return pl.ds(pl.multiple_of(at * rows, 16), rows)
+
+    for step in range(chunks + lines - 1):
+        from_first = step - place
+        from_last = step - (count - 1 - place)
+
+        @pl.when(has_left & (from_first >= 0) & (from_first < chunks))
         def _():
-            copy(0, at).wait_recv()
+            copy(0, from_first).wait_recv()
 
             @pl.when(has_right)
             def _():
+                span = span_of(from_first)
                 to_right[span] = x_ref[span] + from_left[span]
-                copy(0, at).start()
-
-        @pl.when(has_right)
+                copy(0, from_first).start()
+
+        @pl.when(has_right & (from_last >= 0) & (from_last < chunks))
         def _():
-            copy(1, at).wait_recv()
+            copy(1, from_last).wait_recv()
 
             @pl.when(has_left)
             def _():
+                span = span_of(from_last)
                 to_left[span] = x_ref[span] + from_right[span]
-                copy(1, at).start()
-
-        @pl.when(has_left & has_right)
-        def _():
-            o_ref[span] = (x_ref[span] + from_left[span]) + from_right[span]
-
-        @pl.when(jnp.logical_not(has_left))
-        def _():
-            o_ref[span] = x_ref[span] + from_right[span]
-
-        @pl.when(jnp.logical_not(has_right))
-        def _():
-            o_ref[span] = x_ref[span] + from_left[span]
+                copy(1, from_last).start()
+
+    @pl.when(jnp.logical_not(has_left))
+    def _():
+        o_ref[...] = x_ref[...] + from_right[...]
+
+    @pl.when(jnp.logical_not(has_right))
+    def _():
+        o_ref[...] = x_ref[...] + from_left[...]
 
     @pl.when(has_left & has_right)
     def _():
+        o_ref[...] = (x_ref[...] + from_left[...]) + from_right[...]
         for at in range(chunks):
             copy(0, at).wait_send()
             copy(1, at).wait_send()
@@ -412,7 +415,7 @@
     shape = jax.ShapeDtypeStruct(block.shape, block.dtype)
     buffer = pltpu.VMEM(block.shape, block.dtype)
     return pl.pallas_call(
-        partial(line_sum_kernel, chunks),
+        partial(line_sum_kernel, chunks, lax.axis_size("seq")),
         out_shape=shape,
         in_specs=[pl.BlockSpec(memory_space=pltpu.VMEM)],
         out_specs=pl.BlockSpec(memory_space=pltpu.VMEM),
@@ -649,6 +652,266 @@
     return hidden * cdf, cdf + hidden * density
 
 
+NT = ((1,), (1,))
+
+
+def norm_rows(rows):
+    centre = rows - jnp.mean(rows, axis=-1, keepdims=True)
+    inverse = lax.rsqrt(jnp.mean(centre * centre, axis=-1, keepdims=True) + NORM_EPS)
+    return centre * inverse, inverse
+
+
+def norm_rows_back(upstream, scaled, inverse, gain):
+    weighted = upstream * gain
+    inner = (
+        weighted
+        - jnp.mean(weighted, axis=-1, keepdims=True)
+        - scaled * jnp.mean(weighted * scaled, axis=-1, keepdims=True)
+    )
+    return inverse * inner, column_sum(upstream * scaled), column_sum(upstream)
+
+
+def column_sum(rows):
+    return jnp.sum(rows, axis=0, keepdims=True)
+
+
+def clear_first(refs):
+    @pl.when(pl.program_id(0) == 0)
+    def _():
+        for ref in refs:
+            ref[...] = jnp.zeros_like(ref)
+
+
+def dec_middle_kernel(
+    grad_scale,
+    o_ref,
+    y_ref,
+    pixel_ref,
+    masked_ref,
+    out_w,
+    up_w,
+    down_w,
+    head_w,
+    vec_ref,
+    bu_ref,
+    bh_ref,
+    do_ref,
+    dmid_ref,
+    grad_ref,
+    vec_grad,
+    bu_grad,
+    bh_grad,
+    slope_ref,
+    act_ref,
+):
+    clear_first((grad_ref, vec_grad, bu_grad, bh_grad))
+    bo, gain2, shift2, bd, gain3, shift3 = (vec_ref[i : i + 1, :] for i in range(6))
+    attended = o_ref[0]
+    middle = y_ref[0] + dot_f32(attended, out_w[...], NN) + bo
+    scaled2, inverse2 = norm_rows(middle)
+    second = low(scaled2 * gain2 + shift2)
+    size = 512
+    decoded = middle + bd
+    for at in range(0, FF_D, size):
+        span = slice(at, at + size)
+        value, slope = gelu_parts(dot_f32(second, up_w[:, span], NN) + bu_ref[:, span])
+        slope_ref[:, span] = slope
+        act_ref[:, span] = low(value)
+        decoded = decoded + dot_f32(act_ref[:, span], down_w[:, span], NT)
+    scaled3, inverse3 = norm_rows(decoded)
+    third = low(scaled3 * gain3 + shift3)
+    predicted = dot_f32(third, head_w[...], NN) + bh_ref[...]
+    pixel = pixel_ref[0].astype(jnp.float32)
+    centre = pixel - jnp.mean(pixel, axis=-1, keepdims=True)
+    target = centre * lax.rsqrt(
+        jnp.sum(centre * centre, axis=-1, keepdims=True) / (PIX - 1) + PIXEL_EPS
+    )
+    masked = masked_ref[0][:, :1]
+    error = (predicted - target) * masked
+    pred_grad = error * grad_scale
+    pred_low = low(pred_grad)
+    bh_grad[0:1, :] += column_sum(pred_grad)
+    bh_grad[1:2, :] += column_sum(error * error)
+    o_span, u_span = D_D, D_D + FF_D
+    h_span = D_D + 2 * FF_D
+    grad_ref[:, h_span:] += dot_f32(third, pred_low, TN)
+    up3, g_gain3, g_shift3 = norm_rows_back(
+        dot_f32(pred_low, head_w[...], NT), scaled3, inverse3, gain3
+    )
+    up3_low = low(up3)
+    back = jnp.zeros_like(up3)
+    for at in range(0, FF_D, size):
+        span = slice(at, at + size)
+        hidden_grad = low(dot_f32(up3_low, down_w[:, span], NN) * slope_ref[:, span])
+        grad_ref[:, u_span + at : u_span + at + size] += dot_f32(up3_low, act_ref[:, span], TN)
+        grad_ref[:, o_span + at : o_span + at + size] += dot_f32(second, hidden_grad, TN)
+        bu_grad[0:1, span] += column_sum(hidden_grad.astype(jnp.float32))
+        back = back + dot_f32(hidden_grad, up_w[:, span], NT)
+    through, g_gain2, g_shift2 = norm_rows_back(back, scaled2, inverse2, gain2)
+    middle_grad = up3 + through
+    middle_low = low(middle_grad)
+    dmid_ref[0] = middle_grad
+    grad_ref[:, :o_span] += dot_f32(attended, middle_low, TN)
+    do_ref[0] = low(dot_f32(middle_low, out_w[...], NT))
+    sums = (column_sum(middle_grad), g_gain2, g_shift2, column_sum(up3), g_gain3, g_shift3)
+    for at, part in enumerate(sums):
+        vec_grad[at : at + 1, :] += part
+
+
+def whole(shape):
+    return pl.BlockSpec(shape, lambda i: (0,) * len(shape), pipeline_mode=pl.Buffered(1))
+
+
+def columns(rows, width, at):
+    return pl.BlockSpec((rows, width), lambda i: (0, at), pipeline_mode=pl.Buffered(1))
+
+
+def per_image(rows, width):
+    return pl.BlockSpec((1, rows, width), lambda i: (i, 0, 0))
+
+
+def dec_middle(attended, y_own, pixels, masked, dec_full, head_low, vectors, bu, bh, grad_scale):
+    images, rows, _ = attended.shape
+    f32 = jnp.float32
+    return pl.pallas_call(
+        partial(dec_middle_kernel, grad_scale),
+        grid=(images,),
+        in_specs=[
+            per_image(rows, D_D),
+            per_image(rows, D_D),
+            per_image(rows, PIX),
+            per_image(rows, 128),
+            columns(D_D, D_D, 3),
+            columns(D_D, FF_D, 1),
+            columns(D_D, FF_D, 2),
+            whole((D_D, PIX)),
+            whole((8, D_D)),
+            whole((1, FF_D)),
+            whole((1, PIX)),
+        ],
+        out_specs=[
+            per_image(rows, D_D),
+            per_image(rows, D_D),
+            whole((D_D, D_D + 2 * FF_D + PIX)),
+            whole((8, D_D)),
+            whole((8, FF_D)),
+            whole((8, PIX)),
+        ],
+        out_shape=[
+            jax.ShapeDtypeStruct((images, rows, D_D), jnp.bfloat16),
+            jax.ShapeDtypeStruct((images, rows, D_D), f32),
+            jax.ShapeDtypeStruct((D_D, D_D + 2 * FF_D + PIX), f32),
+            jax.ShapeDtypeStruct((8, D_D), f32),
+            jax.ShapeDtypeStruct((8, FF_D), f32),
+            jax.ShapeDtypeStruct((8, PIX), f32),
+        ],
+        scratch_shapes=[pltpu.VMEM((rows, FF_D), f32), pltpu.VMEM((rows, FF_D), jnp.bfloat16)],
+        compiler_params=pltpu.CompilerParams(vmem_limit_bytes=44 * 1024 * 1024),
+        cost_estimate=pl.CostEstimate(
+            flops=12 * images * rows * D_D * (D_D + 2 * FF_D + PIX),
+            bytes_accessed=30 * 1024 * 1024,
+            transcendentals=2 * images * rows * FF_D,
+        ),
+    )(
+        attended, y_own, pixels, masked, dec_full, dec_full, dec_full, head_low, vectors, bu, bh
+    )
+
+
+def dec_entry_back_kernel(
+    y_ref,
+    dq_ref,
+    dk_ref,
+    dv_ref,
+    dmid_ref,
+    rank_ref,
+    q_w,
+    k_w,
+    v_w,
+    vec_ref,
+    de_ref,
+    grad_ref,
+    vec_grad,
+    cls_ref,
+):
+    image = pl.program_id(0)
+    clear_first((grad_ref, vec_grad, cls_ref))
+    gain, shift = vec_ref[0:1, :], vec_ref[1:2, :]
+    scaled, inverse = norm_rows(y_ref[0])
+    normed = low(scaled * gain + shift)
+    dq, dk, dv = dq_ref[0], dk_ref[0], dv_ref[0]
+    own = dq.shape[0]
+    grad_ref[:, :D_D] += dot_f32(normed[:own], dq, TN)
+    grad_ref[:, D_D : 2 * D_D] += dot_f32(normed, dk, TN)
+    grad_ref[:, 2 * D_D :] += dot_f32(normed, dv, TN)
+    up = dot_f32(dk, k_w[...], NT) + dot_f32(dv, v_w[...], NT)
+    up = jnp.concatenate([up[:own] + dot_f32(dq, q_w[...], NT), up[own:]], axis=0)
+    back, g_gain, g_shift = norm_rows_back(up, scaled, inverse, gain)
+    back = jnp.concatenate([back[:own] + dmid_ref[0], back[own:]], axis=0)
+    patches = back[:PATCHES]
+    high = low(patches)
+    rest = low(patches - high.astype(jnp.float32))
+    ranks = rank_ref[0]
+    at = lax.broadcasted_iota(jnp.int32, (KEEP, PATCHES), 0)
+    pick = low(jnp.where(at == ranks, 1.0, 0.0))
+    hidden = low(jnp.where(jnp.broadcast_to(ranks, (16, PATCHES)) >= KEEP, 1.0, 0.0))
+    de_ref[pl.ds(pl.multiple_of(image * KEEP, KEEP), KEEP)] = low(dot_f32(pick, high, NN))
+    g_mask = dot_f32(hidden, high, NN) + dot_f32(hidden, rest, NN)
+    cls_ref[pl.ds(image, 1), :] = back[PATCHES : PATCHES + 1]
+    sums = (
+        g_mask[0:1],
+        g_shift,
+        column_sum(dq.astype(jnp.float32)),
+        column_sum(dv.astype(jnp.float32)),
+        g_gain,
+    )
+    for at, part in enumerate(sums):
+        vec_grad[at : at + 1, :] += part
+
+    @pl.when(image == pl.num_programs(0) - 1)
+    def _():
+        de_ref[de_ref.shape[0] - TAIL :] = low(cls_ref[...])
+
+
+def dec_entry_back(y0, dq, dk, dv, dmid, ranks, dec_full, vectors):
+    images, rows, _ = y0.shape
+    own = dq.shape[1]
+    f32 = jnp.float32
+    return pl.pallas_call(
+        dec_entry_back_kernel,
+        grid=(images,),
+        in_specs=[
+            per_image(rows, D_D),
+            per_image(own, D_D),
+            per_image(rows, D_D),
+            per_image(rows, D_D),
+            per_image(own, D_D),
+            per_image(1, PATCHES),
+            columns(D_D, D_D, 0),
+            columns(D_D, D_D, 1),
+            columns(D_D, D_D, 2),
+            whole((8, D_D)),
+        ],
+        out_specs=[whole((images * KEEP + TAIL, D_D)), whole((D_D, 3 * D_D)), whole((8, D_D))],
+        out_shape=[
+            jax.ShapeDtypeStruct((images * KEEP + TAIL, D_D), jnp.bfloat16),
+            jax.ShapeDtypeStruct((D_D, 3 * D_D), f32),
+            jax.ShapeDtypeStruct((8, D_D), f32),
+        ],
+        scratch_shapes=[pltpu.VMEM((TAIL, D_D), f32)],
+        compiler_params=pltpu.CompilerParams(vmem_limit_bytes=44 * 1024 * 1024),
+        cost_estimate=pl.CostEstimate(
+            flops=12 * images * rows * D_D * D_D * 2,
+            bytes_accessed=24 * 1024 * 1024,
+            transcendentals=0,
+        ),
+    )(y0, dq, dk, dv, dmid, ranks, dec_full, dec_full, dec_full, vectors)
+
+
+def stack_rows(parts):
+    rows = jnp.stack(parts)
+    return jnp.pad(rows, ((0, 8 - len(parts)), (0, 0)))
+
+
 def adamw(weight, moment_one, moment_two, gradient, step_rate, decay_rate):
     moment_one = BETA_ONE * moment_one + (1 - BETA_ONE) * gradient
     moment_two = BETA_TWO * moment_two + (1 - BETA_TWO) * gradient * gradient
@@ -698,9 +961,6 @@
     d_query = dec_full[:, :D_D]
     d_key = dec_full[:, D_D : 2 * D_D]
     d_value = dec_full[:, 2 * D_D : 3 * D_D]
-    d_out = dec_full[:, 3 * D_D : 4 * D_D]
-    d_up = dec_full[:, 4 * D_D : 4 * D_D + FF_D]
-    d_down = dec_full[:, 4 * D_D + FF_D :]
 
     pieces = split_vector(bias_w, bias_widths())
     gains = split_vector(gain_w, [D_E, D_E, D_E, D_D, D_D, D_D])
@@ -771,76 +1031,30 @@
     d_k = low(project(d_n1, d_key))
     d_v = low(project(d_n1, d_value) + d_bv)
     d_o, d_lse = attend_forward(d_q, d_k, d_v, H_D)
-    d_mid = y0_own + project(d_o, d_out) + d_bo
-    d_n2, d_sc2, d_inv2 = norm_forward(d_mid, gains[4], d_shift2)
-    d_n2 = low(d_n2)
-    d_hidden = project(d_n2, d_up) + d_bu
-    d_gelu, d_slope = gelu_parts(d_hidden)
-    d_act = low(d_gelu)
-    decoded = d_mid + project_back(d_act, d_down) + d_bd
-    d_n3, d_sc3, d_inv3 = norm_forward(decoded, gains[5], d_shift3)
-    d_n3 = low(d_n3)
-    predicted = project(d_n3, head_low) + b_head
-    targets = pixels.astype(jnp.float32)
-    centre = targets - jnp.mean(targets, axis=-1, keepdims=True)
-    targets = centre * lax.rsqrt(
-        jnp.sum(centre * centre, axis=-1, keepdims=True) / (PIX - 1) + PIXEL_EPS
-    )
-    errors = predicted - targets
-    own_masked = (own_restore >= KEEP)[..., None]
-    loss_part = (
-        jnp.sum(jnp.where(own_masked, jnp.mean(errors * errors, axis=-1, keepdims=True), 0.0))
-        / masked_total
-    )
-
-    pred_grad = jnp.where(own_masked, errors * (2.0 / (PIX * masked_total)), 0.0)
-    pred_low = low(pred_grad)
-    g_head = weight_grad(d_n3, pred_low)
-    g_b_head = row_sum(pred_grad)
-    d_up3, g_d_gain3, g_d_shift3 = norm_backward(
-        project_back(pred_low, head_low), d_sc3, d_inv3, gains[5]
-    )
-    d_up3_low = low(d_up3)
-    g_d_down = weight_grad(d_up3_low, d_act)
-    g_d_bd = row_sum(d_up3)
-    d_dhidden = low(project(d_up3_low, d_down) * d_slope)
-    g_d_up = weight_grad(d_n2, d_dhidden)
-    g_d_bu = row_sum(d_dhidden)
-    through, g_d_gain2, g_d_shift2 = norm_backward(
-        project_back(d_dhidden, d_up), d_sc2, d_inv2, gains[4]
-    )
-    d_dmid = d_up3 + through
-    d_dmid_low = low(d_dmid)
-    g_d_out = weight_grad(d_o, d_dmid_low)
-    g_d_bo = row_sum(d_dmid)
-    d_do = low(project_back(d_dmid_low, d_out))
-    late_grads, d_do = lax.optimization_barrier(
-        (jnp.concatenate([g_d_out, g_d_up, g_d_down, g_head], axis=1), d_do)
-    )
+    own_masked = (own_restore >= KEEP).astype(jnp.float32)
+    own_masked = jnp.broadcast_to(own_masked[..., None], own_masked.shape + (128,))
+    d_do, d_dmid, late_grads, mid_sums, bu_sums, bh_sums = dec_middle(
+        d_o,
+        y0_own,
+        pixels,
+        own_masked,
+        dec_full,
+        head_low,
+        stack_rows([d_bo, gains[4], d_shift2, d_bd, gains[5], d_shift3]),
+        d_bu[None],
+        b_head[None],
+        2.0 / (PIX * masked_total),
+    )
+    g_d_bo, g_d_gain2, g_d_shift2, g_d_bd, g_d_gain3, g_d_shift3 = (mid_sums[i] for i in range(6))
+    g_d_bu = bu_sums[0]
+    g_b_head = bh_sums[0]
+    loss_part = jnp.sum(bh_sums[1]) / (PIX * masked_total)
     dec_late = lax.psum_scatter(late_grads, "fsdp", scatter_dimension=0, tiled=True)
     d_dq, d_dk, d_dv = attend_backward(d_q, d_k, d_v, d_lse, d_do, d_o, H_D)
-    g_d_qkv = jnp.concatenate(
-        [weight_grad(n1_own, d_dq), weight_grad(d_n1, d_dk), weight_grad(d_n1, d_dv)], axis=1
-    )
-    g_d_bq = row_sum(d_dq)
-    g_d_bv = row_sum(d_dv)
-    dn1 = project_back(d_dk, d_key) + project_back(d_dv, d_value)
-    others = ((0, 0), (0, D_ROWS - own_count), (0, 0))
-    dn1 = dn1 + jnp.pad(project_back(d_dq, d_query), others)
-    dy0, g_d_gain1, g_d_shift1 = norm_backward(dn1, d_sc1, d_inv1, gains[3])
-    dy0 = dy0 + jnp.pad(d_dmid, others)
-    dy0_patch = dy0[:, :PATCHES]
-    g_mask = jnp.sum(jnp.where(is_masked[..., None], dy0_patch, 0.0), axis=(0, 1))
-    dy0_high = low(dy0_patch)
-    dy0_rest = low(dy0_patch - dy0_high.astype(jnp.float32))
-    de_patch = jnp.einsum(
-        "ipr,ipd->ird", pick, dy0_high, preferred_element_type=jnp.float32
-    ) + jnp.einsum("ipr,ipd->ird", pick, dy0_rest, preferred_element_type=jnp.float32)
-    de_part = jnp.concatenate(
-        [de_patch.reshape(images * KEEP, D_D), dy0[:, PATCHES], jnp.zeros((TAIL - images, D_D))],
-        axis=0,
-    )
-    g_d_qkv, de_part = lax.optimization_barrier((g_d_qkv, low(de_part)))
+    de_part, g_d_qkv, entry_sums = dec_entry_back(
+        y0, d_dq, d_dk, d_dv, d_dmid, turned[:, None, :], dec_full, stack_rows([gains[3], d_shift1])
+    )
+    g_mask, g_d_shift1, g_d_bq, g_d_bv, g_d_gain1 = (entry_sums[i] for i in range(5))
     dec_early = lax.psum_scatter(g_d_qkv, "fsdp", scatter_dimension=0, tiled=True)
     de_sum = line_sum(de_part, 7, 1)
     dec_late, de_sum = lax.optimization_barrier((dec_late, de_sum))

time: 802 us -> 670 us (0.84)
  other arithmetic: 166 us -> 70.5 us
  matrix products: 148 us -> 88.5 us
  waiting for transfers between devices: 102 us -> 130 us
  Pallas kernels: 283 us -> 272 us
  local copies, waits for them, and re-layouts: 63.6 us -> 72.8 us
    reduce_sum x6 -> x1, other arithmetic: 36.8 us -> 1.42 us  [shards(): loss_part = jnp.sum(bh_sums[1]) / (PIX * masked_total)]
    dot_general x12 -> x5, matrix products: 50.4 us -> 26.5 us  [project_back(): jnp.einsum('ise,de->isd', row_block, weight, preferred_element_type=jnp.f...]
    all_gather x1, waiting for transfers between devices: 0.02 us -> 21.7 us  [shards(): dec_full = lax.all_gather(low(dec_w), 'fsdp', axis=0, tiled=True)]
    all_gather x1, waiting for transfers between devices: 0.02 us -> 20.8 us  [shards(): lax.all_gather(enc_low[:, 5 * D_E:], 'fsdp', axis=0, tiled=True)]
    dot_general x13 -> x9, matrix products: 58.4 us -> 39 us  [project(): jnp.einsum('isd,de->ise', row_block, weight, preferred_element_type=jnp.f...]
    add x2 -> x0, other arithmetic: 18.3 us -> none  [the longest x1 11.7 us: shards(): dy0 = dy0 + jnp.pad(d_dmid, others)]
    reduce_scatter x1, waiting for transfers between devices: 33.3 us -> 15.1 us  [shards(): lax.psum_scatter(g_d_qkv, 'fsdp', scatter_dimension=0, tiled=True)]
    dot_general x15 -> x8, matrix products: 35.6 us -> 20.8 us  [weight_grad(): jnp.einsum('isd,ise->de', row_block, upstream, preferred_element_type=jnp...]
  transfers between devices with their start and end apart: 8 -> 8, of which waited for: 3 -> 6; matrix products, arithmetic and copies ran while one was open for 29% -> 22% of each run, Pallas kernels for 22% -> 21%
where the time goes in v2:
time: 670 us; the launch traced here: 664 us
  Pallas kernels  272 us (41%)
  waiting for transfers between devices  130 us (19%)
  matrix products  88.5 us (13%)
  local copies, waits for them, and re-layouts  72.8 us (11%)
  other arithmetic  70.5 us (11%)
  between operations  17 us (3%)
  blocking collectives  12.5 us (2%)
    pallas_call x2, Pallas kernels, attend_backward(): pl.pallas_call(partial(attend_backward_kernel, heads, head_dim), grid=(im...  66.4 us
    psum x1, waiting for transfers between devices, shards(): lax.psum(jnp.concatenate([dec_early, dec_late], axis=1), 'seq')  65.9 us
    pallas_call x2, Pallas kernels, line_sum(): pl.pallas_call(partial(line_sum_kernel, chunks, lax.axis_size('seq')), ou...  64.9 us
    pallas_call x1, Pallas kernels, exchange(): pl.pallas_call(partial(exchange_kernel, chunks), out_shape=[jax.ShapeDtyp...  58.9 us
    unnamed x281, local copies, waits for them, and re-layouts  43.9 us
    dot_general x9, matrix products, project(): jnp.einsum('isd,de->ise', row_block, weight, preferred_element_type=jnp.f...  39 us
    pallas_call x2, Pallas kernels, attend_forward(): pl.pallas_call(partial(attend_forward_kernel, heads, head_dim), grid=(ima...  37.9 us
    dot_general x5, matrix products, project_back(): jnp.einsum('ise,de->isd', row_block, weight, preferred_element_type=jnp.f...  26.5 us
  transfers between devices with their start and end apart: 8, of which 6 were waited for; matrix products, arithmetic and copies ran while one was open for 22% of the time, Pallas kernels for 21%

profile of v2, /device:TPU:9, one launch (start us, length us, event | category | flops | bytes accessed | tf_op | source)
XLA Modules:
  0.0 663.5 jit_solution(1253176537131139979)
XLA Ops:
  17.8 37.3 %shard_map.288 = bf16[768,768]{1,0:T(8,128)(2,1)S(1)} custom-call(bf16[768,768]{1,0:T(8,128)(2,1)S(1)} %bitcast.194), custom_call_target="tpu_custom_call" | custom-call | bytes 58982400 | tf_op jit(solution)/shard_map/pallas_call | solution.py:417
  66.4 5.8 multiply_sine_fusion
  81.5 15.2 %shard_map.289 = (bf16[3,272,768]{2,1,0:T(8,128)(2,1)S(1)}, f32[3,6,2,272]{3,2,1,0:T(2,128)S(1)}) custom-call(bf16[3,272,768]{2,1,0:T(8,128)(2,1)S(1)} %get-tuple-element.107.q_ref, bf16[3,272,768]{2,1,0:T(8,128)(2,1)S(1)} %get-tuple-element.106.k_ref, bf16[3,272,768]{2,1,0:T(8,128)(2,1)S(1)} %get-tuple-element.105.v_ref), custom_call_target="tpu_custom_call" | custom-call | flops 2727346176 | bytes 5013504 | tf_op jit(solution)/shard_map/pallas_call | solution.py:272
  100.0 20.8 %all-gather.8.cloned.1.call-done = bf16[768,6656]{1,0:T(8,128)(2,1)} async-done(((bf16[96,6656]{1,0:T(8,128)(2,1)}), bf16[768,6656]{1,0:T(8,128)(2,1)}) %all-gather.8.cloned.1.call-update) | async-done | bytes 10223632 | tf_op jit(solution)/shard_map/all_gather | solution.py:952
  120.8 9.7 %multiply_convert_fusion = (bf16[3,272,3072]{2,1,0:T(8,128)(2,1)S(1)}, f32[3,272,3072]{2,1,0:T(8,128)}) fusion(f32[3072]{0:T(1024)S(1)} %slice.325, bf16[768,6656]{1,0:T(8,128)(2,1)} %all-gather.8.cloned.1.call-done, f32[3,272,768]{2,1,0:T(8,128)} %copy-done.44, f32[768]{0:T(1024)S(1)} %get-tuple-element.146, f32[768]{0:T(1024)S(1)} %get-tuple-element.195, ...), kind=kOutput, calls=%fused_computation.8 | convolution fusion | flops 3868545024 | bytes 22290816 | tf_op jit(solution)/shard_map/isd,de->ise/dot_general | solution.py:83
  147.1 21.7 %all-gather.10.cloned.1.call-done.out_w.up_w.down_w.q_w.k_w.v_w = bf16[512,6144]{1,0:T(8,128)(2,1)} async-done(((bf16[64,6144]{1,0:T(8,128)(2,1)}), bf16[512,6144]{1,0:T(8,128)(2,1)}) %all-gather.10.cloned.1.call-update) | async-done | bytes 6291472 | tf_op jit(solution)/shard_map/all_gather | solution.py:953
  178.2 22.7 %shard_map.290 = (bf16[3,256,512]{2,1,0:T(8,128)(2,1)S(1)}, f32[3,4,4,256]{3,2,1,0:T(4,128)S(1)}) custom-call(bf16[3,256,512]{2,1,0:T(8,128)(2,1)S(1)} %add_convert_fusion.7.q_ref, bf16[3,1040,512]{2,1,0:T(8,128)(2,1)S(1)} %convolution_convert_fusion.k_ref, bf16[3,1040,512]{2,1,0:T(8,128)(2,1)S(1)} %add_convert_fusion.1.v_ref), custom_call_target="tpu_custom_call" | custom-call | flops 6543114240 | bytes 7962624 | tf_op jit(solution)/shard_map/pallas_call | solution.py:272
  201.8 26.1 %shard_map.291 = (bf16[3,256,512]{2,1,0:T(8,128)(2,1)S(1)}, f32[3,256,512]{2,1,0:T(8,128)S(1)}, f32[512,5376]{1,0:T(8,128)}, f32[8,512]{1,0:T(8,128)S(1)}, f32[8,2048]{1,0:T(8,128)S(1)}, /*index=5*/f32[8,768]{1,0:T(8,128)S(1)}) custom-call(bf16[3,256,512]{2,1,0:T(8,128)(2,1)S(1)} %get-tuple-element.45.o_ref, f32[3,256,512]{2,1,0:T(8,128)S(1)} %slice.428.y_ref, ...), custom_call_target="tpu_custom_call" | custom-call | flops 25367150592 | bytes 31457280 | tf_op jit(solution)/shard_map/pallas_call | solution.py:776
  237.2 42.7 %shard_map.292 = (bf16[3,256,512]{2,1,0:T(8,128)(2,1)S(1)}, bf16[3,1040,512]{2,1,0:T(8,128)(2,1)S(1)}, bf16[3,1040,512]{2,1,0:T(8,128)(2,1)S(1)}) custom-call(bf16[3,256,512]{2,1,0:T(8,128)(2,1)S(1)} %copy-done.22, bf16[3,1040,512]{2,1,0:T(8,128)(2,1)S(1)} %copy-done.24, bf16[3,1040,512]{2,1,0:T(8,128)(2,1)S(1)} %copy-done.27, ...), custom_call_target="tpu_custom_call" | custom-call | flops 16357785600 | bytes 15925248 | tf_op jit(solution)/shard_map/pallas_call | solution.py:297
  281.6 17.5 %shard_map.293 = (bf16[784,512]{1,0:T(8,128)(2,1)S(1)}, f32[512,1536]{1,0:T(8,128)S(1)}, f32[8,512]{1,0:T(8,128)S(1)}) custom-call(f32[3,1040,512]{2,1,0:T(8,128)} %get-tuple-element.103.y_ref, bf16[3,256,512]{2,1,0:T(8,128)(2,1)S(1)} %get-tuple-element.47.dq_ref, bf16[3,1040,512]{2,1,0:T(8,128)(2,1)S(1)} %get-tuple-element.48.dk_ref, ...), custom_call_target="tpu_custom_call" | custom-call | flops 19629342720 | bytes 25165824 | tf_op jit(solution)/shard_map/pallas_call | solution.py:879
  300.8 27.7 %shard_map.294 = bf16[784,512]{1,0:T(8,128)(2,1)S(1)} custom-call(bf16[784,512]{1,0:T(8,128)(2,1)S(1)} %get-tuple-element.53.x_ref), custom_call_target="tpu_custom_call" | custom-call | bytes 40140800 | tf_op jit(solution)/shard_map/pallas_call | solution.py:417
  338.1 11.3 %convert_reduce_fusion = (f32[3072]{0:T(1024)S(1)}, bf16[3,272,3072]{2,1,0:T(8,128)(2,1)S(1)}) fusion(f32[3,272,3072]{2,1,0:T(8,128)} %get-tuple-element.186, f32[3072]{0:T(1024)S(1)} %copy-done.102, bf16[768,6656]{1,0:T(8,128)(2,1)} %all-gather.8.cloned.1.call-done, f32[3,272,768]{2,1,0:T(8,128)S(1)} %get-tuple-element.97), kind=kOutput, calls=%fused_computation.7 | convolution fusion | flops 3883582464 | bytes 22290432 | tf_op jit(solution)/shard_map/isd,de->ise/dot_general | solution.py:83
  349.4 9.6 %multiply_reduce_fusion.2 = (f32[768]{0:T(1024)}, f32[3,272]{1,0:T(4,128)S(1)}, f32[3,272]{1,0:T(4,128)S(1)}, f32[768]{0:T(1024)}, f32[3,272,768]{2,1,0:T(8,128)S(1)}) fusion(f32[3,272,768]{2,1,0:T(8,128)S(1)} %copy-done.46, f32[3,272]{1,0:T(4,128)S(1)} %copy-done.87, f32[3,272]{1,0:T(4,128)S(1)} %copy-done.79, f32[768]{0:T(1024)S(1)} %copy-done.95, ...), kind=kOutput, calls=%fused_computation.40 | convolution fusion | flops 3856008192 | bytes 14767872 | tf_op jit(solution)/shard_map/ise,de->isd/dot_general | solution.py:87
  366.3 15.1 %reduce-scatter.4.cloned.1.call-done = f32[64,1536]{1,0:T(8,128)} async-done(((f32[512,1536]{1,0:T(8,128)}), f32[64,1536]{1,0:T(8,128)}) %reduce-scatter.4.cloned.1.call-update) | async-done | bytes 393232 | tf_op jit(solution)/shard_map/reduce_scatter | solution.py:1058
  385.2 23.7 %shard_map.295 = (bf16[3,272,768]{2,1,0:T(8,128)(2,1)S(1)}, bf16[3,272,768]{2,1,0:T(8,128)(2,1)S(1)}, bf16[3,272,768]{2,1,0:T(8,128)(2,1)S(1)}) custom-call(bf16[3,272,768]{2,1,0:T(8,128)(2,1)S(1)} %copy-done.7, bf16[3,272,768]{2,1,0:T(8,128)(2,1)S(1)} %copy-done.5, bf16[3,272,768]{2,1,0:T(8,128)(2,1)S(1)} %copy-done.3, f32[3,6,2,272]{3,2,1,0:T(2,128)S(1)} %copy-done.32, ...), custom_call_target="tpu_custom_call" | custom-call | flops 6818365440 | bytes 10027008 | tf_op jit(solution)/shard_map/pallas_call | solution.py:297
  411.5 5.9 multiply_reduce_fusion.3
  463.5 9.3 %concatenate.51.g_ref = f32[768,2496]{1,0:T(8,128)} concatenate(f32[768,192]{1,0:T(8,128)} %convolution_bitcast_fusion.2, f32[768,192]{1,0:T(8,128)S(1)} %convolution_bitcast_fusion.6, f32[768,192]{1,0:T(8,128)} %convolution_bitcast_fusion.5, f32[768,192]{1,0:T(8,128)} %convolution_bitcast_fusion.4, f32[768,192]{1,0:T(8,128)} %convolution_bitcast_fusion.3, ...), dimensions={1} | concatenate | bytes 15335424 | tf_op jit(solution)/shard_map/concatenate | solution.py:1107
  477.9 12.5 %all-gather = f32[384,128]{1,0:T(8,128)S(1)} all-gather(f32[96,128]{1,0:T(8,128)} %reduce-scatter.8.cloned.1.call-done), channel_id=2, replica_groups=mesh['fsdp'=8,'seq'=4] {'seq'}, dimensions={0}, use_global_device_ids=true | all-gather | bytes 245760 | tf_op jit(solution)/shard_map/all_gather | solution.py:1109
  491.1 65.9 %all-reduce.6.cloned.1.call-done = f32[64,6912]{1,0:T(8,128)} async-done(((f32[64,6912]{1,0:T(8,128)}), f32[64,6912]{1,0:T(8,128)}) %all-reduce.6.cloned.1.call-update) | async-done | bytes 1769488 | tf_op jit(solution)/shard_map/psum | solution.py:1093
  560.2 58.9 %shard_map.296 = (bf16[4,96,2496]{2,1,0:T(8,128)(2,1)S(1)}, f32[8,8,384]{2,1,0:T(8,128)S(1)}) custom-call(f32[768,2496]{1,0:T(8,128)S(1)} %copy-done, f32[8,8,384]{2,1,0:T(8,128)S(1)} %reshape.266.small_ref), custom_call_target="tpu_custom_call" | custom-call | bytes 209715200 | tf_op jit(solution)/shard_map/pallas_call | solution.py:618
  625.6 5.6 multiply_subtract_fusion.2
  632.7 6.0 concatenate.55
  638.7 10.9 %multiply_subtract_fusion = (f32[96,10496]{1,0:T(8,128)}, f32[96,10496]{1,0:T(8,128)}, f32[96,10496]{1,0:T(8,128)}) fusion(f32[96,10496]{1,0:T(8,128)} %param.19, f32[96,10496]{1,0:T(8,128)} %param.20, f32[96,10496]{1,0:T(8,128)} %concatenate.55, f32[96,10496]{1,0:T(8,128)} %param.21), kind=kLoop, calls=%fused_computation.21 | loop fusion | flops 14106624 | bytes 28213248 | tf_op jit(solution)/shard_map/sub | solution.py:920
  650.8 5.5 multiply_subtract_fusion.1
  (413 shorter events, 159.2 us)
Async XLA Ops:
  7.2 65.1 %all-gather.6.cloned.1.call-start = ((), (), s32[]{:S(2)}) async-start(), calls=%async_computation.3 | async-start | bytes 6635520 | tf_op jit(solution)/shard_map/all_gather | solution.py:951
  10.5 110.3 %all-gather.8.cloned.1.call-start = ((), (), s32[]{:S(2)}) async-start(), calls=%async_computation.4 | async-start | bytes 11501568 | tf_op jit(solution)/shard_map/all_gather | solution.py:952
  11.7 157.1 %all-gather.10.cloned.1.call-start = ((), (), s32[]{:S(2)}) async-start(), calls=%async_computation.5 | async-start | bytes 7077888 | tf_op jit(solution)/shard_map/all_gather | solution.py:953
  14.3 318.6 %reduce-scatter.6.cloned.1.call-start = ((), (), s32[]{:S(2)}) async-start(), calls=%async_computation.7 | async-start | bytes 12386304 | tf_op jit(solution)/shard_map/reduce_scatter | solution.py:1052
  15.5 60.8 %copy-start.84 = (f32[768]{0:T(1024)}, f32[768]{0:T(1024)S(1)}, u32[]{:S(2)}) copy-start(f32[768]{0:T(1024)S(1)} %get-tuple-element.194) | copy-start | bytes 9220
  15.5 105.3 %copy-start.94 = (f32[768]{0:T(1024)}, f32[768]{0:T(1024)S(1)}, u32[]{:S(2)}) copy-start(f32[768]{0:T(1024)S(1)} %get-tuple-element.195) | copy-start | bytes 9220
  15.5 105.3 %copy-start.116 = (f32[768]{0:T(1024)}, f32[768]{0:T(1024)S(1)}, u32[]{:S(2)}) copy-start(f32[768]{0:T(1024)S(1)} %get-tuple-element.146) | copy-start | bytes 9220
  15.5 119.8 %copy-start.96 = (f32[768]{0:T(1024)}, f32[768]{0:T(1024)S(1)}, u32[]{:S(2)}) copy-start(f32[768]{0:T(1024)S(1)} %get-tuple-element.196) | copy-start | bytes 9220
  15.6 119.8 %copy-start.118 = (f32[768]{0:T(1024)}, f32[768]{0:T(1024)S(1)}, u32[]{:S(2)}) copy-start(f32[768]{0:T(1024)S(1)} %get-tuple-element.144) | copy-start | bytes 9220
  15.6 50.8 %copy-start.119 = (pred[16]{0:T(512)(128)(4,1)}, pred[16]{0:T(512)(128)(4,1)S(1)}, u32[]{:S(2)}) copy-start(pred[16]{0:T(512)(128)(4,1)S(1)} %iota_compare_fusion.9) | copy-start | bytes 52
  15.6 105.2 %copy-start.101 = (f32[3072]{0:T(1024)}, f32[3072]{0:T(1024)S(1)}, u32[]{:S(2)}) copy-start(f32[3072]{0:T(1024)S(1)} %slice.325) | copy-start | bytes 36868
  16.1 120.3 %copy-start.65 = (s32[3,1024]{1,0:T(4,128)}, s32[3,1024]{1,0:T(4,128)S(1)}, u32[]{:S(2)}) copy-start(s32[3,1024]{1,0:T(4,128)S(1)} %get-tuple-element.101) | copy-start | bytes 36868
  98.1 32.5 %copy-start.78 = (f32[3,272]{1,0:T(4,128)}, f32[3,272]{1,0:T(4,128)S(1)}, u32[]{:S(2)}) copy-start(f32[3,272]{1,0:T(4,128)S(1)} %broadcast_multiply_fusion.13) | copy-start | bytes 9796
  100.0 30.6 %copy-start.86 = (f32[3,272]{1,0:T(4,128)}, f32[3,272]{1,0:T(4,128)S(1)}, u32[]{:S(2)}) copy-start(f32[3,272]{1,0:T(4,128)S(1)} %add_rsqrt_fusion.2) | copy-start | bytes 9796
  178.2 23.6 %copy-start.14 = (f32[2048]{0:T(1024)S(1)}, f32[2048]{0:T(1024)}, u32[]{:S(2)}) copy-start(f32[2048]{0:T(1024)} %slice.349) | copy-start | bytes 24580
  178.2 23.6 %copy-start.15 = (f32[1,768]{1,0:T(1,128)S(1)}, f32[1,768]{1,0:T(1,128)}, u32[]{:S(2)}) copy-start(f32[1,768]{1,0:T(1,128)} %broadcast_in_dim.97.bh_ref) | copy-start | bytes 9220
  201.6 26.2 %copy-start.28 = (bf16[3,256,512]{2,1,0:T(8,128)(2,1)}, bf16[3,256,512]{2,1,0:T(8,128)(2,1)S(1)}, u32[]{:S(2)}) copy-start(bf16[3,256,512]{2,1,0:T(8,128)(2,1)S(1)} %get-tuple-element.45.o_ref) | copy-start | bytes 2359300
  231.8 149.5 %reduce-scatter.4.cloned.1.call-start = ((), (), s32[]{:S(2)}) async-start(), calls=%async_computation.6 | async-start | bytes 3538944 | tf_op jit(solution)/shard_map/reduce_scatter | solution.py:1058
  237.2 44.4 %copy-start.34 = (f32[3,256,512]{2,1,0:T(8,128)S(1)}, f32[3,256,512]{2,1,0:T(8,128)}, u32[]{:S(2)}) copy-start(f32[3,256,512]{2,1,0:T(8,128)} %copy-done.33) | copy-start | bytes 4718596
  281.6 49.7 %copy-start.13 = (f32[8,512]{1,0:T(8,128)S(1)}, f32[8,512]{1,0:T(8,128)}, u32[]{:S(2)}) copy-start(f32[8,512]{1,0:T(8,128)} %copy-done.12) | copy-start | bytes 49156
  332.0 145.9 %reduce-scatter.8.cloned.1.call-start = ((), (), s32[]{:S(2)}) async-start(), calls=%async_computation.9 | async-start | bytes 442368 | tf_op jit(solution)/shard_map/reduce_scatter | solution.py:1108
  385.2 23.8 %copy-start.62 = (bf16[3,272,768]{2,1,0:T(8,128)(2,1)S(1)}, bf16[3,272,768]{2,1,0:T(8,128)(2,1)}, u32[]{:S(2)}) copy-start(bf16[3,272,768]{2,1,0:T(8,128)(2,1)} %copy-done.61) | copy-start | bytes 3760132
  444.5 112.5 %all-reduce.6.cloned.1.call-start = ((), (), s32[]{:S(2)}) async-start(), calls=%async_computation.8 | async-start | bytes 3538944 | tf_op jit(solution)/shard_map/psum | solution.py:1093
  447.4 203.5 %all-gather.12.cloned.1.call-start = ((), (), s32[]{:S(2)}) async-start(), calls=%async_computation.10 | async-start | bytes 1769472 | tf_op jit(solution)/shard_map/all_gather | solution.py:1122
  (112 other events, 658.7 us)
Sparse Core Ops, SparseCore 0:
  10.6 45.4 all-gather.5
  58.6 62.1 all-gather.7
  123.2 45.5 all-gather.9
  232.0 83.5 reduce-scatter.5
  332.1 49.1 reduce-scatter.3
  444.6 33.3 reduce-scatter.7
  481.0 75.8 all-reduce.5
  625.7 25.1 all-gather.11

commit v3 on v2

--- a/solution.py
+++ b/solution.py
@@ -131,18 +131,16 @@
     return jnp.where(place < 1, scores, other)
 
 
-def attend_forward_kernel(heads, head_dim, q_ref, k_ref, v_ref, o_ref, lse_ref):
-    main = k_ref.shape[1] - TAIL
+def attend_forward_group(heads, head_dim, q, k, v):
+    main = k.shape[0] - TAIL
     scale = head_dim ** (-0.5) * LOG2E
-    q_t = q_ref[0].astype(jnp.float32).T * scale
+    q_t = q.astype(jnp.float32).T * scale
     q_high = low(q_t)
     q_rest = low(q_t - q_high.astype(jnp.float32))
-    k_main = k_ref[0, :main]
-    k_tail = k_ref[0, main:]
-    k_main = jnp.concatenate([k_main, k_main], axis=1)
-    k_tail = jnp.concatenate([k_tail, k_tail], axis=1)
-    v_main = low(v_ref[0, :main].astype(jnp.float32).T)
-    v_tail = v_ref[0, main:]
+    k_main = jnp.concatenate([k[:main], k[:main]], axis=1)
+    k_tail = jnp.concatenate([k[main:], k[main:]], axis=1)
+    v_main = low(v[:main].astype(jnp.float32).T)
+    v_tail = v[main:]
     ones = jnp.ones((TAIL, main), jnp.bfloat16)
 
     def scores_of(head):
@@ -151,7 +149,7 @@
         q_h = jnp.concatenate([jnp.where(own, q_high, none), jnp.where(own, q_rest, none)], axis=0)
         return dot_f32(k_main, q_h, NN), live_tail(TAIL, dot_f32(k_tail, q_h, NN), MASKED_SCORE)
 
-    outs = []
+    outs, sums = [], []
     following = scores_of(0)
     for head in range(heads):
         span = slice(head * head_dim, (head + 1) * head_dim)
@@ -169,23 +167,25 @@
         )
         o_t = o_t[:head_dim] + dot_f32(v_tail, p_tail, TN)[span]
         outs.append(o_t * (1.0 / total))
-        lse_ref[0, 0, head : head + 1, :] = top + jnp.log2(total)
-    o_ref[0] = low(jnp.concatenate(outs, axis=0).T)
-
-
-def attend_backward_kernel(
-    heads, head_dim, q_ref, k_ref, v_ref, lse_ref, do_ref, o_ref, dq_ref, dk_ref, dv_ref
-):
-    main = k_ref.shape[1] - TAIL
-    rows = q_ref.shape[1]
+        sums.append(top + jnp.log2(total))
+    return low(jnp.concatenate(outs, axis=0).T), sums
+
+
+def attend_forward_kernel(heads, head_dim, q_ref, k_ref, v_ref, o_ref, lse_ref):
+    o_ref[0], sums = attend_forward_group(heads, head_dim, q_ref[0], k_ref[0], v_ref[0])
+    for head in range(heads):
+        lse_ref[0, 0, head : head + 1, :] = sums[head]
+
+
+def attend_backward_group(heads, head_dim, q, k, v, sums, do, o):
+    main = k.shape[0] - TAIL
+    rows = q.shape[0]
     unit = head_dim ** (-0.5)
-    q = q_ref[0]
-    do = do_ref[0]
     q_t = q.astype(jnp.float32).T * (unit * LOG2E)
     q_high = low(q_t).astype(jnp.float32)
     q_rest = q_t - q_high
     do_t = do.astype(jnp.float32).T
-    inner_t = do_t * o_ref[0].astype(jnp.float32).T
+    inner_t = do_t * o.astype(jnp.float32).T
     place = lax.broadcasted_iota(jnp.int32, q_t.shape, 0)
 
     def with_row(block, offset, value):
@@ -198,7 +198,7 @@
         own = own_span(q_t.shape, 0, head, head_dim)
         span = slice(head * head_dim, (head + 1) * head_dim)
         other = ((head + 1) % heads) * head_dim
-        lse = lse_ref[0, 0, head : head + 1, :]
+        lse = sums[head]
         inner = jnp.sum(inner_t[span], axis=0, keepdims=True)
         rest = with_row(jnp.where(own, q_rest, 0.0), other, -lse)
         score_sides.append(low(jnp.concatenate([jnp.where(own, q_high, 0.0), rest], axis=0)))
@@ -218,8 +218,8 @@
         terms = [dot_f32(part, side, NN) for part, side in zip(parts, sides)]
         return sum(terms[1:], terms[0])
 
-    k_main = k_ref[0, :main]
-    k_tail = k_ref[0, main:]
+    k_main = k[:main]
+    k_tail = k[main:]
     k_main_t = low(k_main.astype(jnp.float32).T)
 
     def with_ones(block):
@@ -229,8 +229,8 @@
         own = jnp.where(own_span(block.shape, 1, head, head_dim), block, jnp.ones_like(block))
         return jnp.concatenate([block, own], axis=1)
 
-    v_main = with_ones(v_ref[0, :main])
-    v_tail = with_ones(v_ref[0, main:])
+    v_main = with_ones(v[:main])
+    v_tail = with_ones(v[main:])
     dq_parts, p_mains, s_mains, p_tails, s_tails = [], [], [], [], []
     for head in range(heads):
         span = slice(head * head_dim, (head + 1) * head_dim)
@@ -244,14 +244,26 @@
         p_tails.append(low(p))
         s_tails.append(s_tail)
         dq_parts.append(dot_f32(k_main_t[span], s, NN) + dot_f32(k_tail, s_tail, TN)[span])
-    dk_ref[0, :main] = low(sum_heads(s_mains, q_sides) * unit)
-    dk_ref[0, main:] = low(sum_heads(s_tails, q_sides) * unit)
-    dv_ref[0, :main] = low(sum_heads(p_mains, do_sides))
-    dv_ref[0, main:] = low(sum_heads(p_tails, do_sides))
-    dq_ref[0] = low(jnp.concatenate(dq_parts, axis=0).T * unit)
+    dk = [low(sum_heads(part, q_sides) * unit) for part in (s_mains, s_tails)]
+    dv = [low(sum_heads(part, do_sides)) for part in (p_mains, p_tails)]
+    dq = low(jnp.concatenate(dq_parts, axis=0).T * unit)
+    return dq, dk, dv
+
+
+def attend_backward_kernel(
+    heads, head_dim, q_ref, k_ref, v_ref, lse_ref, do_ref, o_ref, dq_ref, dk_ref, dv_ref
+):
+    main = k_ref.shape[1] - TAIL
+    sums = [lse_ref[0, 0, head : head + 1, :] for head in range(heads)]
+    dq_ref[0], dk, dv = attend_backward_group(
+        heads, head_dim, q_ref[0], k_ref[0], v_ref[0], sums, do_ref[0], o_ref[0]
+    )
+    dk_ref[0, :main], dk_ref[0, main:] = dk
+    dv_ref[0, :main], dv_ref[0, main:] = dv
 
 
 VMEM_LIMIT = 32 * 1024 * 1024
+KERNEL_LIMIT = 58 * 1024 * 1024
 
 
 def attend_specs(q_rows, k_rows, heads):
@@ -435,14 +447,20 @@
 
 
 def exchange_kernel(
-    chunks,
-    g_ref,
+    table,
+    extra,
+    g_early,
+    g_late,
     small_ref,
-    out_ref,
+    out_early,
+    out_late,
     small_out,
-    pair_in,
-    plane_send,
-    plane_recv,
+    pair_early,
+    pair_late,
+    send_early,
+    send_late,
+    recv_early,
+    recv_late,
     small_in,
     small_line,
     pair_sems,
@@ -458,8 +476,13 @@
     core = lax.rem(own, 2)
     chip = lax.div(own, 2)
     partner = own + 1 - 2 * core
-    block = g_ref.shape[0] // PLANE
-    rows = block // chunks
+    grads = (g_early, g_late)
+    pair_ins = (pair_early, pair_late)
+    sends = (send_early, send_late)
+    recvs = (recv_early, recv_late)
+    outs = (out_early, out_late)
+    block = g_early.shape[0] // PLANE
+    order = range(len(table))
 
     def plane_peer(step):
         return lax.rem(own + step, PLANE)
@@ -488,39 +511,38 @@
             device_id_type=MESH,
         )
 
+    def span_of(at):
+        return pl.ds(table[at][1], table[at][2])
+
     def owned_rows(owner, at):
-        return pl.ds(pl.multiple_of(owner * block + at * rows, 16), rows)
+        start, rows = table[at][1:]
+        return pl.ds(pl.multiple_of(owner * block + start, 16), rows)
 
     def pair_copy(other, at):
+        part = table[at][0]
         target = lax.rem(chip + other, 4)
         return send(
-            g_ref.at[owned_rows(2 * target + 1 - core, at)],
-            pair_in.at[other, pl.ds(at * rows, rows)],
+            grads[part].at[owned_rows(2 * target + 1 - core, at)],
+            pair_ins[part].at[other, span_of(at)],
             pair_sems,
             (other, at),
             {"fsdp": partner},
         )
 
     def plane_copy(other, at):
+        part = table[at][0]
         target = lax.rem(chip + other, 4)
-        span = pl.ds(at * rows, rows)
         return send(
-            plane_send.at[other - 1, span],
-            plane_recv.at[other - 1, span],
+            sends[part].at[other - 1, span_of(at)],
+            recvs[part].at[other - 1, span_of(at)],
             plane_sems,
             (other - 1, at),
             {"fsdp": 2 * target + core},
         )
 
     def line_copy(step, at):
-        span = pl.ds(at * rows, rows)
-        return send(
-            out_ref.at[place, span],
-            out_ref.at[place, span],
-            line_sems,
-            (step - 1, at),
-            {"seq": line_peer(step)},
-        )
+        part = outs[table[at][0]].at[place, span_of(at)]
+        return send(part, part, line_sems, (step - 1, at), {"seq": line_peer(step)})
 
     def small_plane_copy(step):
         return send(
@@ -532,37 +554,27 @@
         )
 
     def small_line_copy(step):
-        return send(
-            small_line.at[place],
-            small_line.at[place],
-            small_line_sems,
-            (step - 1,),
-            {"seq": line_peer(step)},
-        )
+        part = small_line.at[place]
+        return send(part, part, small_line_sems, (step - 1,), {"seq": line_peer(step)})
 
     def small_out_copy(step):
-        return send(
-            small_out.at[own],
-            small_out.at[own],
-            small_out_sems,
-            (step - 1,),
-            {"fsdp": plane_peer(step)},
-        )
-
-    for at in range(chunks):
+        part = small_out.at[own]
+        return send(part, part, small_out_sems, (step - 1,), {"fsdp": plane_peer(step)})
+
+    for at in order:
         for other in (1, 2, 3, 0):
             pair_copy(other, at).start()
         if at == 0:
             for step in range(1, PLANE):
                 small_plane_copy(step).start()
-    for at in range(chunks):
+    for at in order:
+        part = table[at][0]
         for other in (1, 2, 3, 0):
             pair_copy(other, at).wait_recv()
             if other:
-                span = pl.ds(at * rows, rows)
                 target = lax.rem(chip + other, 4)
-                both = g_ref[owned_rows(2 * target + core, at)] + pair_in[other, span]
-                plane_send[other - 1, span] = low(both)
+                mine = grads[part][owned_rows(2 * target + core, at)]
+                sends[part][other - 1, span_of(at)] = low(mine + pair_ins[part][other, span_of(at)])
                 plane_copy(other, at).start()
     for step in range(1, PLANE):
         small_plane_copy(step).wait_recv()
@@ -572,13 +584,17 @@
     small_line[place] = total
     for step in range(1, line):
         small_line_copy(step).start()
-    for at in range(chunks):
-        span = pl.ds(at * rows, rows)
-        total = g_ref[owned_rows(own, at)] + pair_in[0, span]
+    for at in order:
+        part = table[at][0]
+        total = grads[part][owned_rows(own, at)] + pair_ins[part][0, span_of(at)]
         for other in (1, 2, 3):
             plane_copy(other, at).wait_recv()
-            total = total + plane_recv[other - 1, span].astype(jnp.float32)
-        out_ref[place, span] = low(total)
+            total = total + recvs[part][other - 1, span_of(at)].astype(jnp.float32)
+        rounded = low(total)
+        if part == 0:
+            rest = total[:, -extra:] - rounded[:, -extra:].astype(jnp.float32)
+            rounded = jnp.concatenate([rounded, low(rest)], axis=1)
+        outs[part][place, span_of(at)] = rounded
         for step in range(1, line):
             line_copy(step, at).start()
     for step in range(1, line):
@@ -594,44 +610,53 @@
         small_plane_copy(step).wait_send()
     for step in range(1, line):
         small_line_copy(step).wait_send()
-        for at in range(chunks):
+        for at in order:
             line_copy(step, at).wait()
-    for at in range(chunks):
+    for at in order:
         for other in range(4):
             pair_copy(other, at).wait_send()
             if other:
                 plane_copy(other, at).wait_send()
 
 
-def exchange(grads, small, line, collective_id, chunks=3):
+def exchange(early, late, small, line, extra, collective_id):
     plane = lax.axis_size("fsdp")
-    total, width = grads.shape
-    if plane != PLANE or total % (PLANE * 16 * chunks):
-        own = lax.psum_scatter(grads, "fsdp", scatter_dimension=0, tiled=True)
-        return lax.all_gather(low(own), "seq", axis=0, tiled=False), lax.psum(
-            small, ("fsdp", "seq")
-        )
+    total = early.shape[0]
+    if plane != PLANE or total % (PLANE * 48):
+        results = []
+        for part, rest in ((early, extra), (late, 0)):
+            own = lax.psum_scatter(part, "fsdp", scatter_dimension=0, tiled=True)
+            rounded = low(own)
+            if rest:
+                left = own[:, -rest:] - rounded[:, -rest:].astype(jnp.float32)
+                rounded = jnp.concatenate([rounded, low(left)], axis=1)
+            results.append(lax.all_gather(rounded, "seq", axis=0, tiled=False))
+        return results[0], results[1], lax.psum(small, ("fsdp", "seq"))
     block = total // PLANE
+    third = block // 3
+    table = tuple((0, at * third, third) for at in range(3)) + ((1, 0, block),)
+    widths = (early.shape[1], late.shape[1])
     padded = PLANE * SMALL_BLOCK[0] * SMALL_BLOCK[1]
     blocks = jnp.pad(small, (0, padded - small.shape[0])).reshape((PLANE,) + SMALL_BLOCK)
     dma = pltpu.SemaphoreType.DMA
-    gathered, summed = pl.pallas_call(
-        partial(exchange_kernel, chunks),
+    low_type, f32 = jnp.bfloat16, jnp.float32
+    first, second, summed = pl.pallas_call(
+        partial(exchange_kernel, table, extra),
         out_shape=[
-            jax.ShapeDtypeStruct((line, block, width), jnp.bfloat16),
-            jax.ShapeDtypeStruct(blocks.shape, jnp.float32),
-        ],
-        in_specs=[pl.BlockSpec(memory_space=pltpu.VMEM)] * 2,
-        out_specs=[pl.BlockSpec(memory_space=pltpu.VMEM)] * 2,
-        scratch_shapes=[
-            pltpu.VMEM((4, block, width), jnp.float32),
-            pltpu.VMEM((3, block, width), jnp.bfloat16),
-            pltpu.VMEM((3, block, width), jnp.bfloat16),
-            pltpu.VMEM((PLANE - 1,) + SMALL_BLOCK, jnp.float32),
-            pltpu.VMEM((line,) + SMALL_BLOCK, jnp.float32),
-            dma((2, 4, chunks)),
-            dma((2, 3, chunks)),
-            dma((2, line - 1, chunks)),
+            jax.ShapeDtypeStruct((line, block, widths[0] + extra), low_type),
+            jax.ShapeDtypeStruct((line, block, widths[1]), low_type),
+            jax.ShapeDtypeStruct(blocks.shape, f32),
+        ],
+        in_specs=[pl.BlockSpec(memory_space=pltpu.VMEM)] * 3,
+        out_specs=[pl.BlockSpec(memory_space=pltpu.VMEM)] * 3,
+        scratch_shapes=[pltpu.VMEM((4, block, width), f32) for width in widths]
+        + [pltpu.VMEM((3, block, width), low_type) for width in widths * 2]
+        + [
+            pltpu.VMEM((PLANE - 1,) + SMALL_BLOCK, f32),
+            pltpu.VMEM((line,) + SMALL_BLOCK, f32),
+            dma((2, 4, len(table))),
+            dma((2, 3, len(table))),
+            dma((2, line - 1, len(table))),
             dma((2, PLANE - 1)),
             dma((2, line - 1)),
             dma((2, PLANE - 1)),
@@ -642,8 +667,8 @@
         cost_estimate=pl.CostEstimate(
             flops=0, bytes_accessed=200 * 1024 * 1024, transcendentals=0
         ),
-    )(grads, blocks)
-    return gathered, summed.reshape(-1)
+    )(early, late, blocks)
+    return first, second, summed.reshape(-1)
 
 
 def gelu_parts(hidden):
@@ -907,9 +932,332 @@
     )(y0, dq, dk, dv, dmid, ranks, dec_full, dec_full, dec_full, vectors)
 
 
-def stack_rows(parts):
+E_HEADS = 128 * H_E // D_E
+E_DIM = D_E // H_E
+E_OUT = 4 * D_E
+E_UP = 5 * D_E
+E_DOWN = E_UP + FF_E
+E_EMBED = E_DOWN + FF_E
+SIZE = 768
+
+
+def tail_rows(first):
+    at = lax.broadcasted_iota(jnp.int32, (TAIL, first.shape[1]), 0)
+    return jnp.where(at == 0, first, 0.0)
+
+
+def encoder_kernel(
+    kept_ref,
+    place_ref,
+    w_ref,
+    vec_ref,
+    bu_ref,
+    be_ref,
+    x_ref,
+    mid_ref,
+    enc_ref,
+    qkv_ref,
+    lse_ref,
+    o_ref,
+    slope_ref,
+    act_ref,
+    e_ref,
+):
+    (gain1, gain2, gain3, cls, shift1, bq, bv, bo, shift2, bd, shift3) = (
+        vec_ref[i : i + 1, :] for i in range(11)
+    )
+    rows = dot_f32(kept_ref[0], w_ref[:, :D_E], NN) + place_ref[0]
+    x_ref[0] = jnp.concatenate([rows, tail_rows(cls)], axis=0)
+    scaled, _ = norm_rows(x_ref[0])
+    normed = low(scaled * gain1 + shift1)
+    for at, bias in enumerate((bq, None, bv)):
+        value = dot_f32(normed, w_ref[:, (at + 1) * D_E : (at + 2) * D_E], NN)
+        qkv_ref[0, :, at * D_E : (at + 1) * D_E] = low(value if bias is None else value + bias)
+    for group in range(D_E // 128):
+        parts = [
+            qkv_ref[0, :, at * D_E + group * 128 : at * D_E + (group + 1) * 128] for at in range(3)
+        ]
+        out, sums = attend_forward_group(E_HEADS, E_DIM, *parts)
+        o_ref[0, :, group * 128 : (group + 1) * 128] = out
+        for head in range(E_HEADS):
+            at = group * E_HEADS + head
+            lse_ref[0, at : at + 1, :] = sums[head]
+    middle = x_ref[0] + dot_f32(o_ref[0], w_ref[:, E_OUT:E_UP], NN) + bo
+    mid_ref[0] = middle
+    scaled, _ = norm_rows(middle)
+    second = low(scaled * gain2 + shift2)
+    encoded = middle + bd
+    for at in range(0, FF_E, SIZE):
+        span = slice(at, at + SIZE)
+        hidden = dot_f32(second, w_ref[:, E_UP + at : E_UP + at + SIZE], NN) + bu_ref[:, span]
+        value, slope = gelu_parts(hidden)
+        slope_ref[0, :, span] = slope
+        act_ref[0, :, span] = low(value)
+        encoded = encoded + dot_f32(
+            act_ref[0, :, span], w_ref[:, E_DOWN + at : E_DOWN + at + SIZE], NT
+        )
+    enc_ref[0] = encoded
+    scaled, _ = norm_rows(encoded)
+    third = low(scaled * gain3 + shift3)
+    e_ref[0] = low(dot_f32(third, w_ref[:, E_EMBED:], NN) + be_ref[...])
+
+
+def encoder(kept, placed, enc_full, vectors, bu, be):
+    images = kept.shape[0]
+    f32, low_type = jnp.float32, jnp.bfloat16
+    shapes = [
+        ((E_ROWS, D_E), f32),
+        ((E_ROWS, D_E), f32),
+        ((E_ROWS, D_E), f32),
+        ((E_ROWS, 3 * D_E), low_type),
+        ((H_E, E_ROWS), f32),
+        ((E_ROWS, D_E), low_type),
+        ((E_ROWS, FF_E), f32),
+        ((E_ROWS, FF_E), low_type),
+        ((E_ROWS, D_D), low_type),
+    ]
+    return pl.pallas_call(
+        encoder_kernel,
+        grid=(images,),
+        in_specs=[
+            per_image(KEEP, D_E),
+            per_image(KEEP, D_E),
+            whole(enc_full.shape),
+            whole((16, D_E)),
+            whole((1, FF_E)),
+            whole((1, D_D)),
+        ],
+        out_specs=[per_image(*shape) for shape, _ in shapes],
+        out_shape=[jax.ShapeDtypeStruct((images,) + shape, kind) for shape, kind in shapes],
+        compiler_params=pltpu.CompilerParams(vmem_limit_bytes=KERNEL_LIMIT),
+        cost_estimate=pl.CostEstimate(
+            flops=2 * images * E_ROWS * enc_full.size,
+            bytes_accessed=40 * 1024 * 1024,
+            transcendentals=2 * images * E_ROWS * FF_E,
+        ),
+    )(kept, placed, enc_full, vectors, bu, be)
+
+
+def turn_quarter(value, place):
+    width = value.shape[1]
+    quarter = width // 4
+    turned = pltpu.roll(value, lax.rem(width - quarter * place, width), axis=1)
+    return low(turned[:, :quarter])
+
+
+def encoder_back_kernel(
+    place_ref,
+    de_ref,
+    cls_ref,
+    mid_ref,
+    enc_ref,
+    o_ref,
+    slope_ref,
+    act_ref,
+    w_ref,
+    vec_ref,
+    do_ref,
+    dmid_ref,
+    grad_ref,
+    vec_grad,
+    bu_grad,
+    be_grad,
+    de_all,
+    hidden_all,
+):
+    image = pl.program_id(0)
+    place = place_ref[0]
+    clear_first((grad_ref, vec_grad, bu_grad, be_grad))
+    gain2, gain3, shift2, shift3 = (vec_ref[i : i + 1, :] for i in range(4))
+    at = lax.broadcasted_iota(jnp.int32, (TAIL, D_D), 0)
+    cls = column_sum(jnp.where(at == image, cls_ref[...].astype(jnp.float32), 0.0))
+    de_all[:KEEP] = de_ref[...]
+    de_all[KEEP:] = low(tail_rows(cls))
+    de = de_all[...]
+    be_grad[0:1, :] += column_sum(de.astype(jnp.float32))
+    scaled3, inverse3 = norm_rows(enc_ref[0])
+    third = low(scaled3 * gain3 + shift3)
+    quarter = FF_E // 4
+    first = D_E // 4
+    small = D_D // 4
+    grad_ref[:, first + 2 * quarter :] += dot_f32(
+        third, de_all[:, pl.ds(pl.multiple_of(place * small, small), small)], TN
+    )
+    up3, g_gain3, g_shift3 = norm_rows_back(
+        dot_f32(de, w_ref[:, E_EMBED:], NT), scaled3, inverse3, gain3
+    )
+    up3_low = low(up3)
+    scaled2, inverse2 = norm_rows(mid_ref[0])
+    second = low(scaled2 * gain2 + shift2)
+    own_hidden = pl.ds(pl.multiple_of(place * quarter, quarter), quarter)
+    back = jnp.zeros_like(up3)
+    for at in range(0, FF_E, SIZE):
+        span = slice(at, at + SIZE)
+        hidden = dot_f32(up3_low, w_ref[:, E_DOWN + at : E_DOWN + at + SIZE], NN)
+        hidden = low(hidden * slope_ref[0, :, span])
+        hidden_all[:, span] = hidden
+        bu_grad[0:1, span] += column_sum(hidden.astype(jnp.float32))
+        back = back + dot_f32(hidden, w_ref[:, E_UP + at : E_UP + at + SIZE], NT)
+    grad_ref[:, first : first + quarter] += dot_f32(second, hidden_all[:, own_hidden], TN)
+    grad_ref[:, first + quarter : first + 2 * quarter] += dot_f32(
+        up3_low, act_ref[0, :, own_hidden], TN
+    )
+    through, g_gain2, g_shift2 = norm_rows_back(back, scaled2, inverse2, gain2)
+    middle_grad = up3 + through
+    dmid_ref[0] = middle_grad
+    grad_ref[:, :first] += dot_f32(o_ref[0], turn_quarter(middle_grad, place), TN)
+    do_ref[0] = low(dot_f32(low(middle_grad), w_ref[:, E_OUT:E_UP], NT))
+    sums = (column_sum(middle_grad), g_shift2, column_sum(up3), g_shift3, g_gain2, g_gain3)
+    for at, part in enumerate(sums):
+        vec_grad[at : at + 1, :] += part
+
+
+def scalar_spec():
+    return pl.BlockSpec(memory_space=pltpu.SMEM)
+
+
+def encoder_back(place, de_sum, saved, enc_full, vectors):
+    mid, enc, o, slope, act = saved
+    images = mid.shape[0]
+    f32 = jnp.float32
+    width = D_E // 4 + FF_E // 2 + D_D // 4
+    return pl.pallas_call(
+        encoder_back_kernel,
+        grid=(images,),
+        in_specs=[
+            scalar_spec(),
+            pl.BlockSpec((KEEP, D_D), lambda i: (i, 0)),
+            pl.BlockSpec((TAIL, D_D), lambda i: (images * KEEP // TAIL, 0)),
+            per_image(E_ROWS, D_E),
+            per_image(E_ROWS, D_E),
+            per_image(E_ROWS, D_E),
+            per_image(E_ROWS, FF_E),
+            per_image(E_ROWS, FF_E),
+            whole(enc_full.shape),
+            whole((8, D_E)),
+        ],
+        out_specs=[
+            per_image(E_ROWS, D_E),
+            per_image(E_ROWS, D_E),
+            whole((D_E, width)),
+            whole((8, D_E)),
+            whole((8, FF_E)),
+            whole((8, D_D)),
+        ],
+        out_shape=[
+            jax.ShapeDtypeStruct((images, E_ROWS, D_E), jnp.bfloat16),
+            jax.ShapeDtypeStruct((images, E_ROWS, D_E), f32),
+            jax.ShapeDtypeStruct((D_E, width), f32),
+            jax.ShapeDtypeStruct((8, D_E), f32),
+            jax.ShapeDtypeStruct((8, FF_E), f32),
+            jax.ShapeDtypeStruct((8, D_D), f32),
+        ],
+        scratch_shapes=[
+            pltpu.VMEM((E_ROWS, D_D), jnp.bfloat16),
+            pltpu.VMEM((E_ROWS, FF_E), jnp.bfloat16),
+        ],
+        compiler_params=pltpu.CompilerParams(vmem_limit_bytes=KERNEL_LIMIT),
+        cost_estimate=pl.CostEstimate(
+            flops=3 * images * E_ROWS * enc_full.size,
+            bytes_accessed=50 * 1024 * 1024,
+            transcendentals=0,
+        ),
+    )(place, de_sum, de_sum, mid, enc, o, slope, act, enc_full, vectors)
+
+
+def encoder_entry_back_kernel(
+    place_ref,
+    kept_ref,
+    x_ref,
+    qkv_ref,
+    lse_ref,
+    o_ref,
+    do_ref,
+    dmid_ref,
+    w_ref,
+    vec_ref,
+    grad_ref,
+    vec_grad,
+    dqkv_ref,
+):
+    place = place_ref[0]
+    clear_first((grad_ref, vec_grad))
+    gain1, shift1 = (vec_ref[i : i + 1, :] for i in range(2))
+    for group in range(D_E // 128):
+        span = slice(group * 128, (group + 1) * 128)
+        parts = [
+            qkv_ref[0, :, at * D_E + group * 128 : at * D_E + (group + 1) * 128] for at in range(3)
+        ]
+        sums = [
+            lse_ref[0, group * E_HEADS + head : group * E_HEADS + head + 1, :]
+            for head in range(E_HEADS)
+        ]
+        dq, dk, dv = attend_backward_group(
+            E_HEADS, E_DIM, *parts, sums, do_ref[0, :, span], o_ref[0, :, span]
+        )
+        dqkv_ref[:, group * 128 : (group + 1) * 128] = dq
+        for at, pair in ((1, dk), (2, dv)):
+            lanes = slice(at * D_E + group * 128, at * D_E + (group + 1) * 128)
+            dqkv_ref[:KEEP, lanes], dqkv_ref[KEEP:, lanes] = pair
+    scaled, inverse = norm_rows(x_ref[0])
+    normed = low(scaled * gain1 + shift1)
+    quarter = D_E // 4
+    sums = []
+    for at in range(3):
+        part = dqkv_ref[:, at * D_E : (at + 1) * D_E].astype(jnp.float32)
+        if at != 1:
+            sums.append(column_sum(part))
+        grad_ref[:, (at + 1) * quarter : (at + 2) * quarter] += dot_f32(
+            normed, turn_quarter(part, place), TN
+        )
+    through, g_gain1, g_shift1 = norm_rows_back(
+        dot_f32(dqkv_ref[...], w_ref[:, D_E : 4 * D_E], NT), scaled, inverse, gain1
+    )
+    back = dmid_ref[0] + through
+    patches = back[:KEEP]
+    grad_ref[:, :quarter] += dot_f32(kept_ref[0], turn_quarter(patches, place), TN)
+    sums = [column_sum(patches), back[KEEP : KEEP + 1], g_shift1] + sums + [g_gain1]
+    for at, part in enumerate(sums):
+        vec_grad[at : at + 1, :] += part
+
+
+def encoder_entry_back(place, kept, saved, do, dmid, enc_full, vectors):
+    x0, qkv, lse, o = saved
+    images = kept.shape[0]
+    f32 = jnp.float32
+    return pl.pallas_call(
+        encoder_entry_back_kernel,
+        grid=(images,),
+        in_specs=[
+            scalar_spec(),
+            per_image(KEEP, D_E),
+            per_image(E_ROWS, D_E),
+            per_image(E_ROWS, 3 * D_E),
+            per_image(H_E, E_ROWS),
+            per_image(E_ROWS, D_E),
+            per_image(E_ROWS, D_E),
+            per_image(E_ROWS, D_E),
+            columns(D_E, 5 * D_E, 0),
+            whole((8, D_E)),
+        ],
+        out_specs=[whole((D_E, D_E)), whole((8, D_E))],
+        out_shape=[
+            jax.ShapeDtypeStruct((D_E, D_E), f32),
+            jax.ShapeDtypeStruct((8, D_E), f32),
+        ],
+        scratch_shapes=[pltpu.VMEM((E_ROWS, 3 * D_E), jnp.bfloat16)],
+        compiler_params=pltpu.CompilerParams(vmem_limit_bytes=KERNEL_LIMIT),
+        cost_estimate=pl.CostEstimate(
+            flops=8 * images * E_ROWS * D_E * 4 * D_E,
+            bytes_accessed=20 * 1024 * 1024,
+            transcendentals=images * H_E * E_ROWS * E_ROWS,
+        ),
+    )(place, kept, x0, qkv, lse, o, do, dmid, enc_full, vectors)
+
+
+def stack_rows(parts, count=8):
     rows = jnp.stack(parts)
-    return jnp.pad(rows, ((0, 8 - len(parts)), (0, 0)))
+    return jnp.pad(rows, ((0, count - len(parts)), (0, 0)))
 
 
 def adamw(weight, moment_one, moment_two, gradient, step_rate, decay_rate):
@@ -947,17 +1295,9 @@
     images, own_count, _ = pixels.shape
     masked_total = images * lax.axis_size("fsdp") * (PATCHES - KEEP)
 
-    enc_low = low(enc_w)
-    enc_first = lax.all_gather(enc_low[:, : 5 * D_E], "fsdp", axis=0, tiled=True)
-    enc_second = lax.all_gather(enc_low[:, 5 * D_E :], "fsdp", axis=0, tiled=True)
+    enc_full = lax.all_gather(low(enc_w), "fsdp", axis=0, tiled=True)
     dec_full = lax.all_gather(low(dec_w), "fsdp", axis=0, tiled=True)
     head_low = low(head_w)
-    w_patch = enc_first[:, :D_E]
-    e_qkv = enc_first[:, D_E : 4 * D_E]
-    e_out = enc_first[:, 4 * D_E :]
-    e_up = enc_second[:, :FF_E]
-    e_down = enc_second[:, FF_E : 2 * FF_E]
-    w_embed = enc_second[:, 2 * FF_E :]
     d_query = dec_full[:, :D_D]
     d_key = dec_full[:, D_D : 2 * D_D]
     d_value = dec_full[:, 2 * D_D : 3 * D_D]
@@ -983,29 +1323,16 @@
         jnp.where(restore[:, None, :] == ranks[None, :, None], patch_ids, 0), axis=2
     )
 
-    embedded = project(kept, w_patch) + (b_patch + positions(keep_ids, D_E))
-    e_tail = jnp.where(jnp.arange(TAIL)[:, None] == 0, cls_token[None, :], 0.0)
-    x0 = jnp.concatenate(
-        [embedded, jnp.broadcast_to(e_tail[None], (images, TAIL, D_E))], axis=1
-    )
-    e_n1, e_sc1, e_inv1 = norm_forward(x0, gains[0], e_shift1)
-    e_n1 = low(e_n1)
-    e_qkv_bias = jnp.concatenate([e_bq, jnp.zeros_like(e_bq), e_bv])
-    e_mixed = low(project(e_n1, e_qkv) + e_qkv_bias)
-    e_q = e_mixed[:, :, :D_E]
-    e_k = e_mixed[:, :, D_E : 2 * D_E]
-    e_v = e_mixed[:, :, 2 * D_E :]
-    e_o, e_lse = attend_forward(e_q, e_k, e_v, H_E)
-    e_mid = x0 + project(e_o, e_out) + e_bo
-    e_n2, e_sc2, e_inv2 = norm_forward(e_mid, gains[1], e_shift2)
-    e_n2 = low(e_n2)
-    e_hidden = project(e_n2, e_up) + e_bu
-    e_gelu, e_slope = gelu_parts(e_hidden)
-    e_act = low(e_gelu)
-    encoded = e_mid + project_back(e_act, e_down) + e_bd
-    e_n3, e_sc3, e_inv3 = norm_forward(encoded, gains[2], e_shift3)
-    e_n3 = low(e_n3)
-    shrunk = low(project(e_n3, w_embed) + b_embed)
+    x0, e_mid, encoded, e_mixed, e_lse, e_o, e_slope, e_act, shrunk = encoder(
+        kept,
+        b_patch + positions(keep_ids, D_E),
+        enc_full,
+        stack_rows(
+            gains[:3] + [cls_token, e_shift1, e_bq, e_bv, e_bo, e_shift2, e_bd, e_shift3], 16
+        ),
+        e_bu[None],
+        b_embed[None],
+    )
 
     pick = low(turned[:, :, None] == ranks[None, None, :])
     is_masked = turned >= KEEP
@@ -1058,55 +1385,30 @@
     dec_early = lax.psum_scatter(g_d_qkv, "fsdp", scatter_dimension=0, tiled=True)
     de_sum = line_sum(de_part, 7, 1)
     dec_late, de_sum = lax.optimization_barrier((dec_late, de_sum))
-    de = jnp.concatenate(
-        [
-            de_sum[: images * KEEP].reshape(images, KEEP, D_D),
-            jnp.pad(de_sum[images * KEEP :][:images, None], ((0, 0), (0, TAIL - 1), (0, 0))),
-        ],
-        axis=1,
-    )
-
-    def own_columns(tensor):
-        size = tensor.shape[2] // seq_count
-        return lax.dynamic_slice_in_dim(tensor, place * size, size, axis=2)
-
-    g_embed = weight_grad(e_n3, own_columns(de))
-    g_b_embed = row_sum(de)
-    e_up3, g_e_gain3, g_e_shift3 = norm_backward(
-        project_back(de, w_embed), e_sc3, e_inv3, gains[2]
-    )
-    e_up3_low = low(e_up3)
-    g_e_down = weight_grad(e_up3_low, own_columns(e_act))
-    g_e_bd = row_sum(e_up3)
-    e_dhidden = low(project(e_up3_low, e_down) * e_slope)
-    g_e_up = weight_grad(e_n2, own_columns(e_dhidden))
-    g_e_bu = row_sum(e_dhidden)
-    through, g_e_gain2, g_e_shift2 = norm_backward(
-        project_back(e_dhidden, e_up), e_sc2, e_inv2, gains[1]
-    )
-    e_dmid = e_up3 + through
-    e_dmid_low = low(e_dmid)
-    g_e_out = weight_grad(e_o, own_columns(e_dmid_low))
-    g_e_bo = row_sum(e_dmid)
-    e_do = low(project_back(e_dmid_low, e_out))
+
+    place_word = place[None].astype(jnp.int32)
+    e_do, e_dmid, early_grads, back_sums, bu_sums, be_sums = encoder_back(
+        place_word,
+        de_sum,
+        (e_mid, encoded, e_o, e_slope, e_act),
+        enc_full,
+        stack_rows([gains[1], gains[2], e_shift2, e_shift3]),
+    )
+    g_e_bo, g_e_shift2, g_e_bd, g_e_shift3, g_e_gain2, g_e_gain3 = (back_sums[i] for i in range(6))
+    g_e_bu = bu_sums[0]
+    g_b_embed = be_sums[0]
     dec_early, e_do = lax.optimization_barrier((dec_early, e_do))
     dec_grad_all = lax.psum(jnp.concatenate([dec_early, dec_late], axis=1), "seq")
-    e_dq, e_dk, e_dv = attend_backward(e_q, e_k, e_v, e_lse, e_do, e_o, H_E)
-    g_e_qkv = [weight_grad(e_n1, own_columns(part)) for part in (e_dq, e_dk, e_dv)]
-    g_e_bq = row_sum(e_dq)
-    g_e_bv = row_sum(e_dv)
-    e_dmixed = jnp.concatenate([e_dq, e_dk, e_dv], axis=2)
-    through, g_e_gain1, g_e_shift1 = norm_backward(
-        project_back(e_dmixed, e_qkv), e_sc1, e_inv1, gains[0]
-    )
-    dx0 = e_dmid + through
-    dx0_patch = dx0[:, :KEEP]
-    g_patch = weight_grad(kept, own_columns(low(dx0_patch)))
-    g_b_patch = row_sum(dx0_patch)
-    g_cls = jnp.sum(dx0[:, KEEP], axis=0)
-    enc_grads = jnp.concatenate([g_patch] + g_e_qkv + [g_e_out, g_e_up, g_e_down], axis=1)
-    embed_own = lax.psum_scatter(g_embed, "fsdp", scatter_dimension=0, tiled=True)
-    embed_all = lax.all_gather(embed_own, "seq", axis=0, tiled=False)
+    late_grads, entry_sums = encoder_entry_back(
+        place_word,
+        kept,
+        (x0, e_mixed, e_lse, e_o),
+        e_do,
+        e_dmid,
+        enc_full,
+        stack_rows([gains[0], e_shift1]),
+    )
+    g_b_patch, g_cls, g_e_shift1, g_e_bq, g_e_bv, g_e_gain1 = (entry_sums[i] for i in range(6))
 
     once = jnp.where(place == 0, 1.0, 0.0)
     enc_bias = [g_b_patch, g_cls, g_e_shift1, g_e_bq, g_e_bv, g_e_bo, g_e_shift2, g_e_bu]
@@ -1116,8 +1418,10 @@
     enc_gain = jnp.concatenate([g_e_gain1, g_e_gain2, g_e_gain3]) * once
     dec_gain = jnp.concatenate([g_d_gain1, g_d_gain2, g_d_gain3])
     small = jnp.concatenate([enc_gain, dec_gain, enc_bias, dec_bias, loss_part[None]])
-    dec_grad_all, enc_grads = lax.optimization_barrier((dec_grad_all, enc_grads))
-    enc_all, small = exchange(enc_grads, small, seq_count, 2)
+    embed_cols = D_D // seq_count
+    early_all, late_all, small = exchange(
+        early_grads, late_grads, small, seq_count, embed_cols, 2
+    )
     dec_grad = dec_grad_all[:, : 4 * D_D + 2 * FF_D]
     head_grad = lax.all_gather(
         dec_grad_all[:, 4 * D_D + 2 * FF_D :], "fsdp", axis=0, tiled=True
@@ -1129,12 +1433,17 @@
     quarter_e = D_E // seq_count
     quarter_f = FF_E // seq_count
     spans = []
-    for at in range(5):
-        spans += by_column(enc_all, at * quarter_e, quarter_e)
-    spans += by_column(enc_all, 5 * quarter_e, quarter_f)
-    spans += by_column(enc_all, 5 * quarter_e + quarter_f, quarter_f)
+    for at in range(4):
+        spans += by_column(late_all, at * quarter_e, quarter_e)
+    spans += by_column(early_all, 0, quarter_e)
+    spans += by_column(early_all, quarter_e, quarter_f)
+    spans += by_column(early_all, quarter_e + quarter_f, quarter_f)
     spans = [part.astype(jnp.float32) for part in spans]
-    enc_grad = jnp.concatenate(spans + [embed_all[at] for at in range(seq_count)], axis=1)
+    offset = quarter_e + 2 * quarter_f
+    rounded = by_column(early_all, offset, embed_cols)
+    rests = by_column(early_all, offset + embed_cols, embed_cols)
+    spans += [a.astype(jnp.float32) + b.astype(jnp.float32) for a, b in zip(rounded, rests)]
+    enc_grad = jnp.concatenate(spans, axis=1)
     n_gain = gain_w.shape[0]
     n_bias = bias_w.shape[0]
     gain_grad = small[:n_gain]

time: 670 us -> 526 us (0.79)
  waiting for transfers between devices: 130 us -> 39.5 us
  Pallas kernels: 272 us -> 359 us
  matrix products: 88.5 us -> 12.2 us
  local copies, waits for them, and re-layouts: 72.8 us -> 35.3 us
  blocking collectives: 12.5 us -> 0 us
  other arithmetic: 70.5 us -> 58.7 us
    pallas_call x1 -> x4, Pallas kernels: 58.9 us -> 184 us  [the longest x1 85.4 us: exchange(): pl.pallas_call(partial(exchange_kernel, table, extra), out_shape=[jax.Sha...]
    psum x1, waiting for transfers between devices: 65.9 us -> 0.02 us  [shards(): lax.psum(jnp.concatenate([dec_early, dec_late], axis=1), 'seq')]
    dot_general x13 -> x0, matrix products: 47.4 us -> none  [the longest x5 26.5 us: project_back(): jnp.einsum('ise,de->isd', row_block, weight, preferred_element_type=jnp.f...]
    dot_general x9 -> x3, matrix products: 39 us -> 9.22 us  [project(): jnp.einsum('isd,de->ise', row_block, weight, preferred_element_type=jnp.f...]
    pallas_call x2 -> x1, Pallas kernels: 66.4 us -> 42.5 us  [attend_backward(): pl.pallas_call(partial(attend_backward_kernel, heads, head_dim), grid=(im...]
    unnamed x281 -> x154, local copies, waits for them, and re-layouts: 43.9 us -> 20.5 us
    all_gather x1, waiting for transfers between devices: 21.7 us -> 0.12 us  [shards(): dec_full = lax.all_gather(low(dec_w), 'fsdp', axis=0, tiled=True)]
    pallas_call x2 -> x1, Pallas kernels: 37.9 us -> 22.5 us  [attend_forward(): pl.pallas_call(partial(attend_forward_kernel, heads, head_dim), grid=(ima...]
  transfers between devices with their start and end apart: 8 -> 6, of which waited for: 6 -> 4; matrix products, arithmetic and copies ran while one was open for 22% -> 12% of each run, Pallas kernels for 21% -> 60%
where the time goes in v3:
time: 526 us; the launch traced here: 521 us
  Pallas kernels  359 us (68%)
  other arithmetic  58.7 us (11%)
  waiting for transfers between devices  39.5 us (8%)
  local copies, waits for them, and re-layouts  35.3 us (7%)
  between operations  16.2 us (3%)
  matrix products  12.2 us (2%)
    pallas_call x1, Pallas kernels, exchange(): pl.pallas_call(partial(exchange_kernel, table, extra), out_shape=[jax.Sha...  85.4 us
    pallas_call x2, Pallas kernels, line_sum(): pl.pallas_call(partial(line_sum_kernel, chunks, lax.axis_size('seq')), ou...  64.6 us
    pallas_call x1, Pallas kernels, attend_backward(): pl.pallas_call(partial(attend_backward_kernel, heads, head_dim), grid=(im...  42.5 us
    pallas_call x1, Pallas kernels, encoder(): pl.pallas_call(encoder_kernel, grid=(images,), in_specs=[per_image(KEEP,...  36 us
    pallas_call x1, Pallas kernels, encoder_entry_back(): pl.pallas_call(encoder_entry_back_kernel, grid=(images,), in_specs=[scala...  33.1 us
    all_gather x1, waiting for transfers between devices, shards(): enc_full = lax.all_gather(low(enc_w), 'fsdp', axis=0, tiled=True)  31 us
    pallas_call x1, Pallas kernels, encoder_back(): pl.pallas_call(encoder_back_kernel, grid=(images,), in_specs=[scalar_spec...  29.6 us
    pallas_call x1, Pallas kernels, dec_middle(): pl.pallas_call(partial(dec_middle_kernel, grad_scale), grid=(images,), in...  26.1 us
  transfers between devices with their start and end apart: 6, of which 4 were waited for; matrix products, arithmetic and copies ran while one was open for 12% of the time, Pallas kernels for 60%

profile of v3, /device:TPU:9, one launch (start us, length us, event | category | flops | bytes accessed | tf_op | source)
XLA Modules:
  0.0 521.4 jit_solution(15117373177996006726)
XLA Ops:
  7.2 3.6 convert_element_type.258
  15.1 36.9 %shard_map.288 = bf16[768,768]{1,0:T(8,128)(2,1)S(1)} custom-call(bf16[768,768]{1,0:T(8,128)(2,1)S(1)} %bitcast.137), custom_call_target="tpu_custom_call" | custom-call | bytes 58982400 | tf_op jit(solution)/shard_map/pallas_call | solution.py:429
  56.5 3.7 multiply_sine_fusion.1
  62.9 4.2 multiply_sine_fusion
  68.7 31.0 %all-gather.4.cloned.1.call-done.w_ref = bf16[768,10496]{1,0:T(8,128)(2,1)} async-done(((bf16[96,10496]{1,0:T(8,128)(2,1)}), bf16[768,10496]{1,0:T(8,128)(2,1)}) %all-gather.4.cloned.1.call-update) | async-done | bytes 16121872 | tf_op jit(solution)/shard_map/all_gather | solution.py:1298
  99.7 36.0 %shard_map.289 = (f32[3,272,768]{2,1,0:T(8,128)}, f32[3,272,768]{2,1,0:T(8,128)}, f32[3,272,768]{2,1,0:T(8,128)}, bf16[3,272,2304]{2,1,0:T(8,128)(2,1)}, f32[3,1...) custom-call(bf16[3,256,768]{2,1,0:T(8,128)(2,1)} %bitcast.138, ...), custom_call_target="tpu_custom_call" | custom-call | flops 13155434496 | bytes 41943040 | tf_op jit(solution)/shard_map/pallas_call | solution.py:1019
  139.8 3.2 pad_maximum_fusion
  144.4 3.2 add_convert_fusion.1
  147.8 4.0 convolution_convert_fusion.k_ref
  153.8 3.2 add_convert_fusion.v_ref
  157.1 22.5 %shard_map.290 = (bf16[3,256,512]{2,1,0:T(8,128)(2,1)S(1)}, f32[3,4,4,256]{3,2,1,0:T(4,128)S(1)}) custom-call(bf16[3,256,512]{2,1,0:T(8,128)(2,1)S(1)} %add_convert_fusion.2.q_ref, bf16[3,1040,512]{2,1,0:T(8,128)(2,1)S(1)} %convolution_convert_fusion.k_ref, bf16[3,1040,512]{2,1,0:T(8,128)(2,1)S(1)} %add_convert_fusion.v_ref), custom_call_target="tpu_custom_call" | custom-call | flops 6543114240 | bytes 7962624 | tf_op jit(solution)/shard_map/pallas_call | solution.py:284
  180.5 26.1 %shard_map.291 = (bf16[3,256,512]{2,1,0:T(8,128)(2,1)S(1)}, f32[3,256,512]{2,1,0:T(8,128)S(1)}, f32[512,5376]{1,0:T(8,128)}, f32[8,512]{1,0:T(8,128)S(1)}, f32[8,2048]{1,0:T(8,128)S(1)}, /*index=5*/f32[8,768]{1,0:T(8,128)S(1)}) custom-call(bf16[3,256,512]{2,1,0:T(8,128)(2,1)S(1)} %get-tuple-element.55.o_ref, f32[3,256,512]{2,1,0:T(8,128)S(1)} %slice.421.y_ref, ...), custom_call_target="tpu_custom_call" | custom-call | flops 25367150592 | bytes 31457280 | tf_op jit(solution)/shard_map/pallas_call | solution.py:801
  215.9 42.5 %shard_map.292 = (bf16[3,256,512]{2,1,0:T(8,128)(2,1)S(1)}, bf16[3,1040,512]{2,1,0:T(8,128)(2,1)S(1)}, bf16[3,1040,512]{2,1,0:T(8,128)(2,1)S(1)}) custom-call(bf16[3,256,512]{2,1,0:T(8,128)(2,1)S(1)} %copy-done.12, bf16[3,1040,512]{2,1,0:T(8,128)(2,1)S(1)} %copy-done.14, bf16[3,1040,512]{2,1,0:T(8,128)(2,1)S(1)} %copy-done.16, ...), custom_call_target="tpu_custom_call" | custom-call | flops 16357785600 | bytes 15925248 | tf_op jit(solution)/shard_map/pallas_call | solution.py:309
  260.1 19.4 %shard_map.293 = (bf16[784,512]{1,0:T(8,128)(2,1)S(1)}, f32[512,1536]{1,0:T(8,128)}, f32[8,512]{1,0:T(8,128)S(1)}) custom-call(f32[3,1040,512]{2,1,0:T(8,128)} %get-tuple-element.119.y_ref, bf16[3,256,512]{2,1,0:T(8,128)(2,1)S(1)} %get-tuple-element.59.dq_ref, bf16[3,1040,512]{2,1,0:T(8,128)(2,1)S(1)} %get-tuple-element.60.dk_ref, ...), custom_call_target="tpu_custom_call" | custom-call | flops 19629342720 | bytes 25165824 | tf_op jit(solution)/shard_map/pallas_call | solution.py:904
  281.4 27.7 %shard_map.294.de_ref.cls_ref = bf16[784,512]{1,0:T(8,128)(2,1)S(1)} custom-call(bf16[784,512]{1,0:T(8,128)(2,1)S(1)} %get-tuple-element.63.x_ref), custom_call_target="tpu_custom_call" | custom-call | bytes 40140800 | tf_op jit(solution)/shard_map/pallas_call | solution.py:429
  313.0 29.6 %shard_map.295 = (bf16[3,272,768]{2,1,0:T(8,128)(2,1)}, f32[3,272,768]{2,1,0:T(8,128)}, f32[768,1856]{1,0:T(8,128)}, f32[8,768]{1,0:T(8,128)}, f32[8,3072]{1,0:T(8,128)}, /*index=5*/f32[8,512]{1,0:T(8,128)}) custom-call(s32[1]{0:T(128)} %bitcast.place_ref, bf16[784,512]{1,0:T(8,128)(2,1)} %copy-done.4, bf16[784,512]{1,0:T(8,128)(2,1)} %copy-done.4, ...), custom_call_target="tpu_custom_call" | custom-call | flops 19733151744 | bytes 52428800 | tf_op jit(solution)/shard_map/pallas_call | solution.py:1124
  348.5 33.1 %shard_map.296 = (f32[768,768]{1,0:T(8,128)}, f32[8,768]{1,0:T(8,128)}) custom-call(s32[1]{0:T(128)} %bitcast.place_ref, bf16[3,256,768]{2,1,0:T(8,128)(2,1)} %bitcast.139, f32[3,272,768]{2,1,0:T(8,128)} %get-tuple-element.71.x_ref, bf16[3,272,2304]{2,1,0:T(8,128)(2,1)} %get-tuple-element.72.qkv_ref, f32[3,12,272]{2,1,0:T(8,128)} %get-tuple-element.73.lse_ref, ...), custom_call_target="tpu_custom_call" | custom-call | flops 15401484288 | bytes 20971520 | tf_op jit(solution)/shard_map/pallas_call | solution.py:1228
  383.1 2.7 copy-done
  387.5 85.4 %shard_map.297 = (bf16[4,96,1984]{2,1,0:T(8,128)(2,1)S(1)}, bf16[4,96,768]{2,1,0:T(8,128)(2,1)S(1)}, f32[8,8,384]{2,1,0:T(8,128)S(1)}) custom-call(f32[768,1856]{1,0:T(8,128)S(1)} %copy-done, f32[768,768]{1,0:T(8,128)S(1)} %copy-done.1, f32[8,8,384]{2,1,0:T(8,128)S(1)} %reshape.170.small_ref), custom_call_target="tpu_custom_call" | custom-call | bytes 209715200 | tf_op jit(solution)/shard_map/pallas_call | solution.py:643
  475.8 5.0 concatenate.34
  482.6 11.2 %multiply_subtract_fusion = (f32[96,10496]{1,0:T(8,128)}, f32[96,10496]{1,0:T(8,128)}, f32[96,10496]{1,0:T(8,128)}) fusion(f32[96,10496]{1,0:T(8,128)} %param.19, f32[96,10496]{1,0:T(8,128)} %param.20, f32[96,10496]{1,0:T(8,128)} %concatenate.34, f32[96,10496]{1,0:T(8,128)} %param.21), kind=kLoop, calls=%fused_computation.8 | loop fusion | flops 14106624 | bytes 28213248 | tf_op jit(solution)/shard_map/sub | solution.py:1268
  495.7 6.1 %multiply_subtract_fusion.2 = (f32[64,6144]{1,0:T(8,128)}, f32[64,6144]{1,0:T(8,128)}, f32[64,6144]{1,0:T(8,128)}) fusion(f32[64,6144]{1,0:T(8,128)S(1)} %copy-done.28, f32[64,6144]{1,0:T(8,128)} %param.23, f32[64,6912]{1,0:T(8,128)} %all-reduce.8.cloned.1.call-done, f32[64,6144]{1,0:T(8,128)} %param.24), kind=kLoop, calls=%fused_computation.24 | loop fusion | flops 5505024 | bytes 11010048 | tf_op jit(solution)/shard_map/sub | solution.py:1268
  501.8 6.5 %all-gather.8.cloned.1.call-done = f32[512,768]{1,0:T(8,128)} async-done(((f32[64,768]{1,0:T(8,128)}), f32[512,768]{1,0:T(8,128)}) %all-gather.8.cloned.1.call-update) | async-done | bytes 1572880 | tf_op jit(solution)/shard_map/all_gather | solution.py:1426
  508.3 6.0 %multiply_subtract_fusion.1 = (f32[512,768]{1,0:T(8,128)}, f32[512,768]{1,0:T(8,128)}, f32[512,768]{1,0:T(8,128)}) fusion(f32[512,768]{1,0:T(8,128)S(1)} %copy-done.30, f32[512,768]{1,0:T(8,128)} %param.26, f32[512,768]{1,0:T(8,128)} %all-gather.8.cloned.1.call-done, f32[512,768]{1,0:T(8,128)} %param.27), kind=kLoop, calls=%fused_computation.23 | loop fusion | flops 5505024 | bytes 11010048 | tf_op jit(solution)/shard_map/sub | solution.py:1268
  (243 shorter events, 52.4 us)
Async XLA Ops:
  7.2 92.6 %all-gather.4.cloned.1.call-start = ((), (), s32[]{:S(2)}) async-start(), calls=%async_computation.2 | async-start | bytes 18137088 | tf_op jit(solution)/shard_map/all_gather | solution.py:1298
  10.9 136.8 %all-gather.6.cloned.1.call-start = ((), (), s32[]{:S(2)}) async-start(), calls=%async_computation.3 | async-start | bytes 7077888 | tf_op jit(solution)/shard_map/all_gather | solution.py:1299
  13.3 299.7 %reduce-scatter.3.cloned.1.call-start = ((), (), s32[]{:S(2)}) async-start(), calls=%async_computation.4 | async-start | bytes 12386304 | tf_op jit(solution)/shard_map/reduce_scatter | solution.py:1379
  14.6 122.0 %copy-start.33 = (s32[3,1024]{1,0:T(4,128)}, s32[3,1024]{1,0:T(4,128)S(1)}, u32[]{:S(2)}) copy-start(s32[3,1024]{1,0:T(4,128)S(1)} %get-tuple-element.117) | copy-start | bytes 36868
  14.6 38.4 %copy-start.37 = (f32[3840]{0:T(1024)S(1)}, f32[3840]{0:T(1024)}, u32[]{:S(2)}) copy-start(f32[3840]{0:T(1024)} %param.28) | copy-start | bytes 46084
  14.6 38.6 %copy-start.29 = (f32[512,768]{1,0:T(8,128)S(1)}, f32[512,768]{1,0:T(8,128)}, u32[]{:S(2)}) copy-start(f32[512,768]{1,0:T(8,128)} %param.25) | copy-start | bytes 4718596
  99.7 36.8 %copy-start.26 = (f32[1024,512]{1,0:T(8,128)S(1)}, f32[1024,512]{1,0:T(8,128)}, u32[]{:S(2)}) copy-start(f32[1024,512]{1,0:T(8,128)} %pad_maximum_fusion.1) | copy-start | bytes 6291460
  157.1 22.6 %copy-start.15 = (bf16[3,1040,512]{2,1,0:T(8,128)(2,1)}, bf16[3,1040,512]{2,1,0:T(8,128)(2,1)S(1)}, u32[]{:S(2)}) copy-start(bf16[3,1040,512]{2,1,0:T(8,128)(2,1)S(1)} %add_convert_fusion.v_ref) | copy-start | bytes 9584644
  157.1 23.2 %copy-start.58 = (f32[3,256]{1,0:T(4,128)S(1)}, f32[3,256]{1,0:T(4,128)}, u32[]{:S(2)}) copy-start(f32[3,256]{1,0:T(4,128)} %compare_convert_fusion) | copy-start | bytes 9220
  157.1 23.4 %copy-start.7 = (f32[2048]{0:T(1024)S(1)}, f32[2048]{0:T(1024)}, u32[]{:S(2)}) copy-start(f32[2048]{0:T(1024)} %slice.345) | copy-start | bytes 24580
  157.1 23.4 %copy-start.8 = (f32[1,768]{1,0:T(1,128)S(1)}, f32[1,768]{1,0:T(1,128)}, u32[]{:S(2)}) copy-start(f32[1,768]{1,0:T(1,128)} %broadcast_in_dim.106.bh_ref) | copy-start | bytes 9220
  180.3 26.3 %copy-start.17 = (bf16[3,256,512]{2,1,0:T(8,128)(2,1)}, bf16[3,256,512]{2,1,0:T(8,128)(2,1)S(1)}, u32[]{:S(2)}) copy-start(bf16[3,256,512]{2,1,0:T(8,128)(2,1)S(1)} %get-tuple-element.55.o_ref) | copy-start | bytes 2359300
  210.5 133.8 %reduce-scatter.5.cloned.1.call-start = ((), (), s32[]{:S(2)}) async-start(), calls=%async_computation.5 | async-start | bytes 3538944 | tf_op jit(solution)/shard_map/reduce_scatter | solution.py:1385
  215.9 44.2 %copy-start.21 = (f32[3,256,512]{2,1,0:T(8,128)S(1)}, f32[3,256,512]{2,1,0:T(8,128)}, u32[]{:S(2)}) copy-start(f32[3,256,512]{2,1,0:T(8,128)} %copy-done.20) | copy-start | bytes 4718596
  279.5 33.5 %copy-start.6 = (f32[8,512]{1,0:T(8,128)S(1)}, f32[8,512]{1,0:T(8,128)}, u32[]{:S(2)}) copy-start(f32[8,512]{1,0:T(8,128)} %copy-done.5) | copy-start | bytes 49156
  279.5 201.3 %all-reduce.8.cloned.1.call-start = ((), (), s32[]{:S(2)}) async-start(), calls=%async_computation.6 | async-start | bytes 3538944 | tf_op jit(solution)/shard_map/psum | solution.py:1401
  313.0 33.0 %copy-start.32 = (f32[64,5376]{1,0:T(8,128)S(1)}, f32[64,5376]{1,0:T(8,128)}, u32[]{:S(2)}) copy-start(f32[64,5376]{1,0:T(8,128)} %reduce-scatter.3.cloned.1.call-done) | copy-start | bytes 4128772
  348.4 159.9 %all-gather.8.cloned.1.call-start = ((), (), s32[]{:S(2)}) async-start(), calls=%async_computation.7 | async-start | bytes 1769472 | tf_op jit(solution)/shard_map/all_gather | solution.py:1426
  348.5 33.1 %copy-start.61 = (f32[8,768]{1,0:T(8,128)S(1)}, f32[8,768]{1,0:T(8,128)}, u32[]{:S(2)}) copy-start(f32[8,768]{1,0:T(8,128)} %get-tuple-element.80) | copy-start | bytes 73732
  482.5 12.4 %copy-start.36 = (f32[17408]{0:T(1024)S(1)}, f32[17408]{0:T(1024)}, u32[]{:S(2)}) copy-start(f32[17408]{0:T(1024)} %param.31) | copy-start | bytes 208900
  482.6 12.4 %copy-start.39 = (f32[17408]{0:T(1024)S(1)}, f32[17408]{0:T(1024)}, u32[]{:S(2)}) copy-start(f32[17408]{0:T(1024)} %param.32) | copy-start | bytes 208900
  482.6 12.4 %copy-start.40 = (f32[17408]{0:T(1024)S(1)}, f32[17408]{0:T(1024)}, u32[]{:S(2)}) copy-start(f32[17408]{0:T(1024)} %param.33) | copy-start | bytes 208900
  482.6 13.1 %copy-start.28 = (f32[64,6144]{1,0:T(8,128)S(1)}, f32[64,6144]{1,0:T(8,128)}, u32[]{:S(2)}) copy-start(f32[64,6144]{1,0:T(8,128)} %param.22) | copy-start | bytes 4718596
  495.7 12.6 %copy-start.30 = (f32[512,768]{1,0:T(8,128)S(1)}, f32[512,768]{1,0:T(8,128)}, u32[]{:S(2)}) copy-start(f32[512,768]{1,0:T(8,128)} %param.25) | copy-start | bytes 4718596
  (47 other events, 141.1 us)
Sparse Core Ops, SparseCore 0:
  11.0 88.6 all-gather.3
  102.2 45.5 all-gather.5
  210.6 83.5 reduce-scatter.2
  298.1 46.2 reduce-scatter.4
  348.5 102.6 all-reduce.7
  482.6 25.6 all-gather.7

commit v4 on v3

--- a/solution.py
+++ b/solution.py
@@ -423,6 +423,230 @@
             copy(1, at).wait_send()
 
 
+GATHER_CHUNKS = 6
+KEPT_CHUNKS = 8
+
+
+def start_kernel(
+    lines,
+    w_ref,
+    x_ref,
+    full_ref,
+    o_ref,
+    from_left,
+    from_right,
+    to_left,
+    to_right,
+    own_sem,
+    ring_sems,
+    pair_sems,
+    send_sem,
+    recv_sem,
+):
+    own = lax.axis_index("fsdp")
+    place = lax.axis_index("seq")
+    core = lax.rem(own, 2)
+    at_x = lax.rem(lax.div(own, 2), 2)
+    at_y = lax.div(own, 4)
+    odd = lax.rem(place, 2)
+    by_x = 2 - 4 * at_x
+    by_y = 4 - 8 * at_y
+    ahead = own + (1 - odd) * by_x + odd * by_y
+    aside = own + odd * by_x + (1 - odd) * by_y
+    across = own + by_x + by_y
+    partner = own + 1 - 2 * core
+    over = place + 1 - 2 * odd
+    has_left = place > 0
+    has_right = place < lines - 1
+    block = w_ref.shape[0]
+    rows = block // GATHER_CHUNKS
+    kept_rows = x_ref.shape[0] // KEPT_CHUNKS
+    barrier = pltpu.get_barrier_semaphore()
+
+    def greet(device):
+        pl.semaphore_signal(barrier, inc=1, device_id=device, device_id_type=MESH)
+
+    for device in (ahead, aside, partner):
+        greet({"fsdp": device})
+    pl.when(has_left)(lambda: greet({"seq": place - 1}))
+    pl.when(has_right)(lambda: greet({"seq": place + 1}))
+    peers = jnp.where(has_left, 1, 0) + jnp.where(has_right, 1, 0)
+    pl.semaphore_wait(barrier, peers + 3)
+
+    def span_of(owner, at):
+        return pl.ds(pl.multiple_of(owner * block + at * rows, 16), rows)
+
+    def copy_of(source, target, sems, at, device):
+        return pltpu.make_async_remote_copy(
+            src_ref=source,
+            dst_ref=target,
+            send_sem=sems.at[(0,) + at],
+            recv_sem=sems.at[(1,) + at],
+            device_id=device,
+            device_id_type=MESH,
+        )
+
+    def own_rows(at):
+        return w_ref.at[pl.ds(at * rows, rows)]
+
+    def ahead_copy(at):
+        target = full_ref.at[span_of(own, at)]
+        return copy_of(own_rows(at), target, ring_sems, (0, at), {"fsdp": ahead})
+
+    def aside_copy(at):
+        part = full_ref.at[span_of(ahead, at)]
+        return copy_of(part, part, ring_sems, (1, at), {"fsdp": aside})
+
+    def over_copy(at):
+        part = full_ref.at[span_of(ahead, at)]
+        return copy_of(part, part, ring_sems, (2, at), {"seq": over})
+
+    def pair_copy(kind, at):
+        target = full_ref.at[span_of((own, ahead, across, aside)[kind], at)]
+        source = own_rows(at) if kind == 0 else target
+        return copy_of(source, target, pair_sems, (kind, at), {"fsdp": partner})
+
+    def keep_copy(at):
+        return pltpu.make_async_copy(
+            own_rows(at), full_ref.at[span_of(own, at)], own_sem.at[at]
+        )
+
+    def send_own(at):
+        ahead_copy(at).start()
+        pair_copy(0, at).start()
+        keep_copy(at).start()
+
+    def kept_span(at):
+        return pl.ds(pl.multiple_of(at * kept_rows, 16), kept_rows)
+
+    def kept_copy(way, at, source=None):
+        span = kept_span(at)
+        source = (to_right, to_left)[way] if source is None else source
+        return pltpu.make_async_remote_copy(
+            src_ref=source.at[span],
+            dst_ref=(from_left, from_right)[way].at[span],
+            send_sem=send_sem.at[way, at],
+            recv_sem=recv_sem.at[way, at],
+            device_id={"seq": place + 1 if way == 0 else place - 1},
+            device_id_type=MESH,
+        )
+
+    def kept_step(step):
+        if step < KEPT_CHUNKS:
+            pl.when(jnp.logical_not(has_left))(lambda: kept_copy(0, step, x_ref).start())
+            pl.when(jnp.logical_not(has_right))(lambda: kept_copy(1, step, x_ref).start())
+        from_first = step - place
+        from_last = step - (lines - 1 - place)
+
+        @pl.when(has_left & (from_first >= 0) & (from_first < KEPT_CHUNKS))
+        def _():
+            kept_copy(0, from_first).wait_recv()
+
+            @pl.when(has_right)
+            def _():
+                span = kept_span(from_first)
+                to_right[span] = x_ref[span] + from_left[span]
+                kept_copy(0, from_first).start()
+
+        @pl.when(has_right & (from_last >= 0) & (from_last < KEPT_CHUNKS))
+        def _():
+            kept_copy(1, from_last).wait_recv()
+
+            @pl.when(has_left)
+            def _():
+                span = kept_span(from_last)
+                to_left[span] = x_ref[span] + from_right[span]
+                kept_copy(1, from_last).start()
+
+    send_own(0)
+    send_own(1)
+    kept_steps = list(range(KEPT_CHUNKS + lines - 1))
+    for at in range(GATHER_CHUNKS):
+        ahead_copy(at).wait_recv()
+        aside_copy(at).start()
+        over_copy(at).start()
+        pair_copy(1, at).start()
+        if at + 2 < GATHER_CHUNKS:
+            send_own(at + 2)
+        for _ in range(2):
+            if kept_steps:
+                kept_step(kept_steps.pop(0))
+        if at:
+            aside_copy(at - 1).wait_recv()
+            pair_copy(2, at - 1).start()
+            over_copy(at - 1).wait_recv()
+            pair_copy(3, at - 1).start()
+    last = GATHER_CHUNKS - 1
+    aside_copy(last).wait_recv()
+    pair_copy(2, last).start()
+    over_copy(last).wait_recv()
+    pair_copy(3, last).start()
+    for step in kept_steps:
+        kept_step(step)
+
+    @pl.when(jnp.logical_not(has_left))
+    def _():
+        o_ref[...] = x_ref[...] + from_right[...]
+        for at in range(KEPT_CHUNKS):
+            kept_copy(0, at, x_ref).wait_send()
+
+    @pl.when(jnp.logical_not(has_right))
+    def _():
+        o_ref[...] = x_ref[...] + from_left[...]
+        for at in range(KEPT_CHUNKS):
+            kept_copy(1, at, x_ref).wait_send()
+
+    @pl.when(has_left & has_right)
+    def _():
+        o_ref[...] = (x_ref[...] + from_left[...]) + from_right[...]
+        for at in range(KEPT_CHUNKS):
+            kept_copy(0, at).wait_send()
+            kept_copy(1, at).wait_send()
+
+    for at in range(GATHER_CHUNKS):
+        keep_copy(at).wait()
+        ahead_copy(at).wait_send()
+        aside_copy(at).wait_send()
+        over_copy(at).wait_send()
+        for kind in range(4):
+            pair_copy(kind, at).wait()
+
+
+def start_gather(own_w, own_kept, collective_id):
+    plane = lax.axis_size("fsdp")
+    lines = lax.axis_size("seq")
+    block, width = own_w.shape
+    if plane != PLANE or block % (16 * GATHER_CHUNKS) or lines % 2:
+        return lax.all_gather(own_w, "fsdp", axis=0, tiled=True), line_sum(
+            own_kept, KEPT_CHUNKS, collective_id
+        )
+    buffer = pltpu.VMEM(own_kept.shape, own_kept.dtype)
+    dma = pltpu.SemaphoreType.DMA
+    return pl.pallas_call(
+        partial(start_kernel, lines),
+        out_shape=[
+            jax.ShapeDtypeStruct((PLANE * block, width), own_w.dtype),
+            jax.ShapeDtypeStruct(own_kept.shape, own_kept.dtype),
+        ],
+        in_specs=[pl.BlockSpec(memory_space=pl.ANY), pl.BlockSpec(memory_space=pltpu.VMEM)],
+        out_specs=[pl.BlockSpec(memory_space=pl.ANY), pl.BlockSpec(memory_space=pltpu.VMEM)],
+        scratch_shapes=[buffer] * 4
+        + [
+            dma((GATHER_CHUNKS,)),
+            dma((2, 3, GATHER_CHUNKS)),
+            dma((2, 4, GATHER_CHUNKS)),
+            dma((2, KEPT_CHUNKS)),
+            dma((2, KEPT_CHUNKS)),
+        ],
+        compiler_params=pltpu.CompilerParams(
+            collective_id=collective_id, has_side_effects=True, vmem_limit_bytes=VMEM_LIMIT
+        ),
+        cost_estimate=pl.CostEstimate(
+            flops=0, bytes_accessed=200 * 1024 * 1024, transcendentals=0
+        ),
+    )(own_w, own_kept)
+
+
 def line_sum(block, chunks, collective_id):
     shape = jax.ShapeDtypeStruct(block.shape, block.dtype)
     buffer = pltpu.VMEM(block.shape, block.dtype)
@@ -452,9 +676,13 @@
     g_early,
     g_late,
     small_ref,
+    dec_ref,
+    head_ref,
     out_early,
     out_late,
     small_out,
+    dec_out,
+    head_out,
     pair_early,
     pair_late,
     send_early,
@@ -463,6 +691,16 @@
     recv_late,
     small_in,
     small_line,
+    dec_pair,
+    dec_send,
+    dec_recv,
+    dec_sum,
+    dec_line,
+    dec_pair_sems,
+    dec_plane_sems,
+    dec_split_sems,
+    dec_line_sems,
+    head_sems,
     pair_sems,
     plane_sems,
     line_sems,
@@ -561,12 +799,69 @@
         part = small_out.at[own]
         return send(part, part, small_out_sems, (step - 1,), {"fsdp": plane_peer(step)})
 
+    dec_rows = dec_ref.shape[0] // PLANE
+    dec_part = dec_rows // line
+
+    def dec_span(owner):
+        return pl.ds(pl.multiple_of(owner * dec_rows, 16), dec_rows)
+
+    def dec_pair_copy(other):
+        target = lax.rem(chip + other, 4)
+        return send(
+            dec_ref.at[dec_span(2 * target + 1 - core)],
+            dec_pair.at[other],
+            dec_pair_sems,
+            (other,),
+            {"fsdp": partner},
+        )
+
+    def dec_plane_copy(other):
+        target = lax.rem(chip + other, 4)
+        return send(
+            dec_send.at[other - 1],
+            dec_recv.at[other - 1],
+            dec_plane_sems,
+            (other - 1,),
+            {"fsdp": 2 * target + core},
+        )
+
+    def quarter_of(at):
+        return pl.ds(pl.multiple_of(at * dec_part, 16), dec_part)
+
+    def dec_split_copy(step):
+        to = line_peer(step)
+        return send(
+            dec_sum.at[quarter_of(to)],
+            dec_line.at[place],
+            dec_split_sems,
+            (step - 1,),
+            {"seq": to},
+        )
+
+    def dec_line_copy(step):
+        part = dec_out.at[quarter_of(place)]
+        return send(part, part, dec_line_sems, (step - 1,), {"seq": line_peer(step)})
+
+    head_rows = head_ref.shape[0]
+
+    def head_copy(step):
+        target = head_out.at[pl.ds(pl.multiple_of(own * head_rows, 16), head_rows)]
+        return send(head_ref, target, head_sems, (step - 1,), {"fsdp": plane_peer(step)})
+
+    for other in (1, 2, 3, 0):
+        dec_pair_copy(other).start()
     for at in order:
         for other in (1, 2, 3, 0):
             pair_copy(other, at).start()
         if at == 0:
             for step in range(1, PLANE):
                 small_plane_copy(step).start()
+    for other in (1, 2, 3, 0):
+        dec_pair_copy(other).wait_recv()
+        if other:
+            target = lax.rem(chip + other, 4)
+            dec_send[other - 1] = dec_ref[dec_span(2 * target + core)] + dec_pair[other]
+            dec_plane_copy(other).start()
     for at in order:
         part = table[at][0]
         for other in (1, 2, 3, 0):
@@ -584,6 +879,16 @@
     small_line[place] = total
     for step in range(1, line):
         small_line_copy(step).start()
+    total = dec_ref[dec_span(own)] + dec_pair[0]
+    for other in (1, 2, 3):
+        dec_plane_copy(other).wait_recv()
+        total = total + dec_recv[other - 1]
+    dec_sum[...] = total
+    for step in range(1, line):
+        dec_split_copy(step).start()
+    for step in range(1, PLANE):
+        head_copy(step).start()
+    head_out[pl.ds(pl.multiple_of(own * head_rows, 16), head_rows)] = head_ref[...]
     for at in order:
         part = table[at][0]
         total = grads[part][owned_rows(own, at)] + pair_ins[part][0, span_of(at)]
@@ -597,6 +902,16 @@
         outs[part][place, span_of(at)] = rounded
         for step in range(1, line):
             line_copy(step, at).start()
+        if at == 0:
+            dec_line[place] = dec_sum[quarter_of(place)]
+            for step in range(1, line):
+                dec_split_copy(step).wait_recv()
+            total = dec_line[0]
+            for other in range(1, dec_line.shape[0]):
+                total = total + dec_line[other]
+            dec_out[quarter_of(place)] = total
+            for step in range(1, line):
+                dec_line_copy(step).start()
     for step in range(1, line):
         small_line_copy(step).wait_recv()
     total = small_line[0]
@@ -608,7 +923,14 @@
     for step in range(1, PLANE):
         small_out_copy(step).wait()
         small_plane_copy(step).wait_send()
+        head_copy(step).wait()
+    for other in range(4):
+        dec_pair_copy(other).wait_send()
+        if other:
+            dec_plane_copy(other).wait_send()
     for step in range(1, line):
+        dec_split_copy(step).wait_send()
+        dec_line_copy(step).wait()
         small_line_copy(step).wait_send()
         for at in order:
             line_copy(step, at).wait()
@@ -619,10 +941,11 @@
                 plane_copy(other, at).wait_send()
 
 
-def exchange(early, late, small, line, extra, collective_id):
+def exchange(early, late, small, dec, head_own, line, extra, collective_id):
     plane = lax.axis_size("fsdp")
     total = early.shape[0]
-    if plane != PLANE or total % (PLANE * 48):
+    dec_rows = dec.shape[0] // plane
+    if plane != PLANE or total % (PLANE * 48) or dec_rows % (16 * line):
         results = []
         for part, rest in ((early, extra), (late, 0)):
             own = lax.psum_scatter(part, "fsdp", scatter_dimension=0, tiled=True)
@@ -631,7 +954,11 @@
                 left = own[:, -rest:] - rounded[:, -rest:].astype(jnp.float32)
                 rounded = jnp.concatenate([rounded, low(left)], axis=1)
             results.append(lax.all_gather(rounded, "seq", axis=0, tiled=False))
-        return results[0], results[1], lax.psum(small, ("fsdp", "seq"))
+        dec_sum = lax.psum(
+            lax.psum_scatter(dec, "fsdp", scatter_dimension=0, tiled=True), "seq"
+        )
+        head_all = lax.all_gather(head_own, "fsdp", axis=0, tiled=True)
+        return results[0], results[1], lax.psum(small, ("fsdp", "seq")), dec_sum, head_all
     block = total // PLANE
     third = block // 3
     table = tuple((0, at * third, third) for at in range(3)) + ((1, 0, block),)
@@ -640,20 +967,33 @@
     blocks = jnp.pad(small, (0, padded - small.shape[0])).reshape((PLANE,) + SMALL_BLOCK)
     dma = pltpu.SemaphoreType.DMA
     low_type, f32 = jnp.bfloat16, jnp.float32
-    first, second, summed = pl.pallas_call(
+    dec_cols = dec.shape[1]
+    first, second, summed, dec_sum, head_all = pl.pallas_call(
         partial(exchange_kernel, table, extra),
         out_shape=[
             jax.ShapeDtypeStruct((line, block, widths[0] + extra), low_type),
             jax.ShapeDtypeStruct((line, block, widths[1]), low_type),
             jax.ShapeDtypeStruct(blocks.shape, f32),
-        ],
-        in_specs=[pl.BlockSpec(memory_space=pltpu.VMEM)] * 3,
-        out_specs=[pl.BlockSpec(memory_space=pltpu.VMEM)] * 3,
+            jax.ShapeDtypeStruct((dec_rows, dec_cols), f32),
+            jax.ShapeDtypeStruct((PLANE * head_own.shape[0], head_own.shape[1]), f32),
+        ],
+        in_specs=[pl.BlockSpec(memory_space=pltpu.VMEM)] * 5,
+        out_specs=[pl.BlockSpec(memory_space=pltpu.VMEM)] * 5,
         scratch_shapes=[pltpu.VMEM((4, block, width), f32) for width in widths]
         + [pltpu.VMEM((3, block, width), low_type) for width in widths * 2]
         + [
             pltpu.VMEM((PLANE - 1,) + SMALL_BLOCK, f32),
             pltpu.VMEM((line,) + SMALL_BLOCK, f32),
+            pltpu.VMEM((4, dec_rows, dec_cols), f32),
+            pltpu.VMEM((3, dec_rows, dec_cols), f32),
+            pltpu.VMEM((3, dec_rows, dec_cols), f32),
+            pltpu.VMEM((dec_rows, dec_cols), f32),
+            pltpu.VMEM((line, dec_rows // line, dec_cols), f32),
+            dma((2, 4)),
+            dma((2, 3)),
+            dma((2, line - 1)),
+            dma((2, line - 1)),
+            dma((2, PLANE - 1)),
             dma((2, 4, len(table))),
             dma((2, 3, len(table))),
             dma((2, line - 1, len(table))),
@@ -667,8 +1007,8 @@
         cost_estimate=pl.CostEstimate(
             flops=0, bytes_accessed=200 * 1024 * 1024, transcendentals=0
         ),
-    )(early, late, blocks)
-    return first, second, summed.reshape(-1)
+    )(early, late, blocks, dec, head_own)
+    return first, second, summed.reshape(-1), dec_sum, head_all
 
 
 def gelu_parts(hidden):
@@ -840,6 +1180,54 @@
     )(
         attended, y_own, pixels, masked, dec_full, dec_full, dec_full, head_low, vectors, bu, bh
     )
+
+
+def dec_entry_kernel(e_ref, rank_ref, place_ref, q_w, k_w, v_w, vec_ref, y_ref, q_ref, k_ref, v_ref):
+    mask_token, gain, shift, bq, bv = (vec_ref[i : i + 1, :] for i in range(5))
+    ranks = jnp.broadcast_to(rank_ref[0], (E_ROWS, PATCHES))
+    at = lax.broadcasted_iota(jnp.int32, (E_ROWS, PATCHES), 0)
+    hidden = (at >= KEEP) & (at < KEEP + 3) & (ranks >= KEEP)
+    pick = low(jnp.where(((at == ranks) & (at < KEEP)) | hidden, 1.0, 0.0))
+    place = lax.broadcasted_iota(jnp.int32, (TAIL, D_D), 0)
+    token = jnp.zeros((TAIL, D_D), jnp.float32)
+    for row, part in enumerate(pieces_of(mask_token)):
+        token = jnp.where(place == row, part, token)
+    source = jnp.concatenate([e_ref[0, :KEEP], low(token)], axis=0)
+    y_ref[0, :PATCHES] = dot_f32(pick, source, TN) + place_ref[...]
+    cls = column_sum(jnp.where(place == 0, e_ref[0, KEEP:].astype(jnp.float32), 0.0))
+    y_ref[0, PATCHES:] = tail_rows(cls)
+    scaled, _ = norm_rows(y_ref[0])
+    normed = low(scaled * gain + shift)
+    q_ref[0] = low(dot_f32(normed[: q_ref.shape[1]], q_w[...], NN) + bq)
+    k_ref[0] = low(dot_f32(normed, k_w[...], NN))
+    v_ref[0] = low(dot_f32(normed, v_w[...], NN) + bv)
+
+
+def dec_entry(shrunk, ranks, placed, dec_full, vectors, own):
+    images = shrunk.shape[0]
+    kinds = [(D_ROWS, jnp.float32), (own, jnp.bfloat16), (D_ROWS, jnp.bfloat16)]
+    kinds.append(kinds[2])
+    return pl.pallas_call(
+        dec_entry_kernel,
+        grid=(images,),
+        in_specs=[
+            per_image(E_ROWS, D_D),
+            per_image(1, PATCHES),
+            whole((PATCHES, D_D)),
+            columns(D_D, D_D, 0),
+            columns(D_D, D_D, 1),
+            columns(D_D, D_D, 2),
+            whole((8, D_D)),
+        ],
+        out_specs=[per_image(rows, D_D) for rows, _ in kinds],
+        out_shape=[jax.ShapeDtypeStruct((images, rows, D_D), kind) for rows, kind in kinds],
+        compiler_params=pltpu.CompilerParams(vmem_limit_bytes=44 * 1024 * 1024),
+        cost_estimate=pl.CostEstimate(
+            flops=4 * images * D_ROWS * D_D * D_D * 2,
+            bytes_accessed=20 * 1024 * 1024,
+            transcendentals=0,
+        ),
+    )(shrunk, ranks, placed, dec_full, dec_full, dec_full, vectors)
 
 
 def dec_entry_back_kernel(
@@ -1271,6 +1659,56 @@
     return (moment_one, moment_two, weight)
 
 
+def enc_update_kernel(w_ref, m_ref, v_ref, early_ref, late_ref, m_out, v_out, w_out):
+    lines = early_ref.shape[0]
+    quarter_e, quarter_f, quarter_d = D_E // lines, FF_E // lines, D_D // lines
+    pieces = [(late_ref, at * quarter_e, quarter_e) for at in range(4)]
+    pieces += [
+        (early_ref, 0, quarter_e),
+        (early_ref, quarter_e, quarter_f),
+        (early_ref, quarter_e + quarter_f, quarter_f),
+        (early_ref, quarter_e + 2 * quarter_f, quarter_d),
+    ]
+    start = 0
+    for number, (ref, offset, size) in enumerate(pieces):
+        parts = [ref[at, :, offset : offset + size].astype(jnp.float32) for at in range(lines)]
+        if number == len(pieces) - 1:
+            rests = [ref[at, :, offset + size : offset + 2 * size] for at in range(lines)]
+            parts = [a + b.astype(jnp.float32) for a, b in zip(parts, rests)]
+        span = slice(start, start + lines * size)
+        start += lines * size
+        m_out[:, span], v_out[:, span], w_out[:, span] = adamw(
+            w_ref[:, span],
+            m_ref[:, span],
+            v_ref[:, span],
+            jnp.concatenate(parts, axis=1),
+            MATRIX_RATE,
+            MATRIX_DECAY,
+        )
+
+
+def enc_update(weight, moment_one, moment_two, early, late):
+    rows, cols = weight.shape
+    lines = early.shape[0]
+    step = 16 if rows % 16 == 0 else rows
+    plain = pl.BlockSpec((step, cols), lambda i: (i, 0))
+    return pl.pallas_call(
+        enc_update_kernel,
+        grid=(rows // step,),
+        in_specs=[plain] * 3
+        + [
+            pl.BlockSpec((lines, step, part.shape[2]), lambda i: (0, i, 0))
+            for part in (early, late)
+        ],
+        out_specs=[plain] * 3,
+        out_shape=[jax.ShapeDtypeStruct(weight.shape, jnp.float32)] * 3,
+        compiler_params=pltpu.CompilerParams(vmem_limit_bytes=VMEM_LIMIT),
+        cost_estimate=pl.CostEstimate(
+            flops=20 * weight.size, bytes_accessed=26 * weight.size, transcendentals=0
+        ),
+    )(weight, moment_one, moment_two, early, late)
+
+
 def shards(
     pixels,
     restore,
@@ -1295,12 +1733,9 @@
     images, own_count, _ = pixels.shape
     masked_total = images * lax.axis_size("fsdp") * (PATCHES - KEEP)
 
-    enc_full = lax.all_gather(low(enc_w), "fsdp", axis=0, tiled=True)
+    enc_low = low(enc_w)
     dec_full = lax.all_gather(low(dec_w), "fsdp", axis=0, tiled=True)
     head_low = low(head_w)
-    d_query = dec_full[:, :D_D]
-    d_key = dec_full[:, D_D : 2 * D_D]
-    d_value = dec_full[:, 2 * D_D : 3 * D_D]
 
     pieces = split_vector(bias_w, bias_widths())
     gains = split_vector(gain_w, [D_E, D_E, D_E, D_D, D_D, D_D])
@@ -1317,7 +1752,8 @@
     own_restore = turned[:, :own_count]
     own_pick = low(own_restore[:, None, :] == ranks[None, :, None])
     own_kept = jnp.einsum("irp,ipd->ird", own_pick, pixels, preferred_element_type=jnp.float32)
-    kept = line_sum(low(own_kept).reshape(images * KEEP, PIX), 8, 0).reshape(images, KEEP, PIX)
+    enc_full, kept = start_gather(enc_low, low(own_kept).reshape(images * KEEP, PIX), 0)
+    kept = kept.reshape(images, KEEP, PIX)
     patch_ids = jnp.arange(PATCHES, dtype=jnp.int32)
     keep_ids = jnp.sum(
         jnp.where(restore[:, None, :] == ranks[None, :, None], patch_ids, 0), axis=2
@@ -1334,29 +1770,17 @@
         b_embed[None],
     )
 
-    pick = low(turned[:, :, None] == ranks[None, None, :])
-    is_masked = turned >= KEEP
     turned_ids = lax.rem(patch_ids + place * own_count, PATCHES)
-    spread = jnp.einsum(
-        "ipr,ird->ipd", pick, shrunk[:, :KEEP], preferred_element_type=jnp.float32
-    )
-    patch_rows = (
-        jnp.where(is_masked[..., None], mask_token, spread) + positions(turned_ids, D_D)[None]
-    )
-    d_tail = jnp.where(
-        jnp.arange(TAIL)[None, :, None] == 0,
-        shrunk[:, KEEP : KEEP + 1].astype(jnp.float32),
-        0.0,
-    )
-    y0 = jnp.concatenate([patch_rows, d_tail], axis=1)
-    d_n1, d_sc1, d_inv1 = norm_forward(y0, gains[3], d_shift1)
-    d_n1 = low(d_n1)
-
+    ranks_row = turned[:, None, :]
+    y0, d_q, d_k, d_v = dec_entry(
+        shrunk,
+        ranks_row,
+        positions(turned_ids, D_D),
+        dec_full,
+        stack_rows([mask_token, gains[3], d_shift1, d_bq, d_bv]),
+        own_count,
+    )
     y0_own = y0[:, :own_count]
-    n1_own = d_n1[:, :own_count]
-    d_q = low(project(n1_own, d_query) + d_bq)
-    d_k = low(project(d_n1, d_key))
-    d_v = low(project(d_n1, d_value) + d_bv)
     d_o, d_lse = attend_forward(d_q, d_k, d_v, H_D)
     own_masked = (own_restore >= KEEP).astype(jnp.float32)
     own_masked = jnp.broadcast_to(own_masked[..., None], own_masked.shape + (128,))
@@ -1379,12 +1803,12 @@
     dec_late = lax.psum_scatter(late_grads, "fsdp", scatter_dimension=0, tiled=True)
     d_dq, d_dk, d_dv = attend_backward(d_q, d_k, d_v, d_lse, d_do, d_o, H_D)
     de_part, g_d_qkv, entry_sums = dec_entry_back(
-        y0, d_dq, d_dk, d_dv, d_dmid, turned[:, None, :], dec_full, stack_rows([gains[3], d_shift1])
+        y0, d_dq, d_dk, d_dv, d_dmid, ranks_row, dec_full, stack_rows([gains[3], d_shift1])
     )
     g_mask, g_d_shift1, g_d_bq, g_d_bv, g_d_gain1 = (entry_sums[i] for i in range(5))
-    dec_early = lax.psum_scatter(g_d_qkv, "fsdp", scatter_dimension=0, tiled=True)
     de_sum = line_sum(de_part, 7, 1)
     dec_late, de_sum = lax.optimization_barrier((dec_late, de_sum))
+    dec_late = lax.psum(dec_late, "seq")
 
     place_word = place[None].astype(jnp.int32)
     e_do, e_dmid, early_grads, back_sums, bu_sums, be_sums = encoder_back(
@@ -1397,8 +1821,6 @@
     g_e_bo, g_e_shift2, g_e_bd, g_e_shift3, g_e_gain2, g_e_gain3 = (back_sums[i] for i in range(6))
     g_e_bu = bu_sums[0]
     g_b_embed = be_sums[0]
-    dec_early, e_do = lax.optimization_barrier((dec_early, e_do))
-    dec_grad_all = lax.psum(jnp.concatenate([dec_early, dec_late], axis=1), "seq")
     late_grads, entry_sums = encoder_entry_back(
         place_word,
         kept,
@@ -1419,38 +1841,25 @@
     dec_gain = jnp.concatenate([g_d_gain1, g_d_gain2, g_d_gain3])
     small = jnp.concatenate([enc_gain, dec_gain, enc_bias, dec_bias, loss_part[None]])
     embed_cols = D_D // seq_count
-    early_all, late_all, small = exchange(
-        early_grads, late_grads, small, seq_count, embed_cols, 2
-    )
-    dec_grad = dec_grad_all[:, : 4 * D_D + 2 * FF_D]
-    head_grad = lax.all_gather(
-        dec_grad_all[:, 4 * D_D + 2 * FF_D :], "fsdp", axis=0, tiled=True
-    )
-
-    def by_column(gathered, offset, size):
-        return [gathered[at, :, offset : offset + size] for at in range(seq_count)]
-
-    quarter_e = D_E // seq_count
-    quarter_f = FF_E // seq_count
-    spans = []
-    for at in range(4):
-        spans += by_column(late_all, at * quarter_e, quarter_e)
-    spans += by_column(early_all, 0, quarter_e)
-    spans += by_column(early_all, quarter_e, quarter_f)
-    spans += by_column(early_all, quarter_e + quarter_f, quarter_f)
-    spans = [part.astype(jnp.float32) for part in spans]
-    offset = quarter_e + 2 * quarter_f
-    rounded = by_column(early_all, offset, embed_cols)
-    rests = by_column(early_all, offset + embed_cols, embed_cols)
-    spans += [a.astype(jnp.float32) + b.astype(jnp.float32) for a, b in zip(rounded, rests)]
-    enc_grad = jnp.concatenate(spans, axis=1)
+    dec_late, late_grads = lax.optimization_barrier((dec_late, late_grads))
+    early_all, late_all, small, dec_early, head_grad = exchange(
+        early_grads,
+        late_grads,
+        small,
+        g_d_qkv,
+        dec_late[:, D_D + 2 * FF_D :],
+        seq_count,
+        embed_cols,
+        2,
+    )
+    dec_grad = jnp.concatenate([dec_early, dec_late[:, : D_D + 2 * FF_D]], axis=1)
     n_gain = gain_w.shape[0]
     n_bias = bias_w.shape[0]
     gain_grad = small[:n_gain]
     bias_grad = small[n_gain : n_gain + n_bias]
     loss_total = small[n_gain + n_bias]
 
-    enc_new = adamw(enc_w, enc_m, enc_v, enc_grad, MATRIX_RATE, MATRIX_DECAY)
+    enc_new = tuple(enc_update(enc_w, enc_m, enc_v, early_all, late_all))
     dec_new = adamw(dec_w, dec_m, dec_v, dec_grad, MATRIX_RATE, MATRIX_DECAY)
     head_new = adamw(head_w, head_m, head_v, head_grad, MATRIX_RATE, MATRIX_DECAY)
     gain_new = adamw(gain_w, gain_m, gain_v, gain_grad, SMALL_RATE, 0.0)

time: 526 us -> 551 us (1.048)
  Pallas kernels: 359 us -> 439 us
  waiting for transfers between devices: 39.5 us -> 0.11 us
  other arithmetic: 58.7 us -> 34.5 us
  local copies, waits for them, and re-layouts: 35.3 us -> 57.1 us
  matrix products: 12.2 us -> 0.47 us
    pallas_call x0 -> x3, Pallas kernels: none -> 110 us  [the longest x1 94 us: start_gather(): pl.pallas_call(partial(start_kernel, lines), out_shape=[jax.ShapeDtypeStr...]
    all_gather x2 -> x0, waiting for transfers between devices: 37.5 us -> none  [the longest x1 31 us: shards(): enc_full = lax.all_gather(low(enc_w), 'fsdp', axis=0, tiled=True)]
    pallas_call x2 -> x1, Pallas kernels: 64.6 us -> 28.9 us  [line_sum(): pl.pallas_call(partial(line_sum_kernel, chunks, lax.axis_size('seq')), ou...]
    unnamed x154 -> x131, local copies, waits for them, and re-layouts: 20.5 us -> 46.6 us
    sub x5 -> x4, other arithmetic: 24.7 us -> 12.5 us  [adamw(): weight - step_rate * (fixed_one / (jnp.sqrt(fixed_two) + ADAM_EPS) + deca...]
    dot_general x4 -> x0, matrix products: 11.8 us -> none  [the longest x3 9.22 us: project(): jnp.einsum('isd,de->ise', row_block, weight, preferred_element_type=jnp.f...]
    pallas_call x1, Pallas kernels: 85.4 us -> 92.7 us  [exchange(): pl.pallas_call(partial(exchange_kernel, table, extra), out_shape=[jax.Sha...]
    concatenate x2 -> x1, other arithmetic: 5.56 us -> 0.04 us  [shards(): jnp.concatenate([restore, restore], axis=1)]
  transfers between devices with their start and end apart: 6 -> 3, of which waited for: 4 -> 0; matrix products, arithmetic and copies ran while one was open for 12% -> 8% of each run, Pallas kernels for 60% -> 52%
where the time goes in v4:
time: 551 us; the launch traced here: 547 us
  Pallas kernels  439 us (80%)
  local copies, waits for them, and re-layouts  57.1 us (10%)
  other arithmetic  34.5 us (6%)
  between operations  15.4 us (3%)
    pallas_call x1, Pallas kernels, start_gather(): pl.pallas_call(partial(start_kernel, lines), out_shape=[jax.ShapeDtypeStr...  94 us
    pallas_call x1, Pallas kernels, exchange(): pl.pallas_call(partial(exchange_kernel, table, extra), out_shape=[jax.Sha...  92.7 us
    unnamed x131, local copies, waits for them, and re-layouts  46.6 us
    pallas_call x1, Pallas kernels, attend_backward(): pl.pallas_call(partial(attend_backward_kernel, heads, head_dim), grid=(im...  42.6 us
    pallas_call x1, Pallas kernels, encoder(): pl.pallas_call(encoder_kernel, grid=(images,), in_specs=[per_image(KEEP,...  35.9 us
    pallas_call x1, Pallas kernels, encoder_entry_back(): pl.pallas_call(encoder_entry_back_kernel, grid=(images,), in_specs=[scala...  33.2 us
    pallas_call x1, Pallas kernels, encoder_back(): pl.pallas_call(encoder_back_kernel, grid=(images,), in_specs=[scalar_spec...  29.9 us
    pallas_call x1, Pallas kernels, line_sum(): pl.pallas_call(partial(line_sum_kernel, chunks, lax.axis_size('seq')), ou...  28.9 us
  transfers between devices with their start and end apart: 3, of which 0 were waited for; matrix products, arithmetic and copies ran while one was open for 8% of the time, Pallas kernels for 52%

profile of v4, /device:TPU:9, one launch (start us, length us, event | category | flops | bytes accessed | tf_op | source)
XLA Modules:
  0.0 546.9 jit_solution(4554022888266190579)
XLA Ops:
  7.2 2.4 convert_element_type.48
  10.4 2.4 convert_element_type.44.w_ref
  14.3 2.4 convert_element_type.50.head_w
  17.3 94.0 %shard_map.288 = (bf16[768,10496]{1,0:T(8,128)(2,1)S(1)}, bf16[768,768]{1,0:T(8,128)(2,1)S(1)}) custom-call(bf16[96,10496]{1,0:T(8,128)(2,1)S(1)} %convert_element_type.44.w_ref, bf16[768,768]{1,0:T(8,128)(2,1)S(1)} %bitcast.34), custom_call_target="tpu_custom_call" | custom-call | bytes 209715200 | tf_op jit(solution)/shard_map/pallas_call | solution.py:625
  111.4 5.5 %copy-done.15 = bf16[768,10496]{1,0:T(8,128)(2,1)} copy-done((bf16[768,10496]{1,0:T(8,128)(2,1)}, bf16[768,10496]{1,0:T(8,128)(2,1)S(1)}, u32[]{:S(2)}) %copy-start.15) | copy-done | bytes 16121880
  116.9 3.7 multiply_sine_fusion.1
  121.4 4.2 multiply_sine_fusion
  127.2 35.9 %shard_map.289 = (f32[3,272,768]{2,1,0:T(8,128)}, f32[3,272,768]{2,1,0:T(8,128)}, f32[3,272,768]{2,1,0:T(8,128)}, bf16[3,272,2304]{2,1,0:T(8,128)(2,1)}, f32[3,1...) custom-call(bf16[3,256,768]{2,1,0:T(8,128)(2,1)} %bitcast.36, ...), custom_call_target="tpu_custom_call" | custom-call | flops 13155434496 | bytes 41943040 | tf_op jit(solution)/shard_map/pallas_call | solution.py:1407
  164.3 9.0 %shard_map.290 = (f32[3,1040,512]{2,1,0:T(8,128)}, bf16[3,256,512]{2,1,0:T(8,128)(2,1)S(1)}, bf16[3,1040,512]{2,1,0:T(8,128)(2,1)S(1)}, bf16[3,1040,512]{2,1,0:T(8,128)(2,1)S(1)}) custom-call(bf16[3,272,512]{2,1,0:T(8,128)(2,1)S(1)} %copy-done.21, s32[3,1,1024]{2,1,0:T(1,128)S(1)} %broadcast_in_dim.49.rank_ref, f32[1024,512]{1,0:T(8,128)S(1)} %pad_maximum_fusion.place_ref, ...), custom_call_target="tpu_custom_call" | custom-call | flops 6543114240 | bytes 20971520 | tf_op jit(solution)/shard_map/pallas_call | solution.py:1210
  173.3 1.8 slice.206.y_ref
  175.1 22.5 %shard_map.291 = (bf16[3,256,512]{2,1,0:T(8,128)(2,1)S(1)}, f32[3,4,4,256]{3,2,1,0:T(4,128)S(1)}) custom-call(bf16[3,256,512]{2,1,0:T(8,128)(2,1)S(1)} %get-tuple-element.68.q_ref, bf16[3,1040,512]{2,1,0:T(8,128)(2,1)S(1)} %get-tuple-element.69.k_ref, bf16[3,1040,512]{2,1,0:T(8,128)(2,1)S(1)} %get-tuple-element.70.v_ref), custom_call_target="tpu_custom_call" | custom-call | flops 6543114240 | bytes 7962624 | tf_op jit(solution)/shard_map/pallas_call | solution.py:284
  201.2 26.3 %shard_map.292 = (bf16[3,256,512]{2,1,0:T(8,128)(2,1)S(1)}, f32[3,256,512]{2,1,0:T(8,128)S(1)}, f32[512,5376]{1,0:T(8,128)}, f32[8,512]{1,0:T(8,128)S(1)}, f32[8,2048]{1,0:T(8,128)S(1)}, /*index=5*/f32[8,768]{1,0:T(8,128)S(1)}) custom-call(bf16[3,256,512]{2,1,0:T(8,128)(2,1)S(1)} %get-tuple-element.71.o_ref, f32[3,256,512]{2,1,0:T(8,128)S(1)} %slice.206.y_ref, ...), custom_call_target="tpu_custom_call" | custom-call | flops 25367150592 | bytes 31457280 | tf_op jit(solution)/shard_map/pallas_call | solution.py:1141
  231.5 1.9 copy-done.20
  237.3 42.6 %shard_map.293 = (bf16[3,256,512]{2,1,0:T(8,128)(2,1)S(1)}, bf16[3,1040,512]{2,1,0:T(8,128)(2,1)S(1)}, bf16[3,1040,512]{2,1,0:T(8,128)(2,1)S(1)}) custom-call(bf16[3,256,512]{2,1,0:T(8,128)(2,1)S(1)} %copy-done.23, bf16[3,1040,512]{2,1,0:T(8,128)(2,1)S(1)} %copy-done.18, bf16[3,1040,512]{2,1,0:T(8,128)(2,1)S(1)} %copy-done.20, ...), custom_call_target="tpu_custom_call" | custom-call | flops 16357785600 | bytes 15925248 | tf_op jit(solution)/shard_map/pallas_call | solution.py:309
  281.5 17.6 %shard_map.294 = (bf16[784,512]{1,0:T(8,128)(2,1)S(1)}, f32[512,1536]{1,0:T(8,128)S(1)}, f32[8,512]{1,0:T(8,128)S(1)}) custom-call(f32[3,1040,512]{2,1,0:T(8,128)} %get-tuple-element.72.y_ref, bf16[3,256,512]{2,1,0:T(8,128)(2,1)S(1)} %get-tuple-element.76.dq_ref, bf16[3,1040,512]{2,1,0:T(8,128)(2,1)S(1)} %get-tuple-element.77.dk_ref, ...), custom_call_target="tpu_custom_call" | custom-call | flops 19629342720 | bytes 25165824 | tf_op jit(solution)/shard_map/pallas_call | solution.py:1292
  299.1 28.9 %shard_map.295.de_ref.cls_ref = bf16[784,512]{1,0:T(8,128)(2,1)S(1)} custom-call(bf16[784,512]{1,0:T(8,128)(2,1)S(1)} %get-tuple-element.80.x_ref), custom_call_target="tpu_custom_call" | custom-call | bytes 40140800 | tf_op jit(solution)/shard_map/pallas_call | solution.py:653
  330.3 29.9 %shard_map.296 = (bf16[3,272,768]{2,1,0:T(8,128)(2,1)}, f32[3,272,768]{2,1,0:T(8,128)}, f32[768,1856]{1,0:T(8,128)}, f32[8,768]{1,0:T(8,128)}, f32[8,3072]{1,0:T(8,128)}, /*index=5*/f32[8,512]{1,0:T(8,128)}) custom-call(s32[1]{0:T(128)} %bitcast.place_ref, bf16[784,512]{1,0:T(8,128)(2,1)} %copy-done.9, bf16[784,512]{1,0:T(8,128)(2,1)} %copy-done.9, ...), custom_call_target="tpu_custom_call" | custom-call | flops 19733151744 | bytes 52428800 | tf_op jit(solution)/shard_map/pallas_call | solution.py:1512
  361.8 33.2 %shard_map.297 = (f32[768,768]{1,0:T(8,128)}, f32[8,768]{1,0:T(8,128)}) custom-call(s32[1]{0:T(128)} %bitcast.place_ref, bf16[3,256,768]{2,1,0:T(8,128)(2,1)} %bitcast.37, f32[3,272,768]{2,1,0:T(8,128)} %get-tuple-element.89.x_ref, bf16[3,272,2304]{2,1,0:T(8,128)(2,1)} %get-tuple-element.90.qkv_ref, f32[3,12,272]{2,1,0:T(8,128)} %get-tuple-element.91.lse_ref, ...), custom_call_target="tpu_custom_call" | custom-call | flops 15401484288 | bytes 20971520 | tf_op jit(solution)/shard_map/pallas_call | solution.py:1616
  419.1 2.7 copy-done.1
  421.8 92.7 %shard_map.298 = (bf16[4,96,1984]{2,1,0:T(8,128)(2,1)S(1)}, bf16[4,96,768]{2,1,0:T(8,128)(2,1)S(1)}, f32[8,8,384]{2,1,0:T(8,128)S(1)}, f32[64,1536]{1,0:T(8,128)S(1)}, f32[512,768]{1,0:T(8,128)S(1)}) custom-call(f32[768,1856]{1,0:T(8,128)S(1)} %copy-done.1, f32[768,768]{1,0:T(8,128)S(1)} %copy-done.4, f32[8,8,384]{2,1,0:T(8,128)S(1)} %reshape.78.small_ref, ...), custom_call_target="tpu_custom_call" | custom-call | bytes 209715200 | tf_op jit(solution)/shard_map/pallas_call | solution.py:971
  521.2 6.6 %multiply_subtract_fusion = (f32[512,768]{1,0:T(8,128)}, f32[512,768]{1,0:T(8,128)}, f32[512,768]{1,0:T(8,128)}) fusion(f32[512,768]{1,0:T(8,128)} %param.25, f32[512,768]{1,0:T(8,128)} %param.26, f32[512,768]{1,0:T(8,128)} %copy-done.7, f32[512,768]{1,0:T(8,128)} %param.27), kind=kLoop, calls=%fused_computation.11 | loop fusion | flops 5505024 | bytes 11010048 | tf_op jit(solution)/shard_map/sub | solution.py:1656
  527.9 2.1 copy-done.3
  530.0 6.5 %shard_map.299 = (f32[96,10496]{1,0:T(8,128)}, f32[96,10496]{1,0:T(8,128)}, f32[96,10496]{1,0:T(8,128)}) custom-call(f32[96,10496]{1,0:T(8,128)S(1)} %copy-done, f32[96,10496]{1,0:T(8,128)S(1)} %copy-done.2, f32[96,10496]{1,0:T(8,128)S(1)} %copy-done.3, bf16[4,96,1984]{2,1,0:T(8,128)(2,1)S(1)} %copy-done.6, bf16[4,96,768]{2,1,0:T(8,128)(2,1)S(1)} %copy-done.12), custom_call_target="tpu_custom_call" | custom-call | flops 20152320 | bytes 26198016 | tf_op jit(solution)/shard_map/pallas_call | solution.py:1695
  536.5 3.6 multiply_subtract_fusion.1
  (199 shorter events, 53.1 us)
Async XLA Ops:
  7.2 155.9 %all-gather.2.cloned.1.call-start = ((), (), s32[]{:S(2)}) async-start(), calls=%async_computation.1 | async-start | bytes 7077888 | tf_op jit(solution)/shard_map/all_gather | solution.py:1737
  9.6 320.6 %reduce-scatter.2.cloned.1.call-start = ((), (), s32[]{:S(2)}) async-start(), calls=%async_computation.2 | async-start | bytes 12386304 | tf_op jit(solution)/shard_map/reduce_scatter | solution.py:1803
  12.8 4.5 copy-start.43
  12.9 4.4 copy-start.45
  111.4 5.5 %copy-start.15 = (bf16[768,10496]{1,0:T(8,128)(2,1)}, bf16[768,10496]{1,0:T(8,128)(2,1)S(1)}, u32[]{:S(2)}) copy-start(bf16[768,10496]{1,0:T(8,128)(2,1)S(1)} %get-tuple-element.66.w_ref) | copy-start | bytes 48365572
  116.9 4.1 copy-start.16
  175.1 26.1 %copy-start.10 = (bf16[512,768]{1,0:T(8,128)(2,1)S(1)}, bf16[512,768]{1,0:T(8,128)(2,1)}, u32[]{:S(2)}) copy-start(bf16[512,768]{1,0:T(8,128)(2,1)} %convert_element_type.50.head_w) | copy-start | bytes 2359300
  201.0 26.4 %copy-start.24 = (bf16[3,256,512]{2,1,0:T(8,128)(2,1)}, bf16[3,256,512]{2,1,0:T(8,128)(2,1)S(1)}, u32[]{:S(2)}) copy-start(bf16[3,256,512]{2,1,0:T(8,128)(2,1)S(1)} %get-tuple-element.71.o_ref) | copy-start | bytes 2359300
  229.6 187.8 %all-reduce.9.cloned.1.call-start = ((), (), s32[]{:S(2)}) async-start(), calls=%async_computation.3 | async-start | bytes 2752512 | tf_op jit(solution)/shard_map/psum | solution.py:1811
  237.3 44.3 %copy-start.28 = (f32[3,256,512]{2,1,0:T(8,128)S(1)}, f32[3,256,512]{2,1,0:T(8,128)}, u32[]{:S(2)}) copy-start(f32[3,256,512]{2,1,0:T(8,128)} %copy-done.27) | copy-start | bytes 4718596
  361.8 33.2 %copy-start.53 = (f32[8,768]{1,0:T(8,128)S(1)}, f32[8,768]{1,0:T(8,128)}, u32[]{:S(2)}) copy-start(f32[8,768]{1,0:T(8,128)} %get-tuple-element.97) | copy-start | bytes 73732
  421.8 97.1 %copy-start.38 = (f32[3840]{0:T(1024)S(1)}, f32[3840]{0:T(1024)}, u32[]{:S(2)}) copy-start(f32[3840]{0:T(1024)} %param.28) | copy-start | bytes 46084
  421.8 97.1 %copy-start.51 = (f32[3840]{0:T(1024)S(1)}, f32[3840]{0:T(1024)}, u32[]{:S(2)}) copy-start(f32[3840]{0:T(1024)} %param.29) | copy-start | bytes 46084
  421.8 97.1 %copy-start.52 = (f32[3840]{0:T(1024)S(1)}, f32[3840]{0:T(1024)}, u32[]{:S(2)}) copy-start(f32[3840]{0:T(1024)} %param.30) | copy-start | bytes 46084
  421.8 97.8 %copy-start.39 = (f32[17408]{0:T(1024)S(1)}, f32[17408]{0:T(1024)}, u32[]{:S(2)}) copy-start(f32[17408]{0:T(1024)} %param.32) | copy-start | bytes 208900
  521.2 6.6 %copy-start = (f32[96,10496]{1,0:T(8,128)S(1)}, f32[96,10496]{1,0:T(8,128)}, u32[]{:S(2)}) copy-start(f32[96,10496]{1,0:T(8,128)} %w_ref.1) | copy-start | bytes 12091396
  521.2 6.6 %copy-start.2 = (f32[96,10496]{1,0:T(8,128)S(1)}, f32[96,10496]{1,0:T(8,128)}, u32[]{:S(2)}) copy-start(f32[96,10496]{1,0:T(8,128)} %m_ref.1) | copy-start | bytes 12091396
  521.2 6.6 %copy-start.6 = (bf16[4,96,1984]{2,1,0:T(8,128)(2,1)S(1)}, bf16[4,96,1984]{2,1,0:T(8,128)(2,1)}, u32[]{:S(2)}) copy-start(bf16[4,96,1984]{2,1,0:T(8,128)(2,1)} %copy-done.5) | copy-start | bytes 4571140
  521.2 6.7 %copy-start.12 = (bf16[4,96,768]{2,1,0:T(8,128)(2,1)S(1)}, bf16[4,96,768]{2,1,0:T(8,128)(2,1)}, u32[]{:S(2)}) copy-start(bf16[4,96,768]{2,1,0:T(8,128)(2,1)} %copy-done.11) | copy-start | bytes 1769476
  530.0 6.5 %copy-start.14 = (f32[64,1536]{1,0:T(8,128)S(1)}, f32[64,1536]{1,0:T(8,128)}, u32[]{:S(2)}) copy-start(f32[64,1536]{1,0:T(8,128)} %copy-done.13) | copy-start | bytes 1179652
  530.0 6.5 %copy-start.31 = (f32[64,6144]{1,0:T(8,128)S(1)}, f32[64,6144]{1,0:T(8,128)}, u32[]{:S(2)}) copy-start(f32[64,6144]{1,0:T(8,128)} %param.22) | copy-start | bytes 4718596
  530.0 6.5 %slice-start = ((f32[64,5376]{1,0:T(8,128)}), f32[64,4608]{1,0:T(8,128)S(1)}, s32[]{:S(2)}) async-start(f32[64,5376]{1,0:T(8,128)} %all-reduce.9.cloned.1.call-done), calls=%async_computation.4 | async-start | bytes 2359296 | tf_op jit(solution)/shard_map/slice | solution.py:1855
  530.0 6.5 %copy-start.32 = (f32[64,6144]{1,0:T(8,128)S(1)}, f32[64,6144]{1,0:T(8,128)}, u32[]{:S(2)}) copy-start(f32[64,6144]{1,0:T(8,128)} %param.23) | copy-start | bytes 4718596
  530.0 6.5 %copy-start.33 = (f32[64,6144]{1,0:T(8,128)S(1)}, f32[64,6144]{1,0:T(8,128)}, u32[]{:S(2)}) copy-start(f32[64,6144]{1,0:T(8,128)} %param.24) | copy-start | bytes 4718596
  (35 other events, 63.4 us)
Sparse Core Ops, SparseCore 0:
  10.5 72.5 all-gather.1
  229.7 82.1 reduce-scatter.1
  330.4 63.3 all-reduce.8

commit v5 on v4

--- a/solution.py
+++ b/solution.py
@@ -262,8 +262,8 @@
     dv_ref[0, :main], dv_ref[0, main:] = dv
 
 
-VMEM_LIMIT = 32 * 1024 * 1024
-KERNEL_LIMIT = 58 * 1024 * 1024
+VMEM_LIMIT = 60 * 1024 * 1024
+COPY_LIMIT = 32 * 1024 * 1024
 
 
 def attend_specs(q_rows, k_rows, heads):
@@ -423,16 +423,25 @@
             copy(1, at).wait_send()
 
 
-GATHER_CHUNKS = 6
+GATHER_WAYS = ("shared",) * 4 + ("within", "swapped")
+GATHER_CHUNKS = len(GATHER_WAYS)
 KEPT_CHUNKS = 8
+PLACE_ROWS = 128
 
 
 def start_kernel(
     lines,
     w_ref,
     x_ref,
+    kept_ids,
+    patch_ids,
+    wide_ref,
+    narrow_ref,
+    bias_ref,
     full_ref,
     o_ref,
+    wide_out,
+    narrow_out,
     from_left,
     from_right,
     to_left,
@@ -451,8 +460,8 @@
     odd = lax.rem(place, 2)
     by_x = 2 - 4 * at_x
     by_y = 4 - 8 * at_y
-    ahead = own + (1 - odd) * by_x + odd * by_y
-    aside = own + odd * by_x + (1 - odd) * by_y
+    first = own + (1 - odd) * by_x + odd * by_y
+    second = own + odd * by_x + (1 - odd) * by_y
     across = own + by_x + by_y
     partner = own + 1 - 2 * core
     over = place + 1 - 2 * odd
@@ -466,7 +475,7 @@
     def greet(device):
         pl.semaphore_signal(barrier, inc=1, device_id=device, device_id_type=MESH)
 
-    for device in (ahead, aside, partner):
+    for device in (first, second, partner):
         greet({"fsdp": device})
     pl.when(has_left)(lambda: greet({"seq": place - 1}))
     pl.when(has_right)(lambda: greet({"seq": place + 1}))
@@ -489,20 +498,30 @@
     def own_rows(at):
         return w_ref.at[pl.ds(at * rows, rows)]
 
+    def ahead(at):
+        return second if GATHER_WAYS[at] == "swapped" else first
+
+    def aside(at):
+        return first if GATHER_WAYS[at] == "swapped" else second
+
     def ahead_copy(at):
         target = full_ref.at[span_of(own, at)]
-        return copy_of(own_rows(at), target, ring_sems, (0, at), {"fsdp": ahead})
-
-    def aside_copy(at):
-        part = full_ref.at[span_of(ahead, at)]
-        return copy_of(part, part, ring_sems, (1, at), {"fsdp": aside})
-
-    def over_copy(at):
-        part = full_ref.at[span_of(ahead, at)]
-        return copy_of(part, part, ring_sems, (2, at), {"seq": over})
+        return copy_of(own_rows(at), target, ring_sems, (0, at), {"fsdp": ahead(at)})
+
+    def relay_copy(at):
+        part = full_ref.at[span_of(ahead(at), at)]
+        return copy_of(part, part, ring_sems, (1, at), {"fsdp": aside(at)})
+
+    def third_copy(at):
+        if GATHER_WAYS[at] == "shared":
+            part = full_ref.at[span_of(ahead(at), at)]
+            return copy_of(part, part, ring_sems, (2, at), {"seq": over})
+        target = full_ref.at[span_of(own, at)]
+        return copy_of(own_rows(at), target, ring_sems, (2, at), {"fsdp": aside(at)})
 
     def pair_copy(kind, at):
-        target = full_ref.at[span_of((own, ahead, across, aside)[kind], at)]
+        owner = (own, ahead(at), across, aside(at))[kind]
+        target = full_ref.at[span_of(owner, at)]
         source = own_rows(at) if kind == 0 else target
         return copy_of(source, target, pair_sems, (kind, at), {"fsdp": partner})
 
@@ -513,8 +532,16 @@
 
     def send_own(at):
         ahead_copy(at).start()
+        if GATHER_WAYS[at] != "shared":
+            third_copy(at).start()
         pair_copy(0, at).start()
         keep_copy(at).start()
+
+    def receive_rest(at):
+        relay_copy(at).wait_recv()
+        pair_copy(2, at).start()
+        third_copy(at).wait_recv()
+        pair_copy(3, at).start()
 
     def kept_span(at):
         return pl.ds(pl.multiple_of(at * kept_rows, 16), kept_rows)
@@ -558,29 +585,43 @@
                 to_left[span] = x_ref[span] + from_right[span]
                 kept_copy(1, from_last).start()
 
+    def write_positions(at):
+        span = slice(at * PLACE_ROWS, (at + 1) * PLACE_ROWS)
+        for ids, scale, out, bias in (
+            (kept_ids, wide_ref, wide_out, bias_ref),
+            (patch_ids, narrow_ref, narrow_out, None),
+        ):
+            if span.start < ids.shape[0]:
+                half = scale.shape[1]
+                angles = (ids[span, :].astype(jnp.float32) + 1.0) * scale[...]
+                for part, lanes in (
+                    (jnp.sin(angles), slice(0, half)),
+                    (jnp.cos(angles), slice(half, 2 * half)),
+                ):
+                    out[span, lanes] = part if bias is None else part + bias[:, lanes]
+
     send_own(0)
     send_own(1)
     kept_steps = list(range(KEPT_CHUNKS + lines - 1))
+    place_steps = list(range(max(kept_ids.shape[0], patch_ids.shape[0]) // PLACE_ROWS))
     for at in range(GATHER_CHUNKS):
+        for _ in range(2):
+            if kept_steps:
+                kept_step(kept_steps.pop(0))
+        if place_steps:
+            write_positions(place_steps.pop(0))
         ahead_copy(at).wait_recv()
-        aside_copy(at).start()
-        over_copy(at).start()
+        relay_copy(at).start()
+        if GATHER_WAYS[at] == "shared":
+            third_copy(at).start()
         pair_copy(1, at).start()
         if at + 2 < GATHER_CHUNKS:
             send_own(at + 2)
-        for _ in range(2):
-            if kept_steps:
-                kept_step(kept_steps.pop(0))
         if at:
-            aside_copy(at - 1).wait_recv()
-            pair_copy(2, at - 1).start()
-            over_copy(at - 1).wait_recv()
-            pair_copy(3, at - 1).start()
-    last = GATHER_CHUNKS - 1
-    aside_copy(last).wait_recv()
-    pair_copy(2, last).start()
-    over_copy(last).wait_recv()
-    pair_copy(3, last).start()
+            receive_rest(at - 1)
+    for step in place_steps:
+        write_positions(step)
+    receive_rest(GATHER_CHUNKS - 1)
     for step in kept_steps:
         kept_step(step)
 
@@ -606,30 +647,42 @@
     for at in range(GATHER_CHUNKS):
         keep_copy(at).wait()
         ahead_copy(at).wait_send()
-        aside_copy(at).wait_send()
-        over_copy(at).wait_send()
+        relay_copy(at).wait_send()
+        third_copy(at).wait_send()
         for kind in range(4):
             pair_copy(kind, at).wait()
 
 
-def start_gather(own_w, own_kept, collective_id):
+def frequencies(width_dim):
+    halves = width_dim // 2
+    return 10000.0 ** (-jnp.arange(halves, dtype=jnp.float32) / halves)
+
+
+def start_gather(own_w, own_kept, kept_ids, patch_ids, bias, collective_id):
     plane = lax.axis_size("fsdp")
     lines = lax.axis_size("seq")
     block, width = own_w.shape
     if plane != PLANE or block % (16 * GATHER_CHUNKS) or lines % 2:
-        return lax.all_gather(own_w, "fsdp", axis=0, tiled=True), line_sum(
-            own_kept, KEPT_CHUNKS, collective_id
+        return (
+            lax.all_gather(own_w, "fsdp", axis=0, tiled=True),
+            line_sum(own_kept, KEPT_CHUNKS, collective_id),
+            positions(kept_ids, D_E) + bias,
+            positions(patch_ids, D_D),
         )
     buffer = pltpu.VMEM(own_kept.shape, own_kept.dtype)
     dma = pltpu.SemaphoreType.DMA
+    vmem = pl.BlockSpec(memory_space=pltpu.VMEM)
+    anywhere = pl.BlockSpec(memory_space=pl.ANY)
     return pl.pallas_call(
         partial(start_kernel, lines),
         out_shape=[
             jax.ShapeDtypeStruct((PLANE * block, width), own_w.dtype),
             jax.ShapeDtypeStruct(own_kept.shape, own_kept.dtype),
+            jax.ShapeDtypeStruct((kept_ids.shape[0], D_E), jnp.float32),
+            jax.ShapeDtypeStruct((patch_ids.shape[0], D_D), jnp.float32),
         ],
-        in_specs=[pl.BlockSpec(memory_space=pl.ANY), pl.BlockSpec(memory_space=pltpu.VMEM)],
-        out_specs=[pl.BlockSpec(memory_space=pl.ANY), pl.BlockSpec(memory_space=pltpu.VMEM)],
+        in_specs=[anywhere] + [vmem] * 6,
+        out_specs=[anywhere] + [vmem] * 3,
         scratch_shapes=[buffer] * 4
         + [
             dma((GATHER_CHUNKS,)),
@@ -639,12 +692,20 @@
             dma((2, KEPT_CHUNKS)),
         ],
         compiler_params=pltpu.CompilerParams(
-            collective_id=collective_id, has_side_effects=True, vmem_limit_bytes=VMEM_LIMIT
+            collective_id=collective_id, has_side_effects=True, vmem_limit_bytes=COPY_LIMIT
         ),
         cost_estimate=pl.CostEstimate(
             flops=0, bytes_accessed=200 * 1024 * 1024, transcendentals=0
         ),
-    )(own_w, own_kept)
+    )(
+        own_w,
+        own_kept,
+        kept_ids[:, None],
+        patch_ids[:, None],
+        frequencies(D_E)[None],
+        frequencies(D_D)[None],
+        bias[None],
+    )
 
 
 def line_sum(block, chunks, collective_id):
@@ -658,7 +719,7 @@
         scratch_shapes=[buffer] * 4
         + [pltpu.SemaphoreType.DMA((2, chunks)), pltpu.SemaphoreType.DMA((2, chunks))],
         compiler_params=pltpu.CompilerParams(
-            collective_id=collective_id, has_side_effects=True, vmem_limit_bytes=VMEM_LIMIT
+            collective_id=collective_id, has_side_effects=True, vmem_limit_bytes=COPY_LIMIT
         ),
         cost_estimate=pl.CostEstimate(
             flops=0, bytes_accessed=100 * block.size, transcendentals=0
@@ -666,349 +727,327 @@
     )(block)
 
 
-SMALL_BLOCK = (8, 384)
+SMALL_BLOCK = (8, 768)
 PLANE = 8
 
 
+def send(source, target, sems, at, device):
+    return pltpu.make_async_remote_copy(
+        src_ref=source,
+        dst_ref=target,
+        send_sem=sems.at[(0,) + at],
+        recv_sem=sems.at[(1,) + at],
+        device_id=device,
+        device_id_type=MESH,
+    )
+
+
+def greet_all():
+    own, place = lax.axis_index("fsdp"), lax.axis_index("seq")
+    line = lax.axis_size("seq")
+    barrier = pltpu.get_barrier_semaphore()
+    for step in range(1, PLANE):
+        device = {"fsdp": lax.rem(own + step, PLANE)}
+        pl.semaphore_signal(barrier, inc=1, device_id=device, device_id_type=MESH)
+    for step in range(1, line):
+        device = {"seq": lax.rem(place + step, line)}
+        pl.semaphore_signal(barrier, inc=1, device_id=device, device_id_type=MESH)
+    pl.semaphore_wait(barrier, PLANE - 1 + line - 1)
+
+
+class PlaneSum:
+    def __init__(self, grad, pair_in, out, into, pair_sems, plane_sems):
+        self.grad, self.pair_in, self.out, self.into = grad, pair_in, out, into
+        self.pair_sems, self.plane_sems = pair_sems, plane_sems
+        self.own = lax.axis_index("fsdp")
+        self.core = lax.rem(self.own, 2)
+        self.chip = lax.div(self.own, 2)
+        self.rows = grad.shape[0] // PLANE
+
+    @staticmethod
+    def scratch(rows, width, kind):
+        dma = pltpu.SemaphoreType.DMA
+        return [
+            pltpu.VMEM((4, rows, width), jnp.float32),
+            pltpu.VMEM((3, rows, width), kind),
+            pltpu.VMEM((3, rows, width), kind),
+            dma((2, 4)),
+            dma((2, 3)),
+        ]
+
+    def rows_of(self, owner):
+        return pl.ds(pl.multiple_of(owner * self.rows, 16), self.rows)
+
+    def target(self, other):
+        return lax.rem(self.chip + other, 4)
+
+    def pair_copy(self, other):
+        owner = 2 * self.target(other) + 1 - self.core
+        partner = self.own + 1 - 2 * self.core
+        return send(
+            self.grad.at[self.rows_of(owner)],
+            self.pair_in.at[other],
+            self.pair_sems,
+            (other,),
+            {"fsdp": partner},
+        )
+
+    def plane_copy(self, other):
+        owner = 2 * self.target(other) + self.core
+        at = other - 1
+        return send(self.out.at[at], self.into.at[at], self.plane_sems, (at,), {"fsdp": owner})
+
+    def start(self):
+        for other in (3, 1, 2, 0):
+            self.pair_copy(other).start()
+
+    def pass_on(self):
+        for other in (3, 1, 2):
+            self.pair_copy(other).wait_recv()
+            owner = 2 * self.target(other) + self.core
+            both = self.grad[self.rows_of(owner)] + self.pair_in[other]
+            self.out[other - 1] = both.astype(self.out.dtype)
+            self.plane_copy(other).start()
+
+    def total(self):
+        self.pair_copy(0).wait_recv()
+        total = self.grad[self.rows_of(self.own)] + self.pair_in[0]
+        for other in (1, 2, 3):
+            self.plane_copy(other).wait_recv()
+            total = total + self.into[other - 1].astype(jnp.float32)
+        return total
+
+    def finish(self):
+        for other in range(4):
+            self.pair_copy(other).wait_send()
+            if other:
+                self.plane_copy(other).wait_send()
+
+
+class LineGather:
+    def __init__(self, slots, sems):
+        self.slots, self.sems = slots, sems
+        self.place = lax.axis_index("seq")
+        self.line = lax.axis_size("seq")
+
+    def copy(self, step):
+        part = self.slots.at[self.place]
+        to = lax.rem(self.place + step, self.line)
+        return send(part, part, self.sems, (step - 1,), {"seq": to})
+
+    def start(self, value):
+        self.slots[self.place] = value
+        for step in range(1, self.line):
+            self.copy(step).start()
+
+    def wait_recv(self):
+        for step in range(1, self.line):
+            self.copy(step).wait_recv()
+
+    def finish(self):
+        for step in range(1, self.line):
+            self.copy(step).wait_send()
+
+
+class LineSum:
+    def __init__(self, block, parts, result, split_sems, line_sems):
+        self.block, self.parts, self.result = block, parts, result
+        self.split_sems, self.line_sems = split_sems, line_sems
+        self.place = lax.axis_index("seq")
+        self.line = lax.axis_size("seq")
+        self.rows = block.shape[0] // parts.shape[0]
+
+    @staticmethod
+    def scratch(rows, width, line):
+        dma = pltpu.SemaphoreType.DMA
+        return [
+            pltpu.VMEM((rows, width), jnp.float32),
+            pltpu.VMEM((line, rows // line, width), jnp.float32),
+            pltpu.VMEM((rows, width), jnp.float32),
+            dma((2, line - 1)),
+            dma((2, line - 1)),
+        ]
+
+    def quarter(self, at):
+        return pl.ds(pl.multiple_of(at * self.rows, 8), self.rows)
+
+    def split_copy(self, step):
+        to = lax.rem(self.place + step, self.line)
+        source = self.block.at[self.quarter(to)]
+        return send(source, self.parts.at[self.place], self.split_sems, (step - 1,), {"seq": to})
+
+    def line_copy(self, step):
+        to = lax.rem(self.place + step, self.line)
+        part = self.result.at[self.quarter(self.place)]
+        return send(part, part, self.line_sems, (step - 1,), {"seq": to})
+
+    def start(self, value):
+        self.block[...] = value
+        self.parts[self.place] = self.block[self.quarter(self.place)]
+        for step in range(1, self.line):
+            self.split_copy(step).start()
+
+    def spread(self):
+        for step in range(1, self.line):
+            self.split_copy(step).wait_recv()
+        total = self.parts[0]
+        for at in range(1, self.parts.shape[0]):
+            total = total + self.parts[at]
+        self.result[self.quarter(self.place)] = total
+        for step in range(1, self.line):
+            self.line_copy(step).start()
+
+    def finish(self):
+        for step in range(1, self.line):
+            self.line_copy(step).wait()
+            self.split_copy(step).wait_send()
+
+
 def exchange_kernel(
-    table,
-    extra,
-    g_early,
-    g_late,
+    g_ref,
     small_ref,
-    dec_ref,
     head_ref,
-    out_early,
-    out_late,
+    out_ref,
     small_out,
-    dec_out,
     head_out,
-    pair_early,
-    pair_late,
-    send_early,
-    send_late,
-    recv_early,
-    recv_late,
+    pair_in,
+    plane_out,
+    plane_in,
+    pair_sems,
+    plane_sems,
     small_in,
     small_line,
-    dec_pair,
-    dec_send,
-    dec_recv,
-    dec_sum,
-    dec_line,
-    dec_pair_sems,
-    dec_plane_sems,
-    dec_split_sems,
-    dec_line_sems,
-    head_sems,
-    pair_sems,
-    plane_sems,
     line_sems,
     small_plane_sems,
     small_line_sems,
     small_out_sems,
+    head_sems,
+    head_pair_sems,
 ):
     own = lax.axis_index("fsdp")
-    place = lax.axis_index("seq")
-    line = lax.axis_size("seq")
     core = lax.rem(own, 2)
+    partner = own + 1 - 2 * core
     chip = lax.div(own, 2)
-    partner = own + 1 - 2 * core
-    grads = (g_early, g_late)
-    pair_ins = (pair_early, pair_late)
-    sends = (send_early, send_late)
-    recvs = (recv_early, recv_late)
-    outs = (out_early, out_late)
-    block = g_early.shape[0] // PLANE
-    order = range(len(table))
-
-    def plane_peer(step):
+    greet_all()
+    plane = PlaneSum(g_ref, pair_in, plane_out, plane_in, pair_sems, plane_sems)
+    line = LineGather(out_ref, line_sems)
+    small_all = LineGather(small_line, small_line_sems)
+
+    def peer(step):
         return lax.rem(own + step, PLANE)
-
-    def line_peer(step):
-        return lax.rem(place + step, line)
-
-    barrier = pltpu.get_barrier_semaphore()
-    for step in range(1, PLANE):
-        pl.semaphore_signal(
-            barrier, inc=1, device_id={"fsdp": plane_peer(step)}, device_id_type=MESH
-        )
-    for step in range(1, line):
-        pl.semaphore_signal(
-            barrier, inc=1, device_id={"seq": line_peer(step)}, device_id_type=MESH
-        )
-    pl.semaphore_wait(barrier, PLANE - 1 + line - 1)
-
-    def send(source, target, sems, at, device):
-        return pltpu.make_async_remote_copy(
-            src_ref=source,
-            dst_ref=target,
-            send_sem=sems.at[(0,) + at],
-            recv_sem=sems.at[(1,) + at],
-            device_id=device,
-            device_id_type=MESH,
-        )
-
-    def span_of(at):
-        return pl.ds(table[at][1], table[at][2])
-
-    def owned_rows(owner, at):
-        start, rows = table[at][1:]
-        return pl.ds(pl.multiple_of(owner * block + start, 16), rows)
-
-    def pair_copy(other, at):
-        part = table[at][0]
-        target = lax.rem(chip + other, 4)
-        return send(
-            grads[part].at[owned_rows(2 * target + 1 - core, at)],
-            pair_ins[part].at[other, span_of(at)],
-            pair_sems,
-            (other, at),
-            {"fsdp": partner},
-        )
-
-    def plane_copy(other, at):
-        part = table[at][0]
-        target = lax.rem(chip + other, 4)
-        return send(
-            sends[part].at[other - 1, span_of(at)],
-            recvs[part].at[other - 1, span_of(at)],
-            plane_sems,
-            (other - 1, at),
-            {"fsdp": 2 * target + core},
-        )
-
-    def line_copy(step, at):
-        part = outs[table[at][0]].at[place, span_of(at)]
-        return send(part, part, line_sems, (step - 1, at), {"seq": line_peer(step)})
 
     def small_plane_copy(step):
         return send(
-            small_ref.at[plane_peer(step)],
+            small_ref.at[peer(step)],
             small_in.at[step - 1],
             small_plane_sems,
             (step - 1,),
-            {"fsdp": plane_peer(step)},
+            {"fsdp": peer(step)},
         )
-
-    def small_line_copy(step):
-        part = small_line.at[place]
-        return send(part, part, small_line_sems, (step - 1,), {"seq": line_peer(step)})
 
     def small_out_copy(step):
         part = small_out.at[own]
-        return send(part, part, small_out_sems, (step - 1,), {"fsdp": plane_peer(step)})
-
-    dec_rows = dec_ref.shape[0] // PLANE
-    dec_part = dec_rows // line
-
-    def dec_span(owner):
-        return pl.ds(pl.multiple_of(owner * dec_rows, 16), dec_rows)
-
-    def dec_pair_copy(other):
-        target = lax.rem(chip + other, 4)
+        return send(part, part, small_out_sems, (step - 1,), {"fsdp": peer(step)})
+
+    head_rows = head_ref.shape[0]
+
+    def head_span(owner):
+        return pl.ds(pl.multiple_of(owner * head_rows, 16), head_rows)
+
+    def head_copy(other):
+        to = 2 * lax.rem(chip + other, 4) + core
         return send(
-            dec_ref.at[dec_span(2 * target + 1 - core)],
-            dec_pair.at[other],
-            dec_pair_sems,
-            (other,),
-            {"fsdp": partner},
+            head_ref, head_out.at[head_span(own)], head_sems, (other - 1,), {"fsdp": to}
         )
 
-    def dec_plane_copy(other):
-        target = lax.rem(chip + other, 4)
-        return send(
-            dec_send.at[other - 1],
-            dec_recv.at[other - 1],
-            dec_plane_sems,
-            (other - 1,),
-            {"fsdp": 2 * target + core},
-        )
-
-    def quarter_of(at):
-        return pl.ds(pl.multiple_of(at * dec_part, 16), dec_part)
-
-    def dec_split_copy(step):
-        to = line_peer(step)
-        return send(
-            dec_sum.at[quarter_of(to)],
-            dec_line.at[place],
-            dec_split_sems,
-            (step - 1,),
-            {"seq": to},
-        )
-
-    def dec_line_copy(step):
-        part = dec_out.at[quarter_of(place)]
-        return send(part, part, dec_line_sems, (step - 1,), {"seq": line_peer(step)})
-
-    head_rows = head_ref.shape[0]
-
-    def head_copy(step):
-        target = head_out.at[pl.ds(pl.multiple_of(own * head_rows, 16), head_rows)]
-        return send(head_ref, target, head_sems, (step - 1,), {"fsdp": plane_peer(step)})
-
-    for other in (1, 2, 3, 0):
-        dec_pair_copy(other).start()
-    for at in order:
-        for other in (1, 2, 3, 0):
-            pair_copy(other, at).start()
-        if at == 0:
-            for step in range(1, PLANE):
-                small_plane_copy(step).start()
-    for other in (1, 2, 3, 0):
-        dec_pair_copy(other).wait_recv()
-        if other:
-            target = lax.rem(chip + other, 4)
-            dec_send[other - 1] = dec_ref[dec_span(2 * target + core)] + dec_pair[other]
-            dec_plane_copy(other).start()
-    for at in order:
-        part = table[at][0]
-        for other in (1, 2, 3, 0):
-            pair_copy(other, at).wait_recv()
-            if other:
-                target = lax.rem(chip + other, 4)
-                mine = grads[part][owned_rows(2 * target + core, at)]
-                sends[part][other - 1, span_of(at)] = low(mine + pair_ins[part][other, span_of(at)])
-                plane_copy(other, at).start()
+    def head_pair_copy(other):
+        span = head_span(2 * lax.rem(chip + 4 - other, 4) + core)
+        source = head_out.at[span] if other else head_ref
+        return send(source, head_out.at[span], head_pair_sems, (other,), {"fsdp": partner})
+
+    plane.start()
+    for step in range(1, PLANE):
+        small_plane_copy(step).start()
+    plane.pass_on()
     for step in range(1, PLANE):
         small_plane_copy(step).wait_recv()
     total = small_ref[own]
     for step in range(1, PLANE):
         total = total + small_in[step - 1]
-    small_line[place] = total
-    for step in range(1, line):
-        small_line_copy(step).start()
-    total = dec_ref[dec_span(own)] + dec_pair[0]
-    for other in (1, 2, 3):
-        dec_plane_copy(other).wait_recv()
-        total = total + dec_recv[other - 1]
-    dec_sum[...] = total
-    for step in range(1, line):
-        dec_split_copy(step).start()
-    for step in range(1, PLANE):
-        head_copy(step).start()
-    head_out[pl.ds(pl.multiple_of(own * head_rows, 16), head_rows)] = head_ref[...]
-    for at in order:
-        part = table[at][0]
-        total = grads[part][owned_rows(own, at)] + pair_ins[part][0, span_of(at)]
-        for other in (1, 2, 3):
-            plane_copy(other, at).wait_recv()
-            total = total + recvs[part][other - 1, span_of(at)].astype(jnp.float32)
-        rounded = low(total)
-        if part == 0:
-            rest = total[:, -extra:] - rounded[:, -extra:].astype(jnp.float32)
-            rounded = jnp.concatenate([rounded, low(rest)], axis=1)
-        outs[part][place, span_of(at)] = rounded
-        for step in range(1, line):
-            line_copy(step, at).start()
-        if at == 0:
-            dec_line[place] = dec_sum[quarter_of(place)]
-            for step in range(1, line):
-                dec_split_copy(step).wait_recv()
-            total = dec_line[0]
-            for other in range(1, dec_line.shape[0]):
-                total = total + dec_line[other]
-            dec_out[quarter_of(place)] = total
-            for step in range(1, line):
-                dec_line_copy(step).start()
-    for step in range(1, line):
-        small_line_copy(step).wait_recv()
+    small_all.start(total)
+    for other in (3, 1, 2):
+        head_copy(other).start()
+    head_pair_copy(0).start()
+    head_out[head_span(own)] = head_ref[...]
+    line.start(low(plane.total()))
+    small_all.wait_recv()
     total = small_line[0]
     for at in range(1, small_line.shape[0]):
         total = total + small_line[at]
     small_out[own] = total
     for step in range(1, PLANE):
         small_out_copy(step).start()
+    for other in (1, 2, 3):
+        head_copy(other).wait_recv()
+        head_pair_copy(other).start()
+    line.wait_recv()
     for step in range(1, PLANE):
         small_out_copy(step).wait()
         small_plane_copy(step).wait_send()
-        head_copy(step).wait()
     for other in range(4):
-        dec_pair_copy(other).wait_send()
+        head_pair_copy(other).wait()
         if other:
-            dec_plane_copy(other).wait_send()
-    for step in range(1, line):
-        dec_split_copy(step).wait_send()
-        dec_line_copy(step).wait()
-        small_line_copy(step).wait_send()
-        for at in order:
-            line_copy(step, at).wait()
-    for at in order:
-        for other in range(4):
-            pair_copy(other, at).wait_send()
-            if other:
-                plane_copy(other, at).wait_send()
-
-
-def exchange(early, late, small, dec, head_own, line, extra, collective_id):
-    plane = lax.axis_size("fsdp")
-    total = early.shape[0]
-    dec_rows = dec.shape[0] // plane
-    if plane != PLANE or total % (PLANE * 48) or dec_rows % (16 * line):
-        results = []
-        for part, rest in ((early, extra), (late, 0)):
-            own = lax.psum_scatter(part, "fsdp", scatter_dimension=0, tiled=True)
-            rounded = low(own)
-            if rest:
-                left = own[:, -rest:] - rounded[:, -rest:].astype(jnp.float32)
-                rounded = jnp.concatenate([rounded, low(left)], axis=1)
-            results.append(lax.all_gather(rounded, "seq", axis=0, tiled=False))
-        dec_sum = lax.psum(
-            lax.psum_scatter(dec, "fsdp", scatter_dimension=0, tiled=True), "seq"
+            head_copy(other).wait_send()
+    plane.finish()
+    line.finish()
+    small_all.finish()
+
+
+def plane_fits(rows):
+    line = lax.axis_size("seq")
+    return lax.axis_size("fsdp") == PLANE and rows % (PLANE * 16) == 0 and line == 4
+
+
+def exchange(late, small, head_own, line, collective_id):
+    if not plane_fits(late.shape[0]):
+        own = lax.psum_scatter(late, "fsdp", scatter_dimension=0, tiled=True)
+        return (
+            lax.all_gather(low(own), "seq", axis=0, tiled=False),
+            lax.psum(small, ("fsdp", "seq")),
+            lax.all_gather(head_own, "fsdp", axis=0, tiled=True),
         )
-        head_all = lax.all_gather(head_own, "fsdp", axis=0, tiled=True)
-        return results[0], results[1], lax.psum(small, ("fsdp", "seq")), dec_sum, head_all
-    block = total // PLANE
-    third = block // 3
-    table = tuple((0, at * third, third) for at in range(3)) + ((1, 0, block),)
-    widths = (early.shape[1], late.shape[1])
-    padded = PLANE * SMALL_BLOCK[0] * SMALL_BLOCK[1]
-    blocks = jnp.pad(small, (0, padded - small.shape[0])).reshape((PLANE,) + SMALL_BLOCK)
+    rows, width = late.shape[0] // PLANE, late.shape[1]
+    blocks = small.reshape((PLANE,) + SMALL_BLOCK)
     dma = pltpu.SemaphoreType.DMA
-    low_type, f32 = jnp.bfloat16, jnp.float32
-    dec_cols = dec.shape[1]
-    first, second, summed, dec_sum, head_all = pl.pallas_call(
-        partial(exchange_kernel, table, extra),
+    vmem = pl.BlockSpec(memory_space=pltpu.VMEM)
+    gathered, summed, head_all = pl.pallas_call(
+        exchange_kernel,
         out_shape=[
-            jax.ShapeDtypeStruct((line, block, widths[0] + extra), low_type),
-            jax.ShapeDtypeStruct((line, block, widths[1]), low_type),
-            jax.ShapeDtypeStruct(blocks.shape, f32),
-            jax.ShapeDtypeStruct((dec_rows, dec_cols), f32),
-            jax.ShapeDtypeStruct((PLANE * head_own.shape[0], head_own.shape[1]), f32),
+            jax.ShapeDtypeStruct((line, rows, width), jnp.bfloat16),
+            jax.ShapeDtypeStruct(blocks.shape, jnp.float32),
+            jax.ShapeDtypeStruct((PLANE * head_own.shape[0], head_own.shape[1]), jnp.float32),
         ],
-        in_specs=[pl.BlockSpec(memory_space=pltpu.VMEM)] * 5,
-        out_specs=[pl.BlockSpec(memory_space=pltpu.VMEM)] * 5,
-        scratch_shapes=[pltpu.VMEM((4, block, width), f32) for width in widths]
-        + [pltpu.VMEM((3, block, width), low_type) for width in widths * 2]
+        in_specs=[vmem] * 3,
+        out_specs=[vmem] * 3,
+        scratch_shapes=PlaneSum.scratch(rows, width, jnp.bfloat16)
         + [
-            pltpu.VMEM((PLANE - 1,) + SMALL_BLOCK, f32),
-            pltpu.VMEM((line,) + SMALL_BLOCK, f32),
-            pltpu.VMEM((4, dec_rows, dec_cols), f32),
-            pltpu.VMEM((3, dec_rows, dec_cols), f32),
-            pltpu.VMEM((3, dec_rows, dec_cols), f32),
-            pltpu.VMEM((dec_rows, dec_cols), f32),
-            pltpu.VMEM((line, dec_rows // line, dec_cols), f32),
-            dma((2, 4)),
-            dma((2, 3)),
+            pltpu.VMEM((PLANE - 1,) + SMALL_BLOCK, jnp.float32),
+            pltpu.VMEM((line,) + SMALL_BLOCK, jnp.float32),
             dma((2, line - 1)),
-            dma((2, line - 1)),
-            dma((2, PLANE - 1)),
-            dma((2, 4, len(table))),
-            dma((2, 3, len(table))),
-            dma((2, line - 1, len(table))),
             dma((2, PLANE - 1)),
             dma((2, line - 1)),
             dma((2, PLANE - 1)),
+            dma((2, 3)),
+            dma((2, 4)),
         ],
         compiler_params=pltpu.CompilerParams(
-            collective_id=collective_id, has_side_effects=True, vmem_limit_bytes=VMEM_LIMIT
+            collective_id=collective_id, has_side_effects=True, vmem_limit_bytes=COPY_LIMIT
         ),
         cost_estimate=pl.CostEstimate(
-            flops=0, bytes_accessed=200 * 1024 * 1024, transcendentals=0
+            flops=0, bytes_accessed=100 * 1024 * 1024, transcendentals=0
         ),
-    )(early, late, blocks, dec, head_own)
-    return first, second, summed.reshape(-1), dec_sum, head_all
+    )(late, blocks, head_own)
+    return gathered, summed.reshape(small.shape), head_all
 
 
 def gelu_parts(hidden):
@@ -1064,12 +1103,10 @@
     dmid_ref,
     grad_ref,
     vec_grad,
-    bu_grad,
-    bh_grad,
     slope_ref,
     act_ref,
 ):
-    clear_first((grad_ref, vec_grad, bu_grad, bh_grad))
+    clear_first((grad_ref, vec_grad))
     bo, gain2, shift2, bd, gain3, shift3 = (vec_ref[i : i + 1, :] for i in range(6))
     attended = o_ref[0]
     middle = y_ref[0] + dot_f32(attended, out_w[...], NN) + bo
@@ -1095,8 +1132,8 @@
     error = (predicted - target) * masked
     pred_grad = error * grad_scale
     pred_low = low(pred_grad)
-    bh_grad[0:1, :] += column_sum(pred_grad)
-    bh_grad[1:2, :] += column_sum(error * error)
+    vec_grad[6:7, :] += column_sum(pred_grad)
+    vec_grad[7:8, :] += column_sum(error * error)
     o_span, u_span = D_D, D_D + FF_D
     h_span = D_D + 2 * FF_D
     grad_ref[:, h_span:] += dot_f32(third, pred_low, TN)
@@ -1110,7 +1147,8 @@
         hidden_grad = low(dot_f32(up3_low, down_w[:, span], NN) * slope_ref[:, span])
         grad_ref[:, u_span + at : u_span + at + size] += dot_f32(up3_low, act_ref[:, span], TN)
         grad_ref[:, o_span + at : o_span + at + size] += dot_f32(second, hidden_grad, TN)
-        bu_grad[0:1, span] += column_sum(hidden_grad.astype(jnp.float32))
+        row = 8 + at // size
+        vec_grad[row : row + 1, :size] += column_sum(hidden_grad.astype(jnp.float32))
         back = back + dot_f32(hidden_grad, up_w[:, span], NT)
     through, g_gain2, g_shift2 = norm_rows_back(back, scaled2, inverse2, gain2)
     middle_grad = up3 + through
@@ -1120,7 +1158,7 @@
     do_ref[0] = low(dot_f32(middle_low, out_w[...], NT))
     sums = (column_sum(middle_grad), g_gain2, g_shift2, column_sum(up3), g_gain3, g_shift3)
     for at, part in enumerate(sums):
-        vec_grad[at : at + 1, :] += part
+        vec_grad[at : at + 1, :D_D] += part
 
 
 def whole(shape):
@@ -1158,20 +1196,16 @@
             per_image(rows, D_D),
             per_image(rows, D_D),
             whole((D_D, D_D + 2 * FF_D + PIX)),
-            whole((8, D_D)),
-            whole((8, FF_D)),
-            whole((8, PIX)),
+            whole((16, PIX)),
         ],
         out_shape=[
             jax.ShapeDtypeStruct((images, rows, D_D), jnp.bfloat16),
             jax.ShapeDtypeStruct((images, rows, D_D), f32),
             jax.ShapeDtypeStruct((D_D, D_D + 2 * FF_D + PIX), f32),
-            jax.ShapeDtypeStruct((8, D_D), f32),
-            jax.ShapeDtypeStruct((8, FF_D), f32),
-            jax.ShapeDtypeStruct((8, PIX), f32),
+            jax.ShapeDtypeStruct((16, PIX), f32),
         ],
         scratch_shapes=[pltpu.VMEM((rows, FF_D), f32), pltpu.VMEM((rows, FF_D), jnp.bfloat16)],
-        compiler_params=pltpu.CompilerParams(vmem_limit_bytes=44 * 1024 * 1024),
+        compiler_params=pltpu.CompilerParams(vmem_limit_bytes=VMEM_LIMIT),
         cost_estimate=pl.CostEstimate(
             flops=12 * images * rows * D_D * (D_D + 2 * FF_D + PIX),
             bytes_accessed=30 * 1024 * 1024,
@@ -1221,7 +1255,7 @@
         ],
         out_specs=[per_image(rows, D_D) for rows, _ in kinds],
         out_shape=[jax.ShapeDtypeStruct((images, rows, D_D), kind) for rows, kind in kinds],
-        compiler_params=pltpu.CompilerParams(vmem_limit_bytes=44 * 1024 * 1024),
+        compiler_params=pltpu.CompilerParams(vmem_limit_bytes=VMEM_LIMIT),
         cost_estimate=pl.CostEstimate(
             flops=4 * images * D_ROWS * D_D * D_D * 2,
             bytes_accessed=20 * 1024 * 1024,
@@ -1278,7 +1312,7 @@
         g_gain,
     )
     for at, part in enumerate(sums):
-        vec_grad[at : at + 1, :] += part
+        vec_grad[at : at + 1, :D_D] += part
 
     @pl.when(image == pl.num_programs(0) - 1)
     def _():
@@ -1304,14 +1338,14 @@
             columns(D_D, D_D, 2),
             whole((8, D_D)),
         ],
-        out_specs=[whole((images * KEEP + TAIL, D_D)), whole((D_D, 3 * D_D)), whole((8, D_D))],
+        out_specs=[whole((images * KEEP + TAIL, D_D)), whole((D_D, 3 * D_D)), whole((8, D_E))],
         out_shape=[
             jax.ShapeDtypeStruct((images * KEEP + TAIL, D_D), jnp.bfloat16),
             jax.ShapeDtypeStruct((D_D, 3 * D_D), f32),
-            jax.ShapeDtypeStruct((8, D_D), f32),
+            jax.ShapeDtypeStruct((8, D_E), f32),
         ],
         scratch_shapes=[pltpu.VMEM((TAIL, D_D), f32)],
-        compiler_params=pltpu.CompilerParams(vmem_limit_bytes=44 * 1024 * 1024),
+        compiler_params=pltpu.CompilerParams(vmem_limit_bytes=VMEM_LIMIT),
         cost_estimate=pl.CostEstimate(
             flops=12 * images * rows * D_D * D_D * 2,
             bytes_accessed=24 * 1024 * 1024,
@@ -1417,7 +1451,7 @@
         ],
         out_specs=[per_image(*shape) for shape, _ in shapes],
         out_shape=[jax.ShapeDtypeStruct((images,) + shape, kind) for shape, kind in shapes],
-        compiler_params=pltpu.CompilerParams(vmem_limit_bytes=KERNEL_LIMIT),
+        compiler_params=pltpu.CompilerParams(vmem_limit_bytes=VMEM_LIMIT),
         cost_estimate=pl.CostEstimate(
             flops=2 * images * E_ROWS * enc_full.size,
             bytes_accessed=40 * 1024 * 1024,
@@ -1434,7 +1468,7 @@
 
 
 def encoder_back_kernel(
-    place_ref,
+    hosted,
     de_ref,
     cls_ref,
     mid_ref,
@@ -1444,25 +1478,32 @@
     act_ref,
     w_ref,
     vec_ref,
-    do_ref,
-    dmid_ref,
-    grad_ref,
-    vec_grad,
-    bu_grad,
-    be_grad,
-    de_all,
-    hidden_all,
+    *refs,
 ):
+    if hosted:
+        dec_ref, do_ref, dmid_ref, grad_ref, vec_grad, dec_out, de_all, hidden_all, *refs = refs
+        plane = PlaneSum(dec_ref, *refs[:5])
+        line = LineSum(*refs[5:])
+    else:
+        do_ref, dmid_ref, grad_ref, vec_grad, de_all, hidden_all = refs
     image = pl.program_id(0)
-    place = place_ref[0]
-    clear_first((grad_ref, vec_grad, bu_grad, be_grad))
+    last = pl.num_programs(0) - 1
+    place = lax.axis_index("seq")
+    clear_first((grad_ref, vec_grad))
+    if hosted:
+
+        @pl.when(image == 0)
+        def _():
+            greet_all()
+            plane.start()
+
     gain2, gain3, shift2, shift3 = (vec_ref[i : i + 1, :] for i in range(4))
     at = lax.broadcasted_iota(jnp.int32, (TAIL, D_D), 0)
     cls = column_sum(jnp.where(at == image, cls_ref[...].astype(jnp.float32), 0.0))
     de_all[:KEEP] = de_ref[...]
     de_all[KEEP:] = low(tail_rows(cls))
     de = de_all[...]
-    be_grad[0:1, :] += column_sum(de.astype(jnp.float32))
+    vec_grad[6:7, :D_D] += column_sum(de.astype(jnp.float32))
     scaled3, inverse3 = norm_rows(enc_ref[0])
     third = low(scaled3 * gain3 + shift3)
     quarter = FF_E // 4
@@ -1484,7 +1525,8 @@
         hidden = dot_f32(up3_low, w_ref[:, E_DOWN + at : E_DOWN + at + SIZE], NN)
         hidden = low(hidden * slope_ref[0, :, span])
         hidden_all[:, span] = hidden
-        bu_grad[0:1, span] += column_sum(hidden.astype(jnp.float32))
+        row = 8 + at // SIZE
+        vec_grad[row : row + 1, :] += column_sum(hidden.astype(jnp.float32))
         back = back + dot_f32(hidden, w_ref[:, E_UP + at : E_UP + at + SIZE], NT)
     grad_ref[:, first : first + quarter] += dot_f32(second, hidden_all[:, own_hidden], TN)
     grad_ref[:, first + quarter : first + 2 * quarter] += dot_f32(
@@ -1498,63 +1540,83 @@
     sums = (column_sum(middle_grad), g_shift2, column_sum(up3), g_shift3, g_gain2, g_gain3)
     for at, part in enumerate(sums):
         vec_grad[at : at + 1, :] += part
-
-
-def scalar_spec():
-    return pl.BlockSpec(memory_space=pltpu.SMEM)
-
-
-def encoder_back(place, de_sum, saved, enc_full, vectors):
+    if hosted:
+        pl.when(image == 0)(plane.pass_on)
+        pl.when(image == 1)(lambda: line.start(plane.total()))
+
+        @pl.when(image == last)
+        def _():
+            line.spread()
+            line.finish()
+            plane.finish()
+            dec_out[...] = line.result[...]
+
+
+def encoder_back(de_sum, saved, enc_full, vectors, dec, collective_id):
     mid, enc, o, slope, act = saved
     images = mid.shape[0]
     f32 = jnp.float32
     width = D_E // 4 + FF_E // 2 + D_D // 4
-    return pl.pallas_call(
-        encoder_back_kernel,
+    dec_rows, dec_cols = dec.shape[0] // lax.axis_size("fsdp"), dec.shape[1]
+    hosted = plane_fits(dec.shape[0]) and images >= 3
+    results = pl.pallas_call(
+        partial(encoder_back_kernel, hosted),
         grid=(images,),
         in_specs=[
-            scalar_spec(),
             pl.BlockSpec((KEEP, D_D), lambda i: (i, 0)),
             pl.BlockSpec((TAIL, D_D), lambda i: (images * KEEP // TAIL, 0)),
             per_image(E_ROWS, D_E),
             per_image(E_ROWS, D_E),
             per_image(E_ROWS, D_E),
-            per_image(E_ROWS, FF_E),
+            pl.BlockSpec((1, E_ROWS, FF_E), lambda i: (i, 0, 0), pipeline_mode=pl.Buffered(1)),
             per_image(E_ROWS, FF_E),
             whole(enc_full.shape),
             whole((8, D_E)),
-        ],
+        ]
+        + [whole(dec.shape)] * hosted,
         out_specs=[
             per_image(E_ROWS, D_E),
             per_image(E_ROWS, D_E),
             whole((D_E, width)),
-            whole((8, D_E)),
-            whole((8, FF_E)),
-            whole((8, D_D)),
-        ],
+            whole((16, D_E)),
+        ]
+        + [whole((dec_rows, dec_cols))] * hosted,
         out_shape=[
             jax.ShapeDtypeStruct((images, E_ROWS, D_E), jnp.bfloat16),
             jax.ShapeDtypeStruct((images, E_ROWS, D_E), f32),
             jax.ShapeDtypeStruct((D_E, width), f32),
-            jax.ShapeDtypeStruct((8, D_E), f32),
-            jax.ShapeDtypeStruct((8, FF_E), f32),
-            jax.ShapeDtypeStruct((8, D_D), f32),
-        ],
+            jax.ShapeDtypeStruct((16, D_E), f32),
+        ]
+        + [jax.ShapeDtypeStruct((dec_rows, dec_cols), f32)] * hosted,
         scratch_shapes=[
             pltpu.VMEM((E_ROWS, D_D), jnp.bfloat16),
             pltpu.VMEM((E_ROWS, FF_E), jnp.bfloat16),
-        ],
-        compiler_params=pltpu.CompilerParams(vmem_limit_bytes=KERNEL_LIMIT),
+        ]
+        + (
+            PlaneSum.scratch(dec_rows, dec_cols, f32)
+            + LineSum.scratch(dec_rows, dec_cols, lax.axis_size("seq"))
+            if hosted
+            else []
+        ),
+        compiler_params=pltpu.CompilerParams(
+            vmem_limit_bytes=VMEM_LIMIT,
+            **(dict(collective_id=collective_id, has_side_effects=True) if hosted else {}),
+        ),
         cost_estimate=pl.CostEstimate(
             flops=3 * images * E_ROWS * enc_full.size,
             bytes_accessed=50 * 1024 * 1024,
             transcendentals=0,
         ),
-    )(place, de_sum, de_sum, mid, enc, o, slope, act, enc_full, vectors)
+    )(de_sum, de_sum, mid, enc, o, slope, act, enc_full, vectors, *([dec] * hosted))
+    if hosted:
+        return results
+    dec_sum = lax.psum(lax.psum_scatter(dec, "fsdp", scatter_dimension=0, tiled=True), "seq")
+    return *results, dec_sum
 
 
 def encoder_entry_back_kernel(
-    place_ref,
+    hosted,
+    extra,
     kept_ref,
     x_ref,
     qkv_ref,
@@ -1564,12 +1626,25 @@
     dmid_ref,
     w_ref,
     vec_ref,
-    grad_ref,
-    vec_grad,
-    dqkv_ref,
+    *refs,
 ):
-    place = place_ref[0]
+    if hosted:
+        early_ref, grad_ref, vec_grad, early_out, dqkv_ref, *refs = refs
+        plane = PlaneSum(early_ref, *refs[:5])
+        line = LineGather(*refs[5:])
+    else:
+        grad_ref, vec_grad, dqkv_ref = refs
+    place = lax.axis_index("seq")
+    image = pl.program_id(0)
+    last = pl.num_programs(0) - 1
     clear_first((grad_ref, vec_grad))
+    if hosted:
+
+        @pl.when(image == 0)
+        def _():
+            greet_all()
+            plane.start()
+
     gain1, shift1 = (vec_ref[i : i + 1, :] for i in range(2))
     for group in range(D_E // 128):
         span = slice(group * 128, (group + 1) * 128)
@@ -1607,17 +1682,36 @@
     sums = [column_sum(patches), back[KEEP : KEEP + 1], g_shift1] + sums + [g_gain1]
     for at, part in enumerate(sums):
         vec_grad[at : at + 1, :] += part
-
-
-def encoder_entry_back(place, kept, saved, do, dmid, enc_full, vectors):
+    if hosted:
+        pl.when(image == 0)(plane.pass_on)
+        pl.when(image == 1)(lambda: line.start(with_rests(plane.total(), extra)))
+
+        @pl.when(image == last)
+        def _():
+            line.wait_recv()
+            line.finish()
+            plane.finish()
+            early_out[...] = line.slots[...]
+
+
+def with_rests(total, extra):
+    rounded = low(total)
+    rest = total[:, -extra:] - rounded[:, -extra:].astype(jnp.float32)
+    return jnp.concatenate([rounded, low(rest)], axis=1)
+
+
+def encoder_entry_back(kept, saved, do, dmid, enc_full, vectors, early, extra, collective_id):
     x0, qkv, lse, o = saved
     images = kept.shape[0]
     f32 = jnp.float32
-    return pl.pallas_call(
-        encoder_entry_back_kernel,
+    line = lax.axis_size("seq")
+    rows, width = early.shape[0] // lax.axis_size("fsdp"), early.shape[1]
+    gathered = (line, rows, width + extra)
+    hosted = plane_fits(early.shape[0]) and images >= 3
+    results = pl.pallas_call(
+        partial(encoder_entry_back_kernel, hosted, extra),
         grid=(images,),
         in_specs=[
-            scalar_spec(),
             per_image(KEEP, D_E),
             per_image(E_ROWS, D_E),
             per_image(E_ROWS, 3 * D_E),
@@ -1627,20 +1721,35 @@
             per_image(E_ROWS, D_E),
             columns(D_E, 5 * D_E, 0),
             whole((8, D_E)),
-        ],
-        out_specs=[whole((D_E, D_E)), whole((8, D_E))],
+        ]
+        + [whole(early.shape)] * hosted,
+        out_specs=[whole((D_E, D_E)), whole((8, D_E))] + [whole(gathered)] * hosted,
         out_shape=[
             jax.ShapeDtypeStruct((D_E, D_E), f32),
             jax.ShapeDtypeStruct((8, D_E), f32),
-        ],
-        scratch_shapes=[pltpu.VMEM((E_ROWS, 3 * D_E), jnp.bfloat16)],
-        compiler_params=pltpu.CompilerParams(vmem_limit_bytes=KERNEL_LIMIT),
+        ]
+        + [jax.ShapeDtypeStruct(gathered, jnp.bfloat16)] * hosted,
+        scratch_shapes=[pltpu.VMEM((E_ROWS, 3 * D_E), jnp.bfloat16)]
+        + (
+            PlaneSum.scratch(rows, width, jnp.bfloat16)
+            + [pltpu.VMEM(gathered, jnp.bfloat16), pltpu.SemaphoreType.DMA((2, line - 1))]
+            if hosted
+            else []
+        ),
+        compiler_params=pltpu.CompilerParams(
+            vmem_limit_bytes=VMEM_LIMIT,
+            **(dict(collective_id=collective_id, has_side_effects=True) if hosted else {}),
+        ),
         cost_estimate=pl.CostEstimate(
             flops=8 * images * E_ROWS * D_E * 4 * D_E,
             bytes_accessed=20 * 1024 * 1024,
             transcendentals=images * H_E * E_ROWS * E_ROWS,
         ),
-    )(place, kept, x0, qkv, lse, o, do, dmid, enc_full, vectors)
+    )(kept, x0, qkv, lse, o, do, dmid, enc_full, vectors, *([early] * hosted))
+    if hosted:
+        return results
+    own = lax.psum_scatter(early, "fsdp", scatter_dimension=0, tiled=True)
+    return *results, lax.all_gather(with_rests(own, extra), "seq", axis=0, tiled=False)
 
 
 def stack_rows(parts, count=8):
@@ -1709,6 +1818,50 @@
     )(weight, moment_one, moment_two, early, late)
 
 
+ENC_BACK, ENC_ENTRY, DEC_MIDDLE, DEC_ENTRY, SMALL_ROWS = 0, 16, 24, 40, 64
+LOSS_ROW = DEC_MIDDLE + 7
+GAIN_ROWS = (ENC_ENTRY + 5, ENC_BACK + 4, ENC_BACK + 5, DEC_ENTRY + 4, DEC_MIDDLE + 1, DEC_MIDDLE + 4)
+BIAS_ROWS = (
+    (ENC_ENTRY, ENC_ENTRY + 1, ENC_ENTRY + 2, ENC_ENTRY + 3, ENC_ENTRY + 4, ENC_BACK, ENC_BACK + 1)
+    + (ENC_BACK + 8, ENC_BACK + 2, ENC_BACK + 3, ENC_BACK + 6)
+    + (DEC_ENTRY, DEC_ENTRY + 1, DEC_ENTRY + 2, DEC_ENTRY + 3, DEC_MIDDLE, DEC_MIDDLE + 2)
+    + (DEC_MIDDLE + 8, DEC_MIDDLE + 3, DEC_MIDDLE + 5, DEC_MIDDLE + 6)
+)
+
+
+def small_update_kernel(sums_ref, *refs):
+    gains, biases, gain_out, bias_out = refs[:3], refs[3:6], refs[6:9], refs[9:12]
+    gain_spans = list(zip(GAIN_ROWS, [D_E] * 3 + [D_D] * 3))
+    bias_spans = []
+    for row, width in zip(BIAS_ROWS, bias_widths()):
+        pieces = 4 if width > D_E else 1
+        bias_spans += [(row + at, width // pieces) for at in range(pieces)]
+    for spans, ins, outs in ((gain_spans, gains, gain_out), (bias_spans, biases, bias_out)):
+        start = 0
+        for row, width in spans:
+            span = slice(start, start + width)
+            start += width
+            weight, moment_one, moment_two = (ref[:, span] for ref in ins)
+            news = adamw(
+                weight, moment_one, moment_two, sums_ref[row : row + 1, :width], SMALL_RATE, 0.0
+            )
+            for out, new in zip(outs, news):
+                out[:, span] = new
+
+
+def small_update(sums, *vectors):
+    rows = [vector[None] for vector in vectors]
+    vmem = pl.BlockSpec(memory_space=pltpu.VMEM)
+    news = pl.pallas_call(
+        small_update_kernel,
+        in_specs=[vmem] * 7,
+        out_specs=[vmem] * 6,
+        out_shape=[jax.ShapeDtypeStruct(row.shape, jnp.float32) for row in rows],
+        compiler_params=pltpu.CompilerParams(vmem_limit_bytes=COPY_LIMIT),
+    )(sums, *rows)
+    return tuple(new[0] for new in news)
+
+
 def shards(
     pixels,
     restore,
@@ -1733,8 +1886,6 @@
     images, own_count, _ = pixels.shape
     masked_total = images * lax.axis_size("fsdp") * (PATCHES - KEEP)
 
-    enc_low = low(enc_w)
-    dec_full = lax.all_gather(low(dec_w), "fsdp", axis=0, tiled=True)
     head_low = low(head_w)
 
     pieces = split_vector(bias_w, bias_widths())
@@ -1752,16 +1903,25 @@
     own_restore = turned[:, :own_count]
     own_pick = low(own_restore[:, None, :] == ranks[None, :, None])
     own_kept = jnp.einsum("irp,ipd->ird", own_pick, pixels, preferred_element_type=jnp.float32)
-    enc_full, kept = start_gather(enc_low, low(own_kept).reshape(images * KEEP, PIX), 0)
-    kept = kept.reshape(images, KEEP, PIX)
     patch_ids = jnp.arange(PATCHES, dtype=jnp.int32)
     keep_ids = jnp.sum(
         jnp.where(restore[:, None, :] == ranks[None, :, None], patch_ids, 0), axis=2
     )
+    enc_full, kept, kept_places, patch_places = start_gather(
+        low(enc_w),
+        low(own_kept).reshape(images * KEEP, PIX),
+        keep_ids.reshape(-1),
+        lax.rem(patch_ids + place * own_count, PATCHES),
+        b_patch,
+        0,
+    )
+    kept, dec_low = lax.optimization_barrier((kept, low(dec_w)))
+    dec_full = lax.all_gather(dec_low, "fsdp", axis=0, tiled=True)
+    kept = kept.reshape(images, KEEP, PIX)
 
     x0, e_mid, encoded, e_mixed, e_lse, e_o, e_slope, e_act, shrunk = encoder(
         kept,
-        b_patch + positions(keep_ids, D_E),
+        kept_places.reshape(images, KEEP, D_E),
         enc_full,
         stack_rows(
             gains[:3] + [cls_token, e_shift1, e_bq, e_bv, e_bo, e_shift2, e_bd, e_shift3], 16
@@ -1770,12 +1930,11 @@
         b_embed[None],
     )
 
-    turned_ids = lax.rem(patch_ids + place * own_count, PATCHES)
     ranks_row = turned[:, None, :]
     y0, d_q, d_k, d_v = dec_entry(
         shrunk,
         ranks_row,
-        positions(turned_ids, D_D),
+        patch_places,
         dec_full,
         stack_rows([mask_token, gains[3], d_shift1, d_bq, d_bv]),
         own_count,
@@ -1784,7 +1943,7 @@
     d_o, d_lse = attend_forward(d_q, d_k, d_v, H_D)
     own_masked = (own_restore >= KEEP).astype(jnp.float32)
     own_masked = jnp.broadcast_to(own_masked[..., None], own_masked.shape + (128,))
-    d_do, d_dmid, late_grads, mid_sums, bu_sums, bh_sums = dec_middle(
+    d_do, d_dmid, late_grads, middle_sums = dec_middle(
         d_o,
         y0_own,
         pixels,
@@ -1796,75 +1955,58 @@
         b_head[None],
         2.0 / (PIX * masked_total),
     )
-    g_d_bo, g_d_gain2, g_d_shift2, g_d_bd, g_d_gain3, g_d_shift3 = (mid_sums[i] for i in range(6))
-    g_d_bu = bu_sums[0]
-    g_b_head = bh_sums[0]
-    loss_part = jnp.sum(bh_sums[1]) / (PIX * masked_total)
     dec_late = lax.psum_scatter(late_grads, "fsdp", scatter_dimension=0, tiled=True)
     d_dq, d_dk, d_dv = attend_backward(d_q, d_k, d_v, d_lse, d_do, d_o, H_D)
-    de_part, g_d_qkv, entry_sums = dec_entry_back(
+    de_part, g_d_qkv, dec_entry_sums = dec_entry_back(
         y0, d_dq, d_dk, d_dv, d_dmid, ranks_row, dec_full, stack_rows([gains[3], d_shift1])
     )
-    g_mask, g_d_shift1, g_d_bq, g_d_bv, g_d_gain1 = (entry_sums[i] for i in range(5))
     de_sum = line_sum(de_part, 7, 1)
     dec_late, de_sum = lax.optimization_barrier((dec_late, de_sum))
     dec_late = lax.psum(dec_late, "seq")
 
-    place_word = place[None].astype(jnp.int32)
-    e_do, e_dmid, early_grads, back_sums, bu_sums, be_sums = encoder_back(
-        place_word,
+    embed_cols = D_D // seq_count
+    e_do, e_dmid, early_grads, enc_back_sums, dec_early = encoder_back(
         de_sum,
         (e_mid, encoded, e_o, e_slope, e_act),
         enc_full,
         stack_rows([gains[1], gains[2], e_shift2, e_shift3]),
-    )
-    g_e_bo, g_e_shift2, g_e_bd, g_e_shift3, g_e_gain2, g_e_gain3 = (back_sums[i] for i in range(6))
-    g_e_bu = bu_sums[0]
-    g_b_embed = be_sums[0]
-    late_grads, entry_sums = encoder_entry_back(
-        place_word,
+        g_d_qkv,
+        2,
+    )
+    late_grads, enc_entry_sums, early_all = encoder_entry_back(
         kept,
         (x0, e_mixed, e_lse, e_o),
         e_do,
         e_dmid,
         enc_full,
         stack_rows([gains[0], e_shift1]),
-    )
-    g_b_patch, g_cls, g_e_shift1, g_e_bq, g_e_bv, g_e_gain1 = (entry_sums[i] for i in range(6))
+        early_grads,
+        embed_cols,
+        3,
+    )
 
     once = jnp.where(place == 0, 1.0, 0.0)
-    enc_bias = [g_b_patch, g_cls, g_e_shift1, g_e_bq, g_e_bv, g_e_bo, g_e_shift2, g_e_bu]
-    enc_bias = jnp.concatenate(enc_bias + [g_e_bd, g_e_shift3, g_b_embed]) * once
-    dec_bias = [g_mask, g_d_shift1, g_d_bq, g_d_bv, g_d_bo, g_d_shift2, g_d_bu, g_d_bd]
-    dec_bias = jnp.concatenate(dec_bias + [g_d_shift3, g_b_head])
-    enc_gain = jnp.concatenate([g_e_gain1, g_e_gain2, g_e_gain3]) * once
-    dec_gain = jnp.concatenate([g_d_gain1, g_d_gain2, g_d_gain3])
-    small = jnp.concatenate([enc_gain, dec_gain, enc_bias, dec_bias, loss_part[None]])
-    embed_cols = D_D // seq_count
+    small = jnp.concatenate(
+        [
+            enc_back_sums * once,
+            enc_entry_sums * once,
+            middle_sums,
+            dec_entry_sums,
+            jnp.zeros((SMALL_ROWS - DEC_ENTRY - 8, D_E), jnp.float32),
+        ],
+        axis=0,
+    )
     dec_late, late_grads = lax.optimization_barrier((dec_late, late_grads))
-    early_all, late_all, small, dec_early, head_grad = exchange(
-        early_grads,
-        late_grads,
-        small,
-        g_d_qkv,
-        dec_late[:, D_D + 2 * FF_D :],
-        seq_count,
-        embed_cols,
-        2,
-    )
+    late_all, small, head_grad = exchange(
+        late_grads, small, dec_late[:, D_D + 2 * FF_D :], seq_count, 4
+    )
+    loss_total = jnp.sum(small[LOSS_ROW]) / (PIX * masked_total)
     dec_grad = jnp.concatenate([dec_early, dec_late[:, : D_D + 2 * FF_D]], axis=1)
-    n_gain = gain_w.shape[0]
-    n_bias = bias_w.shape[0]
-    gain_grad = small[:n_gain]
-    bias_grad = small[n_gain : n_gain + n_bias]
-    loss_total = small[n_gain + n_bias]
-
+    small_new = small_update(small, gain_w, gain_m, gain_v, bias_w, bias_m, bias_v)
     enc_new = tuple(enc_update(enc_w, enc_m, enc_v, early_all, late_all))
     dec_new = adamw(dec_w, dec_m, dec_v, dec_grad, MATRIX_RATE, MATRIX_DECAY)
     head_new = adamw(head_w, head_m, head_v, head_grad, MATRIX_RATE, MATRIX_DECAY)
-    gain_new = adamw(gain_w, gain_m, gain_v, gain_grad, SMALL_RATE, 0.0)
-    bias_new = adamw(bias_w, bias_m, bias_v, bias_grad, SMALL_RATE, 0.0)
-    return (loss_total,) + enc_new + dec_new + head_new + gain_new + bias_new
+    return (loss_total,) + enc_new + dec_new + head_new + tuple(small_new)
 
 
 def solution(mesh):

time: 551 us -> 532 us (0.966); the launches traced: 547 us -> 522 us
  local copies, waits for them, and re-layouts: 57.1 us -> 18.4 us
  Pallas kernels: 439 us -> 457 us
  other arithmetic: 34.5 us -> 25.1 us
    unnamed x131 -> x44, local copies, waits for them, and re-layouts: 46.6 us -> 8.8 us
    pallas_call x3 -> x4, Pallas kernels: 156 us -> 179 us  [the longest x1 75.7 us: encoder_back(): pl.pallas_call(partial(encoder_back_kernel, hosted), grid=(images,), in_s...]
    pallas_call x1, Pallas kernels: 94 us -> 78.7 us  [start_gather(): pl.pallas_call(partial(start_kernel, lines), out_shape=[jax.ShapeDtypeStr...]
    sin x2 -> x0, other arithmetic: 7.87 us -> none  [positions(): return jnp.concatenate([jnp.sin(angles), jnp.cos(angles)], axis=-1)]
    sub x4 -> x2, other arithmetic: 12.5 us -> 12.1 us  [adamw(): weight - step_rate * (fixed_one / (jnp.sqrt(fixed_two) + ADAM_EPS) + deca...]
  transfers between devices with their start and end apart: 3 -> 3, of which waited for: 0 -> 1; matrix products, arithmetic and copies ran while one was open for 8% -> 2% of each run, Pallas kernels for 52% -> 52%
where the time goes in v5:
time: 532 us; the launch traced here: 522 us
  Pallas kernels  457 us (86%)
  other arithmetic  25.1 us (5%)
  local copies, waits for them, and re-layouts  18.4 us (3%)
  between operations  16.5 us (3%)
    pallas_call x1, Pallas kernels, start_gather(): pl.pallas_call(partial(start_kernel, lines), out_shape=[jax.ShapeDtypeStr...  78.7 us
    pallas_call x1, Pallas kernels, encoder_back(): pl.pallas_call(partial(encoder_back_kernel, hosted), grid=(images,), in_s...  75.7 us
    pallas_call x1, Pallas kernels, encoder_entry_back(): pl.pallas_call(partial(encoder_entry_back_kernel, hosted, extra), grid=(i...  68 us
    pallas_call x1, Pallas kernels, attend_backward(): pl.pallas_call(partial(attend_backward_kernel, heads, head_dim), grid=(im...  41.7 us
    pallas_call x1, Pallas kernels, encoder(): pl.pallas_call(encoder_kernel, grid=(images,), in_specs=[per_image(KEEP,...  36.4 us
    pallas_call x1, Pallas kernels, exchange(): pl.pallas_call(exchange_kernel, out_shape=[jax.ShapeDtypeStruct((line, ro...  34.9 us
    pallas_call x1, Pallas kernels, line_sum(): pl.pallas_call(partial(line_sum_kernel, chunks, lax.axis_size('seq')), ou...  27.8 us
    pallas_call x1, Pallas kernels, dec_middle(): pl.pallas_call(partial(dec_middle_kernel, grad_scale), grid=(images,), in...  27.6 us
  transfers between devices with their start and end apart: 3, of which 1 were waited for; matrix products, arithmetic and copies ran while one was open for 2% of the time, Pallas kernels for 52%

profile of v5, /device:TPU:9, one launch (start us, length us, event | category | flops | bytes accessed | tf_op | source)
XLA Modules:
  0.0 521.5 jit_solution(1477203980261836342)
XLA Ops:
  7.3 2.4 convert_element_type.28.w_ref
  10.6 2.4 convert_element_type.30
  12.9 1.8 convolution_convert_fusion
  14.7 78.7 %shard_map.288 = (bf16[768,10496]{1,0:T(8,128)(2,1)}, bf16[768,768]{1,0:T(8,128)(2,1)S(1)}, f32[768,768]{1,0:T(8,128)S(1)}, f32[1024,512]{1,0:T(8,128)S(1)}) custom-call(bf16[96,10496]{1,0:T(8,128)(2,1)S(1)} %convert_element_type.28.w_ref, bf16[768,768]{1,0:T(8,128)(2,1)S(1)} %bitcast.30, s32[768,1]{1,0:T(8,128)S(1)} %bitcast.31, ...), custom_call_target="tpu_custom_call" | custom-call | bytes 209715200 | tf_op jit(solution)/shard_map/pallas_call | solution.py:676
  93.4 1.4 copy-done.8
  94.8 1.3 copy-done.9
  101.1 2.4 convert_element_type.32.head_w
  104.7 36.4 %shard_map.289 = (f32[3,272,768]{2,1,0:T(8,128)}, f32[3,272,768]{2,1,0:T(8,128)}, f32[3,272,768]{2,1,0:T(8,128)}, bf16[3,272,2304]{2,1,0:T(8,128)(2,1)}, f32[3,1...) custom-call(bf16[3,256,768]{2,1,0:T(8,128)(2,1)} %bitcast.39, ...), custom_call_target="tpu_custom_call" | custom-call | flops 13155434496 | bytes 41943040 | tf_op jit(solution)/shard_map/pallas_call | solution.py:1441
  141.1 2.7 all-gather.2.cloned.1.call-done.q_w.k_w.v_w.out_w.up_w.down_w
  143.8 9.9 %shard_map.290 = (f32[3,1040,512]{2,1,0:T(8,128)}, bf16[3,256,512]{2,1,0:T(8,128)(2,1)}, bf16[3,1040,512]{2,1,0:T(8,128)(2,1)}, bf16[3,1040,512]{2,1,0:T(8,128)(2,1)}) custom-call(bf16[3,272,512]{2,1,0:T(8,128)(2,1)} %get-tuple-element.75.e_ref, s32[3,1,1024]{2,1,0:T(1,128)} %broadcast_in_dim.65.rank_ref, f32[1024,512]{1,0:T(8,128)} %copy-done.9, ...), custom_call_target="tpu_custom_call" | custom-call | flops 6543114240 | bytes 20971520 | tf_op jit(solution)/shard_map/pallas_call | solution.py:1244
  153.7 2.7 slice.116.y_ref
  156.4 22.9 %shard_map.291 = (bf16[3,256,512]{2,1,0:T(8,128)(2,1)}, f32[3,4,4,256]{3,2,1,0:T(4,128)}) custom-call(bf16[3,256,512]{2,1,0:T(8,128)(2,1)} %get-tuple-element.78.q_ref, bf16[3,1040,512]{2,1,0:T(8,128)(2,1)} %get-tuple-element.79.k_ref, bf16[3,1040,512]{2,1,0:T(8,128)(2,1)} %get-tuple-element.80.v_ref), custom_call_target="tpu_custom_call" | custom-call | flops 6543114240 | bytes 7962624 | tf_op jit(solution)/shard_map/pallas_call | solution.py:284
  180.2 27.6 %shard_map.292 = (bf16[3,256,512]{2,1,0:T(8,128)(2,1)}, f32[3,256,512]{2,1,0:T(8,128)}, f32[512,5376]{1,0:T(8,128)}, f32[16,768]{1,0:T(8,128)}) custom-call(bf16[3,256,512]{2,1,0:T(8,128)(2,1)} %get-tuple-element.81.o_ref, f32[3,256,512]{2,1,0:T(8,128)} %slice.116.y_ref, bf16[3,256,768]{2,1,0:T(8,128)(2,1)} %pixel_ref.1, ...), custom_call_target="tpu_custom_call" | custom-call | flops 25367150592 | bytes 31457280 | tf_op jit(solution)/shard_map/pallas_call | solution.py:1179
  210.4 41.7 %shard_map.293 = (bf16[3,256,512]{2,1,0:T(8,128)(2,1)}, bf16[3,1040,512]{2,1,0:T(8,128)(2,1)}, bf16[3,1040,512]{2,1,0:T(8,128)(2,1)}) custom-call(bf16[3,256,512]{2,1,0:T(8,128)(2,1)} %get-tuple-element.78.q_ref, bf16[3,1040,512]{2,1,0:T(8,128)(2,1)} %get-tuple-element.79.k_ref, bf16[3,1040,512]{2,1,0:T(8,128)(2,1)} %get-tuple-element.80.v_ref, ...), custom_call_target="tpu_custom_call" | custom-call | flops 16357785600 | bytes 15925248 | tf_op jit(solution)/shard_map/pallas_call | solution.py:309
  252.1 20.8 %shard_map.294 = (bf16[784,512]{1,0:T(8,128)(2,1)}, f32[512,1536]{1,0:T(8,128)}, f32[8,768]{1,0:T(8,128)}) custom-call(f32[3,1040,512]{2,1,0:T(8,128)} %get-tuple-element.82.y_ref, bf16[3,256,512]{2,1,0:T(8,128)(2,1)} %get-tuple-element.86.dq_ref, bf16[3,1040,512]{2,1,0:T(8,128)(2,1)} %get-tuple-element.87.dk_ref, ...), custom_call_target="tpu_custom_call" | custom-call | flops 19629342720 | bytes 25165824 | tf_op jit(solution)/shard_map/pallas_call | solution.py:1326
  272.9 1.4 copy-done.3
  274.3 27.8 %shard_map.295.de_ref.cls_ref = bf16[784,512]{1,0:T(8,128)(2,1)S(1)} custom-call(bf16[784,512]{1,0:T(8,128)(2,1)S(1)} %copy-done.3), custom_call_target="tpu_custom_call" | custom-call | bytes 40140800 | tf_op jit(solution)/shard_map/pallas_call | solution.py:714
  303.0 75.7 %shard_map.296 = (bf16[3,272,768]{2,1,0:T(8,128)(2,1)}, f32[3,272,768]{2,1,0:T(8,128)}, f32[768,1856]{1,0:T(8,128)}, f32[16,768]{1,0:T(8,128)}, f32[64,1536]{1,0:T(8,128)}) custom-call(bf16[784,512]{1,0:T(8,128)(2,1)} %copy-done.2, bf16[784,512]{1,0:T(8,128)(2,1)} %copy-done.2, f32[3,272,768]{2,1,0:T(8,128)} %get-tuple-element.97.mid_ref, ...), custom_call_target="tpu_custom_call" | custom-call | flops 19733151744 | bytes 52428800 | tf_op jit(solution)/shard_map/pallas_call | solution.py:1562
  378.7 68.0 %shard_map.297 = (f32[768,768]{1,0:T(8,128)}, f32[8,768]{1,0:T(8,128)}, bf16[4,96,1984]{2,1,0:T(8,128)(2,1)}) custom-call(bf16[3,256,768]{2,1,0:T(8,128)(2,1)} %bitcast.40, f32[3,272,768]{2,1,0:T(8,128)} %get-tuple-element.92.x_ref, bf16[3,272,2304]{2,1,0:T(8,128)(2,1)} %get-tuple-element.93.qkv_ref, f32[3,12,272]{2,1,0:T(8,128)} %get-tuple-element.94.lse_ref, ...), custom_call_target="tpu_custom_call" | custom-call | flops 15401484288 | bytes 20971520 | tf_op jit(solution)/shard_map/pallas_call | solution.py:1711
  448.7 34.9 %shard_map.298 = (bf16[4,96,768]{2,1,0:T(8,128)(2,1)S(1)}, f32[8,8,768]{2,1,0:T(8,128)S(1)}, f32[512,768]{1,0:T(8,128)S(1)}) custom-call(f32[768,768]{1,0:T(8,128)S(1)} %copy-done, f32[8,8,768]{2,1,0:T(8,128)S(1)} %bitcast.33, f32[64,768]{1,0:T(8,128)S(1)} %slice.125.head_ref), custom_call_target="tpu_custom_call" | custom-call | bytes 104857600 | tf_op jit(solution)/shard_map/pallas_call | solution.py:1023
  483.6 1.1 copy-done.1
  489.5 6.5 %multiply_subtract_fusion = (f32[512,768]{1,0:T(8,128)}, f32[512,768]{1,0:T(8,128)}, f32[512,768]{1,0:T(8,128)}) fusion(f32[512,768]{1,0:T(8,128)} %param.25, f32[512,768]{1,0:T(8,128)} %param.26, f32[512,768]{1,0:T(8,128)} %copy-done.1, f32[512,768]{1,0:T(8,128)} %param.27), kind=kLoop, calls=%fused_computation.7 | loop fusion | flops 5505024 | bytes 11010048 | tf_op jit(solution)/shard_map/sub | solution.py:1765
  496.0 11.7 %shard_map.299 = (f32[96,10496]{1,0:T(8,128)}, f32[96,10496]{1,0:T(8,128)}, f32[96,10496]{1,0:T(8,128)}) custom-call(f32[96,10496]{1,0:T(8,128)} %w_ref.1, f32[96,10496]{1,0:T(8,128)} %m_ref.1, f32[96,10496]{1,0:T(8,128)} %v_ref.1, bf16[4,96,1984]{2,1,0:T(8,128)(2,1)} %get-tuple-element.113.early_ref, bf16[4,96,768]{2,1,0:T(8,128)(2,1)} %copy-done.4), custom_call_target="tpu_custom_call" | custom-call | flops 20152320 | bytes 26198016 | tf_op jit(solution)/shard_map/pallas_call | solution.py:1804
  507.7 5.6 %multiply_subtract_fusion.1 = (f32[64,6144]{1,0:T(8,128)}, f32[64,6144]{1,0:T(8,128)}, f32[64,6144]{1,0:T(8,128)}) fusion(f32[64,6144]{1,0:T(8,128)S(1)} %copy-done.11, f32[64,6144]{1,0:T(8,128)} %param.23, f32[64,4608]{1,0:T(8,128)S(1)} %slice-done, f32[64,1536]{1,0:T(8,128)S(1)} %copy-done.12, f32[64,6144]{1,0:T(8,128)} %param.24), kind=kLoop, calls=%fused_computation.8 | loop fusion | flops 5898240 | bytes 11010048 | tf_op jit(solution)/shard_map/sub | solution.py:1765
  (99 shorter events, 17.4 us)
Async XLA Ops:
  7.2 136.6 %all-gather.2.cloned.1.call-start = ((), (), s32[]{:S(2)}) async-start(), calls=%async_computation.1 | async-start | bytes 7077888 | tf_op jit(solution)/shard_map/all_gather | solution.py:1919
  7.3 2.6 copy-start.14
  7.3 3.2 copy-start.5
  14.7 84.4 %copy-start.13 = (f32[3840]{0:T(1024)S(1)}, f32[3840]{0:T(1024)}, u32[]{:S(2)}) copy-start(f32[3840]{0:T(1024)} %param.28) | copy-start | bytes 46084
  93.4 1.4 copy-start.8
  94.8 1.3 copy-start.9
  96.2 1.0 copy-start.10
  97.2 205.7 %reduce-scatter.2.cloned.1.call-start = ((), (), s32[]{:S(2)}) async-start(), calls=%async_computation.2 | async-start | bytes 12386304 | tf_op jit(solution)/shard_map/reduce_scatter | solution.py:1958
  207.8 0.7 copy-start.18
  207.8 0.7 copy-start.19
  207.8 239.9 %all-reduce.8.cloned.1.call-start = ((), (), s32[]{:S(2)}) async-start(), calls=%async_computation.3 | async-start | bytes 2752512 | tf_op jit(solution)/shard_map/psum | solution.py:1965
  272.9 1.4 copy-start.3
  302.0 0.9 copy-start.2
  378.7 68.0 %copy-start.16 = (f32[16,768]{1,0:T(8,128)S(1)}, f32[16,768]{1,0:T(8,128)}, u32[]{:S(2)}) copy-start(f32[16,768]{1,0:T(8,128)} %get-tuple-element.107) | copy-start | bytes 147460
  378.7 69.0 %copy-start.15 = (f32[16,768]{1,0:T(8,128)S(1)}, f32[16,768]{1,0:T(8,128)}, u32[]{:S(2)}) copy-start(f32[16,768]{1,0:T(8,128)} %get-tuple-element.109) | copy-start | bytes 147460
  378.7 69.0 %copy-start.17 = (f32[8,768]{1,0:T(8,128)S(1)}, f32[8,768]{1,0:T(8,128)}, u32[]{:S(2)}) copy-start(f32[8,768]{1,0:T(8,128)} %get-tuple-element.110) | copy-start | bytes 73732
  446.7 2.0 copy-start
  448.7 37.5 %copy-start.6 = (f32[17408]{0:T(1024)S(1)}, f32[17408]{0:T(1024)}, u32[]{:S(2)}) copy-start(f32[17408]{0:T(1024)} %param.32) | copy-start | bytes 208900
  448.7 37.5 %copy-start.7 = (f32[17408]{0:T(1024)S(1)}, f32[17408]{0:T(1024)}, u32[]{:S(2)}) copy-start(f32[17408]{0:T(1024)} %param.33) | copy-start | bytes 208900
  483.6 1.1 copy-start.1
  484.8 0.8 copy-start.4
  496.0 11.7 %copy-start.11 = (f32[64,6144]{1,0:T(8,128)S(1)}, f32[64,6144]{1,0:T(8,128)}, u32[]{:S(2)}) copy-start(f32[64,6144]{1,0:T(8,128)} %param.22) | copy-start | bytes 4718596
  496.0 11.7 %slice-start = ((f32[64,5376]{1,0:T(8,128)}), f32[64,4608]{1,0:T(8,128)S(1)}, s32[]{:S(2)}) async-start(f32[64,5376]{1,0:T(8,128)} %all-reduce.8.cloned.1.call-done), calls=%async_computation.4 | async-start | bytes 2359296 | tf_op jit(solution)/shard_map/slice | solution.py:2004
  496.0 11.7 %copy-start.12 = (f32[64,1536]{1,0:T(8,128)S(1)}, f32[64,1536]{1,0:T(8,128)}, u32[]{:S(2)}) copy-start(f32[64,1536]{1,0:T(8,128)} %get-tuple-element.118) | copy-start | bytes 1179652
Sparse Core Ops, SparseCore 0:
  97.3 46.4 all-gather.1
  208.0 83.6 reduce-scatter.1
  303.1 78.2 all-reduce.7
